TPU v7x, 128 devices: a whole 4x4x4 slice. The times are simulated.
128 devices in a mesh: row: 8 (over y, z_hi), col: 16 (over x, z_lo, core).
Axes of the slice: x: 4, y: 4, z: 4 (z_hi: 2, z_lo: 2; z = z_hi * 2 + z_lo), core: 2. Of those that a mesh axis runs over, the one named last changes fastest.
Arguments:
- owned_blocks: bfloat16 [2048, 16, 128, 128], P(('row', 'col')), may hold values from -0.8984375 to 0.8984375
- owned_rows: int32 [2048], P(('row', 'col')), may hold values from 0 to 64, as said below
- owned_cols: int32 [2048, 16], P(('row', 'col')), may hold values from 0 to 31
- keep: int32 [16, 512], P('row', 'col'), may hold values 0 or 1
Outputs:
- purified: bfloat16 [2048, 65536], P('row', 'col')
Inputs may be any that keep to these rules, and one draw needn't show every extreme that they name: `owned_rows`: every block row of P stands in exactly one slot, in a slot of its own band; in every band some owner fills all 2 of its slots for that band.
All inputs are finite; a program needn't handle non-finite values. No bound on the sum of `keep` on one device may be relied on, other than what follows from the above.
Results may differ from a plain program's by a relative error of at most 0.005.
Values may be sent and summed in bfloat16 or wider, within the bound.
No kernel may reach another device: no remote copies, remote signals or barrier semaphores. Data moves between devices by JAX's collectives and lax.ppermute only.
A program may use at most 256 MiB of HBM per device.

v0:
```python
import jax
import jax.numpy as jnp
from jax import lax
from jax.sharding import PartitionSpec as P


def passed_along(value, axis, by):
    devices = lax.axis_size(axis)
    return lax.ppermute(value, axis, [(i, (i + by) % devices) for i in range(devices)])


def local(owned_blocks, owned_rows, owned_cols, keep):
    grid_rows = lax.axis_size("row")
    grid_cols = lax.axis_size("col")
    my_row = lax.axis_index("row")
    my_col = lax.axis_index("col")
    block_size = owned_blocks.shape[-1]
    slot_count = owned_rows.shape[0]
    per_band = slot_count // grid_rows
    window_rows = keep.shape[0]
    group_cols = keep.shape[1]
    band_rows = 2 * group_cols
    stacked = owned_blocks.reshape(grid_rows, per_band, grid_cols, block_size, block_size)
    local_rows = owned_rows.reshape(grid_rows, per_band)
    local_cols = owned_cols.reshape(grid_rows, per_band, grid_cols)
    dest_row = jnp.arange(grid_rows, dtype=jnp.int32)[:, None, None]
    dest_col = jnp.arange(grid_cols, dtype=jnp.int32)[None, :, None]
    slot_ids = jnp.arange(per_band, dtype=jnp.int32)[None, None, :]
    band_table = (dest_row + dest_col) % grid_rows
    outgoing = stacked[band_table, slot_ids, dest_col]
    row_labels = local_rows[band_table, slot_ids]
    col_labels = local_cols[band_table, slot_ids, dest_col]
    labels = jnp.stack([row_labels, col_labels], axis=-1)
    arrived, arrived_tags = (
        lax.all_to_all(
            outgoing.reshape(grid_rows * grid_cols, per_band, block_size, block_size),
            ("row", "col"),
            split_axis=0,
            concat_axis=0,
            tiled=True,
        ),
        lax.all_to_all(
            labels.reshape(grid_rows * grid_cols, per_band, 2),
            ("row", "col"),
            split_axis=0,
            concat_axis=0,
            tiled=True,
        ),
    )
    arrived = arrived.reshape(-1, block_size, block_size)
    arrived_tags = arrived_tags.reshape(-1, 2)
    band_blocks = (
        jnp.zeros((band_rows, block_size, block_size), owned_blocks.dtype)
        .at[arrived_tags[:, 0]]
        .set(arrived, mode="drop")
    )
    band_cols = (
        jnp.zeros((band_rows,), jnp.int32)
        .at[arrived_tags[:, 0]]
        .set(arrived_tags[:, 1], mode="drop")
    )
    home_row = (my_row + my_col) % grid_rows
    chosen = jnp.arange(grid_rows, dtype=jnp.int32) == home_row
    window_out = jnp.where(
        chosen[:, None, None, None],
        band_blocks[None, :window_rows],
        jnp.zeros((), owned_blocks.dtype),
    )
    window_tags = jnp.where(chosen[:, None], band_cols[None, :window_rows], 0)
    window_in, window_tags_in = (
        lax.all_to_all(window_out, "row", split_axis=0, concat_axis=0, tiled=True),
        lax.all_to_all(window_tags, "row", split_axis=0, concat_axis=0, tiled=True),
    )
    source_row = (my_row - my_col) % grid_rows
    window_piece = lax.dynamic_index_in_dim(window_in, source_row, 0, keepdims=False)
    window_piece_tags = lax.dynamic_index_in_dim(window_tags_in, source_row, 0, keepdims=False)
    every_blocks, every_tags = (
        lax.all_gather(window_piece, "col", axis=0, tiled=True),
        lax.all_gather(window_piece_tags, "col", axis=0, tiled=True),
    )
    every_blocks = every_blocks.reshape(grid_cols, window_rows, block_size, block_size)
    every_tags = every_tags.reshape(grid_cols, window_rows)
    within = jnp.arange(window_rows, dtype=jnp.int32)
    halves = jnp.arange(2, dtype=jnp.int32)
    square = jnp.zeros((group_cols, window_rows, block_size, block_size), jnp.float32)
    all_cols = lax.all_gather(band_cols, "row", axis=0, tiled=True)
    stored_cols = all_cols.reshape(grid_rows, band_rows)
    current = band_blocks
    kept_list = []
    for section_index in range(grid_rows):
        band_id = (my_row + my_col + section_index) % grid_rows
        source_cols = lax.dynamic_index_in_dim(
            stored_cols, (band_id - my_col) % grid_rows, 0, keepdims=False
        )
        groups = band_id + grid_rows * halves
        left_blocks = every_blocks[groups]
        first_inner_row = halves[:, None] * group_cols + every_tags[groups]
        first_right_blocks = current[first_inner_row]
        first_target = source_cols[first_inner_row]
        first_products = jnp.einsum(
            "uiab,uibc->uiac", left_blocks, first_right_blocks, preferred_element_type=jnp.float32
        )
        square = square.at[first_target, jnp.broadcast_to(within[None, :], first_target.shape)].add(
            first_products
        )
        kept_list.append(current)
        if section_index + 1 < grid_rows:
            current = passed_along(current, "row", -1)
    stored = jnp.stack(kept_list)
    block_base = my_row + my_col
    keep_mask = keep.T.astype(jnp.float32)[:, :, None, None]
    filtered = (square * keep_mask).astype(jnp.bfloat16)
    piece = lax.all_gather(filtered, "col", axis=0, tiled=True)
    piece_rows = piece.shape[0]
    positions = jnp.arange(piece_rows, dtype=jnp.int32)
    kgroup = positions // group_cols
    band_id = kgroup % grid_rows
    inner_row = kgroup // grid_rows * group_cols + positions % group_cols
    right_blocks = stored[(band_id - block_base) % grid_rows, inner_row]
    target = stored_cols[(band_id - my_col) % grid_rows, inner_row]
    products = jnp.einsum("mrab,mbc->mrac", piece, right_blocks, preferred_element_type=jnp.float32)
    cubed = (
        jnp.zeros((group_cols, window_rows, block_size, block_size), jnp.float32)
        .at[target]
        .add(products)
    )
    purified = (3.0 * filtered.astype(jnp.float32) - 2.0 * cubed).astype(jnp.bfloat16)
    return purified.transpose(1, 2, 0, 3).reshape(window_rows * block_size, group_cols * block_size)


def solution(mesh):
    placed = (
        P(("row", "col"), None, None, None),
        P(("row", "col")),
        P(("row", "col"), None),
        P("row", "col"),
    )
    return jax.shard_map(
        local, mesh=mesh, in_specs=placed, out_specs=P("row", "col"), check_vma=False
    )
```

profile of v0, /device:TPU:6, one launch (start us, length us, event | category | flops | bytes accessed | tf_op | source)
XLA Modules:
  0.0 1021.0 jit_solution(17748605505248447957)
XLA Ops:
  12.7 10.5 %all-to-all-start = ((s32[128,2,2]{1,2,0:T(2,128)}), s32[128,2,2]{1,2,0:T(2,128)S(1)}, u32[]{:S(2)}, u32[]{:S(2)}) async-start(s32[128,2,2]{1,2,0:T(2,128)} %copy.23), calls=%async_computation | async-start | bytes 262144 | tf_op jit(solution)/shard_map/all_to_all | solution.py:42
  23.2 14.2 %gather_fusion.4 = bf16[256,128,128]{2,1,0:T(8,128)(2,1)} fusion(bf16[8,2,16,128,128]{4,3,2,1,0:T(8,128)(2,1)} %bitcast.193, s32[256]{0:T(256)S(1)} %reshape.893), kind=kCustom, calls=%fused_computation.4 | custom fusion | bytes 16780288 | tf_op jit(solution)/shard_map/gather | solution.py:30
  37.3 10.2 %all-to-all-start.2 = ((bf16[128,2,128,128]{3,2,1,0:T(8,128)(2,1)}), bf16[128,2,128,128]{3,2,1,0:T(8,128)(2,1)}, u32[]{:S(2)}, u32[]{:S(2)}) async-start(bf16[128,2,128,128]{3,2,1,0:T(8,128)(2,1)} %bitcast.192), calls=%async_computation.2 | async-start | bytes 16777216 | tf_op jit(solution)/shard_map/all_to_all | solution.py:35
  47.7 107.9 %all-to-all-done.2 = bf16[128,2,128,128]{3,2,1,0:T(8,128)(2,1)} async-done(((bf16[128,2,128,128]{3,2,1,0:T(8,128)(2,1)}), bf16[128,2,128,128]{3,2,1,0:T(8,128)(2,1)}, u32[]{:S(2)}, u32[]{:S(2)}) %all-to-all-start.2) | async-done | bytes 8388640 | tf_op jit(solution)/shard_map/all_to_all | solution.py:35
  156.2 23.9 %scatter_fusion = bf16[64,128,128]{2,1,0:T(8,128)(2,1)S(1)} fusion(bf16[64,128,128]{2,1,0:T(8,128)(2,1)S(1)} %broadcast_in_dim.80, s32[256]{0:T(256)S(1)} %bitcast.221, bf16[256,128,128]{2,1,0:T(8,128)(2,1)} %bitcast.11), kind=kCustom, calls=%fused_computation.38 | custom fusion | bytes 25166848 | tf_op jit(solution)/shard_map/scatter | solution.py:55
  180.2 48.7 %collective-permute-done = bf16[64,128,128]{2,1,0:T(8,128)(2,1)S(1)} collective-permute-done((bf16[64,128,128]{2,1,0:T(8,128)(2,1)S(1)}, bf16[64,128,128]{2,1,0:T(8,128)(2,1)S(1)}, u32[]{:S(2)}, u32[]{:S(2)}) %collective-permute-start) | collective-permute-done | bytes 2097184 | tf_op jit(solution)/shard_map/ppermute | solution.py:9
  232.6 45.4 %collective-permute-done.1 = bf16[64,128,128]{2,1,0:T(8,128)(2,1)S(1)} collective-permute-done((bf16[64,128,128]{2,1,0:T(8,128)(2,1)S(1)}, bf16[64,128,128]{2,1,0:T(8,128)(2,1)S(1)}, u32[]{:S(2)}, u32[]{:S(2)}) %collective-permute-start.1) | collective-permute-done | bytes 2097184 | tf_op jit(solution)/shard_map/ppermute | solution.py:9
  279.3 4.8 collective-permute-start.2
  284.1 43.2 %collective-permute-done.2 = bf16[64,128,128]{2,1,0:T(8,128)(2,1)} collective-permute-done((bf16[64,128,128]{2,1,0:T(8,128)(2,1)S(1)}, bf16[64,128,128]{2,1,0:T(8,128)(2,1)}, u32[]{:S(2)}, u32[]{:S(2)}) %collective-permute-start.2) | collective-permute-done | bytes 2097184 | tf_op jit(solution)/shard_map/ppermute | solution.py:9
  327.3 6.2 collective-permute-start.3
  333.5 42.6 %collective-permute-done.3 = bf16[64,128,128]{2,1,0:T(8,128)(2,1)} collective-permute-done((bf16[64,128,128]{2,1,0:T(8,128)(2,1)}, bf16[64,128,128]{2,1,0:T(8,128)(2,1)}, u32[]{:S(2)}, u32[]{:S(2)}) %collective-permute-start.3) | collective-permute-done | bytes 2097184 | tf_op jit(solution)/shard_map/ppermute | solution.py:9
  376.1 6.1 collective-permute-start.4
  388.6 35.3 %all-to-all-done.1 = s32[8,1,2]{2,1,0:T(1,128)S(1)} async-done(((s32[8,1,2]{2,1,0:T(1,128)}), s32[8,1,2]{2,1,0:T(1,128)S(1)}, u32[]{:S(2)}, u32[]{:S(2)}) %all-to-all-start.1) | async-done | bytes 96 | tf_op jit(solution)/shard_map/all_to_all | solution.py:72
  423.9 7.4 all-to-all-start.3
  434.7 5.7 collective-permute-start.5
  440.6 49.0 %all-reduce = s32[512]{0:T(512)S(1)} all-reduce(s32[512]{0:T(512)S(1)} %dynamic-update-slice), channel_id=1, replica_groups=mesh['row'=8,'col'=16] {'row'}, use_global_device_ids=true, to_apply=%add | all-reduce | flops 512 | bytes 4096
  489.8 17.7 %all-reduce.1 = s32[32]{0:T(128)S(1)} all-reduce(s32[32]{0:T(128)S(1)} %fusion.31), channel_id=2, replica_groups=mesh['row'=8,'col'=16] {'col'}, use_global_device_ids=true, to_apply=%add.1 | all-reduce | flops 32 | bytes 256
  528.0 58.9 %all-gather.7.cloned.1.call-done = bf16[1,32,128,128]{3,2,0,1:T(8,128)(2,1)} async-done(((bf16[1,2,128,128]{3,2,0,1:T(8,128)(2,1)}), bf16[1,32,128,128]{3,2,0,1:T(8,128)(2,1)}) %all-gather.7.cloned.1.call-update) | async-done | bytes 1048592 | tf_op jit(solution)/shard_map/all_gather | solution.py:78
  640.0 3.9 multiply_convert_fusion
  668.6 17.0 %gather_fusion.36 = bf16[512,128,128]{2,1,0:T(8,128)(2,1)} fusion(bf16[8,64,128,128]{3,2,1,0:T(8,128)(2,1)} %bitcast_dynamic-update-slice_fusion, s32[512]{0:T(512)S(1)} %bitcast.190), kind=kCustom, calls=%fused_computation.36 | custom fusion | bytes 33558528 | tf_op jit(solution)/shard_map/gather | solution.py:119
  685.6 128.0 %all-gather.5.cloned.1.call-done = bf16[512,2,128,128]{3,2,1,0:T(8,128)(2,1)} async-done(((bf16[32,2,128,128]{3,2,1,0:T(8,128)(2,1)}), bf16[512,2,128,128]{3,2,1,0:T(8,128)(2,1)}) %all-gather.5.cloned.1.call-update) | async-done | bytes 33554448 | tf_op jit(solution)/shard_map/all_gather | solution.py:113
  813.6 41.3 %fusion = f32[512,2,128,128]{3,2,1,0:T(8,128)} fusion(bf16[512,2,128,128]{3,2,1,0:T(8,128)(2,1)} %all-gather.5.cloned.1.call-done, bf16[512,128,128]{2,1,0:T(8,128)(2,1)} %gather_fusion.36), kind=kOutput, calls=%fused_computation.48 | convolution fusion | flops 4294967296 | bytes 117440512 | tf_op jit(solution)/shard_map/mrab,mbc->mrac/dot_general | solution.py:121
  857.4 148.5 %scatter_fusion.9 = f32[32,2,128,128]{3,2,1,0:T(8,128)} fusion(f32[32,2,128,128]{3,2,1,0:T(8,128)} %broadcast.1141, s32[512]{0:T(512)S(1)} %bitcast.219, f32[512,2,128,128]{3,2,1,0:T(8,128)} %fusion), kind=kCustom, calls=%fused_computation.47 | custom fusion | flops 16777216 | bytes 201328640 | tf_op jit(solution)/shard_map/scatter-add | solution.py:125
  1005.9 4.6 fusion.2
  (207 shorter events, 124.6 us)
Async XLA Ops:
  12.7 24.6 %all-to-all-start = ((s32[128,2,2]{1,2,0:T(2,128)}), s32[128,2,2]{1,2,0:T(2,128)S(1)}, u32[]{:S(2)}, u32[]{:S(2)}) async-start(s32[128,2,2]{1,2,0:T(2,128)} %copy.23), calls=%async_computation | async-start | bytes 262144 | tf_op jit(solution)/shard_map/all_to_all | solution.py:42
  37.3 118.3 %all-to-all-start.2 = ((bf16[128,2,128,128]{3,2,1,0:T(8,128)(2,1)}), bf16[128,2,128,128]{3,2,1,0:T(8,128)(2,1)}, u32[]{:S(2)}, u32[]{:S(2)}) async-start(bf16[128,2,128,128]{3,2,1,0:T(8,128)(2,1)} %bitcast.192), calls=%async_computation.2 | async-start | bytes 16777216 | tf_op jit(solution)/shard_map/all_to_all | solution.py:35
  156.1 226.2 %copy-start.18 = (s32[2,32]{1,0:T(2,128)S(1)}, s32[2,32]{1,0:T(2,128)}, u32[]{:S(2)}) copy-start(s32[2,32]{1,0:T(2,128)} %param.7) | copy-start | bytes 772
  156.1 275.4 %copy-start.21 = (u32[128]{0:T(128)S(1)}, u32[128]{0:T(128)}, u32[]{:S(2)}) copy-start(u32[128]{0:T(128)} %constant.443) | copy-start | bytes 1540
  156.2 276.0 %copy-start.20 = (u32[128]{0:T(128)S(1)}, u32[128]{0:T(128)}, u32[]{:S(2)}) copy-start(u32[128]{0:T(128)} %constant.438) | copy-start | bytes 1540
  180.1 48.7 %collective-permute-start = (bf16[64,128,128]{2,1,0:T(8,128)(2,1)S(1)}, bf16[64,128,128]{2,1,0:T(8,128)(2,1)S(1)}, u32[]{:S(2)}, u32[]{:S(2)}) collective-permute-start(bf16[64,128,128]{2,1,0:T(8,128)(2,1)S(1)} %scatter_fusion), channel_id=1, source_target_pairs={{0,112},{16,0},{32,16},{48,32},{64,48},{80,64},{96,80},{112,96},{1... | collective-permute-start | bytes 6291464 | tf_op jit(solution)/shard_map/ppermute | solution.py:9
  230.2 47.8 %collective-permute-start.1 = (bf16[64,128,128]{2,1,0:T(8,128)(2,1)S(1)}, bf16[64,128,128]{2,1,0:T(8,128)(2,1)S(1)}, u32[]{:S(2)}, u32[]{:S(2)}) collective-permute-start(bf16[64,128,128]{2,1,0:T(8,128)(2,1)S(1)} %collective-permute-done), channel_id=1, source_target_pairs={{0,112},{16,0},{32,16},{48,32},{64,48},{80,64},{96,80},{112,96},{1... | collective-permute-start | bytes 6291464 | tf_op jit(solution)/shard_map/ppermute | solution.py:9
  279.3 48.0 %collective-permute-start.2 = (bf16[64,128,128]{2,1,0:T(8,128)(2,1)S(1)}, bf16[64,128,128]{2,1,0:T(8,128)(2,1)}, u32[]{:S(2)}, u32[]{:S(2)}) collective-permute-start(bf16[64,128,128]{2,1,0:T(8,128)(2,1)S(1)} %collective-permute-done.1), channel_id=1, source_target_pairs={{0,112},{16,0},{32,16},{48,32},{64,48},{80,64},{96,80},{112,96},{1... | collective-permute-start | bytes 6291464 | tf_op jit(solution)/shard_map/ppermute | solution.py:9
  327.3 48.8 %collective-permute-start.3 = (bf16[64,128,128]{2,1,0:T(8,128)(2,1)}, bf16[64,128,128]{2,1,0:T(8,128)(2,1)}, u32[]{:S(2)}, u32[]{:S(2)}) collective-permute-start(bf16[64,128,128]{2,1,0:T(8,128)(2,1)} %collective-permute-done.2), channel_id=1, source_target_pairs={{0,112},{16,0},{32,16},{48,32},{64,48},{80,64},{96,80},{112,96},{1... | collective-permute-start | bytes 6291464 | tf_op jit(solution)/shard_map/ppermute | solution.py:9
  376.1 58.6 %collective-permute-start.4 = (bf16[64,128,128]{2,1,0:T(8,128)(2,1)}, bf16[64,128,128]{2,1,0:T(8,128)(2,1)}, u32[]{:S(2)}, u32[]{:S(2)}) collective-permute-start(bf16[64,128,128]{2,1,0:T(8,128)(2,1)} %collective-permute-done.3), channel_id=1, source_target_pairs={{0,112},{16,0},{32,16},{48,32},{64,48},{80,64},{96,80},{112,96},{1... | collective-permute-start | bytes 6291464 | tf_op jit(solution)/shard_map/ppermute | solution.py:9
  382.3 137.8 %copy-start.15 = (s32[1024]{0:T(1024)}, s32[1024]{0:T(1024)S(1)}, u32[]{:S(2)}) copy-start(s32[1024]{0:T(1024)S(1)} %pad_clamp_fusion.5) | copy-start | bytes 12292
  382.3 137.8 %copy-start.16 = (s32[1024]{0:T(1024)}, s32[1024]{0:T(1024)S(1)}, u32[]{:S(2)}) copy-start(s32[1024]{0:T(1024)S(1)} %pad_clamp_fusion.3) | copy-start | bytes 12292
  382.3 137.8 %copy-start.17 = (s32[1024]{0:T(1024)}, s32[1024]{0:T(1024)S(1)}, u32[]{:S(2)}) copy-start(s32[1024]{0:T(1024)S(1)} %pad_clamp_fusion.1) | copy-start | bytes 12292
  384.5 39.4 %all-to-all-start.1 = ((s32[8,1,2]{2,1,0:T(1,128)}), s32[8,1,2]{2,1,0:T(1,128)S(1)}, u32[]{:S(2)}, u32[]{:S(2)}) async-start(s32[8,1,2]{2,1,0:T(1,128)} %broadcast_select_fusion.1), calls=%async_computation.1 | async-start | bytes 8192 | tf_op jit(solution)/shard_map/all_to_all | solution.py:72
  423.9 88.2 %all-to-all-start.3 = ((bf16[8,2,128,128]{3,2,1,0:T(8,128)(2,1)}), bf16[8,2,128,128]{3,2,1,0:T(8,128)(2,1)S(1)}, u32[]{:S(2)}, u32[]{:S(2)}) async-start(bf16[8,2,128,128]{3,2,1,0:T(8,128)(2,1)} %broadcast_select_fusion), calls=%async_computation.3 | async-start | bytes 1048576 | tf_op jit(solution)/shard_map/all_to_all | solution.py:71
  431.3 155.7 %all-gather.7.cloned.1.call-start = ((), (), s32[]{:S(2)}) async-start(), calls=%async_computation.5 | async-start | bytes 1114112 | tf_op jit(solution)/shard_map/all_gather | solution.py:78
  434.7 86.9 %collective-permute-start.5 = (bf16[64,128,128]{2,1,0:T(8,128)(2,1)}, bf16[64,128,128]{2,1,0:T(8,128)(2,1)}, u32[]{:S(2)}, u32[]{:S(2)}) collective-permute-start(bf16[64,128,128]{2,1,0:T(8,128)(2,1)} %collective-permute-done.4), channel_id=1, source_target_pairs={{0,112},{16,0},{32,16},{48,32},{64,48},{80,64},{96,80},{112,96},{1... | collective-permute-start | bytes 6291464 | tf_op jit(solution)/shard_map/ppermute | solution.py:9
  512.7 300.9 %all-gather.5.cloned.1.call-start = ((), (), s32[]{:S(2)}) async-start(), calls=%async_computation.4 | async-start | bytes 35651584 | tf_op jit(solution)/shard_map/all_gather | solution.py:113
  518.7 83.7 %copy-start.7 = (s32[1024]{0:T(1024)}, s32[1024]{0:T(1024)S(1)}, u32[]{:S(2)}) copy-start(s32[1024]{0:T(1024)S(1)} %pad_clamp_fusion.6) | copy-start | bytes 12292
  521.6 113.6 %collective-permute-start.6 = (bf16[64,128,128]{2,1,0:T(8,128)(2,1)}, bf16[64,128,128]{2,1,0:T(8,128)(2,1)}, u32[]{:S(2)}, u32[]{:S(2)}) collective-permute-start(bf16[64,128,128]{2,1,0:T(8,128)(2,1)} %collective-permute-done.5), channel_id=1, source_target_pairs={{0,112},{16,0},{32,16},{48,32},{64,48},{80,64},{96,80},{112,96},{1... | collective-permute-start | bytes 6291464 | tf_op jit(solution)/shard_map/ppermute | solution.py:9
  522.4 80.0 %copy-start.9 = (s32[1024]{0:T(1024)}, s32[1024]{0:T(1024)S(1)}, u32[]{:S(2)}) copy-start(s32[1024]{0:T(1024)S(1)} %pad_clamp_fusion.2) | copy-start | bytes 12292
  523.2 79.2 %copy-start.8 = (s32[1024]{0:T(1024)}, s32[1024]{0:T(1024)S(1)}, u32[]{:S(2)}) copy-start(s32[1024]{0:T(1024)S(1)} %pad_clamp_fusion) | copy-start | bytes 12292
  613.4 24.2 %copy-start.13 = (s32[4]{0:T(128)S(1)}, s32[4]{0:T(128)}, u32[]{:S(2)}) copy-start(s32[4]{0:T(128)} %reshape.1231) | copy-start | bytes 52
  613.6 26.4 %copy-start.6 = (f32[32,2]{1,0:T(8,128)S(1)}, f32[32,2]{1,0:T(8,128)}, u32[]{:S(2)}) copy-start(f32[32,2]{1,0:T(8,128)} %copy.26) | copy-start | bytes 772
  (11 other events, 101.9 us)
Sparse Core Ops, SparseCore 0:
  512.9 74.0 all-gather.6
  644.1 169.4 all-gather.4
where the time goes:
time: 1030 us; the launch traced here: 1020 us
  waiting for transfers between devices  510 us (50%)
  other arithmetic  178 us (17%)
  local copies, waits for them, and re-layouts  149 us (14%)
  blocking collectives  66.7 us (6%)
  starting transfers between devices  57.4 us (6%)
  matrix products  43.6 us (4%)
  between operations  15.6 us (2%)
    ppermute x7, waiting for transfers between devices, passed_along(): lax.ppermute(value, axis, [(i, (i + by) % devices) for i in range(devices)])  180 us
    scatter-add x1, other arithmetic, local(): cubed = jnp.zeros((group_cols, window_rows, block_size, block_size), jnp....  148 us
    all_gather x1, waiting for transfers between devices, local(): piece = lax.all_gather(filtered, 'col', axis=0, tiled=True)  128 us
    all_to_all x1, waiting for transfers between devices, local(): lax.all_to_all(outgoing.reshape(grid_rows * grid_cols, per_band, block_si...  108 us
    unnamed x2, blocking collectives  66.7 us
    all_gather x1, waiting for transfers between devices, local(): lax.all_gather(window_piece, 'col', axis=0, tiled=True)  58.9 us
    dot_general x1, matrix products, local(): jnp.einsum('mrab,mbc->mrac', piece, right_blocks, preferred_element_type=...  41.3 us
    all_to_all x1, waiting for transfers between devices, local(): lax.all_to_all(window_tags, 'row', split_axis=0, concat_axis=0, tiled=True)  35.3 us
  transfers between devices with their start and end apart: 13, of which 8 were waited for; matrix products, arithmetic and copies ran while one was open for 13% of the time, Pallas kernels for 0%

commit v1 on v0

v1 whole, which is shorter than its diff:
```python
import functools

import jax
import jax.numpy as jnp
from jax import lax
from jax.experimental import pallas as pl
from jax.experimental.pallas import tpu as pltpu
from jax.sharding import PartitionSpec as P

AXES = ("row", "col")
B = 128
ROWS, COLS = 8, 16
GROUP = 32
MIB = 1 << 20


def moved(by_y, flip_z):
    pairs = []
    for r in range(ROWS):
        y, z = r // 2, r % 2
        pairs.append((r, (y + by_y) % 4 * 2 + (z ^ flip_z)))
    return pairs


def send_row(value, by_y, flip_z):
    return lax.ppermute(value, "row", moved(by_y, flip_z))


def pack_kernel(where, arrived, band, inner, window, sems):
    def one(source, target, sem):
        pltpu.make_async_copy(arrived.at[source], target, sem).start()

    @pl.loop(0, 2)
    def _(n):
        one(where[n], window.at[n], sems.at[2])

    @pl.loop(0, 32)
    def _(n):
        one(where[64 + n], inner.at[n], sems.at[1])

    @pl.loop(0, 64)
    def _(n):
        one(where[n], band.at[n], sems.at[0])

    for n, target in enumerate((band, inner, window)):
        pltpu.make_async_copy(
            arrived.at[pl.ds(0, target.shape[0])], target, sems.at[n]
        ).wait()


def pack(where, arrived):
    shapes = [jax.ShapeDtypeStruct((n, B, B), jnp.bfloat16) for n in (64, 32, 2)]
    return pl.pallas_call(
        pack_kernel,
        grid_spec=pltpu.PrefetchScalarGridSpec(
            num_scalar_prefetch=1,
            grid=(),
            in_specs=[pl.BlockSpec(memory_space=pl.ANY)],
            out_specs=[pl.BlockSpec(memory_space=pltpu.VMEM)] * 3,
            scratch_shapes=[pltpu.SemaphoreType.DMA((3,))],
        ),
        out_shape=shapes,
        compiler_params=pltpu.CompilerParams(vmem_limit_bytes=16 * MIB),
        cost_estimate=pl.CostEstimate(flops=0, bytes_accessed=6 * MIB, transcendentals=0),
        name="pack",
    )(where, arrived)


def square_kernel(leader, mask, left, inner, *refs):
    out, total = refs[-2:]
    total[...] = jnp.zeros_like(total)
    for g in range(COLS):
        for i in range(2):
            at = leader[i * 16 + g]
            total[i * 16 + at] += jnp.dot(
                left[g, i],
                inner[g % ROWS, i, g // ROWS],
                preferred_element_type=jnp.float32,
            )
    for n in range(32):
        out[n] = (total[n] * mask[n].astype(jnp.float32)).astype(jnp.bfloat16)


def square(leader, mask, left, inner, first):
    return pl.pallas_call(
        square_kernel,
        grid_spec=pltpu.PrefetchScalarGridSpec(
            num_scalar_prefetch=2,
            grid=(),
            in_specs=[pl.BlockSpec(memory_space=pltpu.VMEM)] * 2
            + [pl.BlockSpec(memory_space=pl.ANY)] * len(first),
            out_specs=pl.BlockSpec(memory_space=pltpu.VMEM),
            scratch_shapes=[pltpu.VMEM((32, B, B), jnp.float32)],
        ),
        out_shape=jax.ShapeDtypeStruct((32, B, B), jnp.bfloat16),
        compiler_params=pltpu.CompilerParams(vmem_limit_bytes=16 * MIB),
        cost_estimate=pl.CostEstimate(
            flops=32 * 2 * B**3, bytes_accessed=3 * MIB, transcendentals=0
        ),
        name="square",
    )(leader, mask, left, inner, *first)


def cubed_kernel(groups, inner_at, target, *refs):
    filtered, pieces = refs[0], refs[1:9]
    out, held_f, held_p, total, sem_f, sem_p = refs[9:]

    def f_copy(m):
        return pltpu.make_async_copy(filtered.at[groups[m]], held_f.at[m], sem_f.at[m])

    def p_copy(m):
        return pltpu.make_async_copy(
            pieces[m // 2].at[pl.ds(m % 2 * GROUP, GROUP)], held_p.at[m], sem_p.at[m]
        )

    for m in range(16):
        f_copy(m).start()
        p_copy(m).start()
    own = pltpu.make_async_copy(filtered.at[groups[16]], held_f.at[16], sem_f.at[16])
    own.start()
    total[...] = jnp.zeros_like(total)

    @pl.loop(0, 16)
    def _(m):
        f_copy(m).wait()
        pltpu.make_async_copy(
            pieces[0].at[pl.ds(0, GROUP)], held_p.at[m], sem_p.at[m]
        ).wait()
        base = groups[m] * 32
        for n in range(32):
            at = target[base + n] + n // 16 * GROUP
            total[at] += jnp.dot(
                held_f[m, n],
                held_p[m, inner_at[base + n]],
                preferred_element_type=jnp.float32,
            )

    own.wait()
    own_base = groups[16] * 32
    for n in range(32):
        at = inner_at[own_base + n] + n // 16 * GROUP
        total[at] += -1.5 * held_f[16, n].astype(jnp.float32)
    for i in range(2):
        for j in range(GROUP):
            out[i * B : (i + 1) * B, j * B : (j + 1) * B] = (
                -2.0 * total[i * GROUP + j]
            ).astype(jnp.bfloat16)


def cubed(groups, inner_at, target, filtered, pieces):
    return pl.pallas_call(
        cubed_kernel,
        grid_spec=pltpu.PrefetchScalarGridSpec(
            num_scalar_prefetch=3,
            grid=(),
            in_specs=[pl.BlockSpec(memory_space=pl.ANY)] * 9,
            out_specs=pl.BlockSpec(memory_space=pltpu.VMEM),
            scratch_shapes=[
                pltpu.VMEM((17, 32, B, B), jnp.bfloat16),
                pltpu.VMEM((16, GROUP, B, B), jnp.bfloat16),
                pltpu.VMEM((64, B, B), jnp.float32),
                pltpu.SemaphoreType.DMA((17,)),
                pltpu.SemaphoreType.DMA((16,)),
            ],
        ),
        out_shape=jax.ShapeDtypeStruct((2 * B, GROUP * B), jnp.bfloat16),
        compiler_params=pltpu.CompilerParams(vmem_limit_bytes=48 * MIB),
        cost_estimate=pl.CostEstimate(
            flops=4 * 512 * 2 * B**3, bytes_accessed=36 * MIB, transcendentals=0
        ),
        name="cubed",
    )(groups, inner_at, target, filtered, *pieces)


def is_equal(values, count):
    return values[..., None] == jnp.arange(count, dtype=jnp.int32)


def picked(values, table):
    return jnp.sum(jnp.where(is_equal(values, table.shape[0]), table, 0), axis=-1)


def local(owned_blocks, owned_rows, owned_cols, keep):
    r, c = lax.axis_index("row"), lax.axis_index("col")
    outgoing = owned_blocks.reshape(ROWS, 2, COLS, B, B).transpose(0, 2, 1, 3, 4)
    arrived = lax.all_to_all(
        outgoing.reshape(ROWS * COLS, 2, B, B), AXES, split_axis=0, concat_axis=0, tiled=True
    ).reshape(256, B, B)

    tags = jnp.concatenate([owned_cols.reshape(-1), owned_rows, jnp.zeros(752, jnp.int32)])
    tags = lax.all_to_all(
        jnp.broadcast_to(tags.reshape(1, 8, 128), (ROWS * COLS, 8, 128)),
        AXES,
        split_axis=0,
        concat_axis=0,
        tiled=True,
    )
    all_rows = tags[:, 2, :16]
    all_cols = tags[:, :2].reshape(2048, COLS)
    bands = (jnp.arange(16, dtype=jnp.int32) // 2)[None]
    ids = GROUP * (bands + ROWS * (all_rows // GROUP)) + all_rows % GROUP
    ids = jnp.where(all_rows < 64, ids, -1).reshape(2048)
    spots = (ids[None] == jnp.arange(512, dtype=jnp.int32)[:, None]).astype(jnp.bfloat16)
    cols = jnp.dot(
        spots, all_cols.astype(jnp.bfloat16), preferred_element_type=jnp.float32
    ).astype(jnp.int32)

    band_tags = lax.dynamic_slice_in_dim(all_rows, 2 * r, 2, 1).reshape(256)
    place = jnp.sum(
        jnp.where(
            band_tags[None] == jnp.arange(64, dtype=jnp.int32)[:, None],
            jnp.arange(256, dtype=jnp.int32)[None],
            0,
        ),
        axis=1,
    )
    window_cols = cols.reshape(16, GROUP, COLS)[:ROWS, :2]
    wanted = lax.dynamic_slice_in_dim(
        window_cols.reshape(ROWS, 2, 2, ROWS), r, 1, 3
    )[..., 0]
    wanted = wanted + GROUP * jnp.arange(2, dtype=jnp.int32)
    where = jnp.concatenate([place, picked(wanted.reshape(32), place)])

    mine = lax.dynamic_index_in_dim(window_cols, r, 0, keepdims=False)
    rows_in = (mine + GROUP * jnp.arange(COLS, dtype=jnp.int32)[None]).reshape(32)
    tcol = (
        jnp.dot(
            is_equal(rows_in, 512).astype(jnp.bfloat16),
            cols.astype(jnp.bfloat16),
            preferred_element_type=jnp.float32,
        )
        .astype(jnp.int32)
        .reshape(2, 16, COLS)
    )
    my_cols = lax.dynamic_slice_in_dim(cols, c, 1, 1).reshape(COLS, GROUP)
    inner_at = tcol.transpose(2, 0, 1)
    target = jnp.sum(
        jnp.where(is_equal(inner_at, GROUP), my_cols[:, None, None, :], 0), axis=-1
    )
    here = lax.dynamic_index_in_dim(inner_at, c, 0, keepdims=False)
    same = here[:, :, None] == here[:, None, :]
    order = jnp.arange(16, dtype=jnp.int32)
    leader = jnp.min(jnp.where(same, order, 16), axis=-1)
    kept = jnp.sum(jnp.where(is_equal(here, GROUP), keep[:, None, :], 0), axis=-1)
    mask = jnp.where(leader == order, kept, 0)

    band, inner, window = pack(where, arrived)

    pieces = {(0, 0): band}
    pieces[1, 0] = send_row(band, -1, 0)
    pieces[3, 0] = send_row(band, 1, 0)
    pieces[0, 1] = send_row(band, 0, 1)
    pieces[1, 1] = send_row(pieces[0, 1], -1, 0)
    pieces[3, 1] = send_row(pieces[0, 1], 1, 0)
    pieces[2, 0] = send_row(pieces[1, 0], -1, 0)
    pieces[2, 1] = send_row(pieces[3, 1], 1, 0)

    left = lax.all_gather(window, "col", axis=0, tiled=True).reshape(COLS, 2, B, B)
    inner = lax.all_to_all(
        inner.reshape(ROWS, 4, B, B), "row", split_axis=0, concat_axis=0, tiled=True
    ).reshape(ROWS, 2, 2, B, B)
    filtered = square(
        leader.reshape(32),
        mask.reshape(32),
        left,
        inner,
        [pieces[key] for key in ((1, 0), (3, 0), (0, 1))],
    )
    filtered = lax.all_gather(filtered[None], "col", axis=0, tiled=True)

    order = [(0, 0), (1, 0), (3, 0), (0, 1), (2, 0), (3, 1), (1, 1), (2, 1)]
    groups = []
    for dy, dz in order:
        band_id = (r // 2 + dy) % 4 * 2 + (r % 2 + dz) % 2
        groups += [band_id, band_id + ROWS]
    groups = jnp.stack(groups + [c]).astype(jnp.int32)
    return cubed(
        groups,
        inner_at.reshape(512),
        target.reshape(512),
        filtered,
        [pieces[key] for key in order],
    )


def solution(mesh):
    placed = (P(AXES, None, None, None), P(AXES), P(AXES, None), P("row", "col"))
    return jax.shard_map(
        local, mesh=mesh, in_specs=placed, out_specs=P("row", "col"), check_vma=False
    )
```

time: 1030 us -> 340 us (0.33)
  waiting for transfers between devices: 510 us -> 253 us
  other arithmetic: 178 us -> 2.31 us
  local copies, waits for them, and re-layouts: 149 us -> 17.7 us
  blocking collectives: 66.7 us -> 0 us
  matrix products: 43.6 us -> 1.04 us
  starting transfers between devices: 57.4 us -> 29.9 us
  Pallas kernels: 0 us -> 20.1 us
    all_gather x2, waiting for transfers between devices: 187 us -> 0.01 us  [the longest x1 0.01 us: local(): lax.all_gather(window, 'col', axis=0, tiled=True).reshape(COLS, 2, B, B)]
    scatter-add x9 -> x0, other arithmetic: 168 us -> none  [the longest x1 148 us: local(): cubed = jnp.zeros((group_cols, window_rows, block_size, block_size), jnp....]
    ppermute x7, waiting for transfers between devices: 180 us -> 90 us  [send_row(): return lax.ppermute(value, 'row', moved(by_y, flip_z))]
    gather x45 -> x0, local copies, waits for them, and re-layouts: 79.6 us -> none  [the longest x1 17 us: local(): right_blocks = stored[(band_id - block_base) % grid_rows, inner_row]]
    unnamed x2 -> x0, blocking collectives: 66.7 us -> none
    dot_general x9 -> x2, matrix products: 43.6 us -> 1.04 us  [the longest x1 0.84 us: local(): jnp.dot(spots, all_cols.astype(jnp.bfloat16), preferred_element_type=jnp....]
    scatter x2 -> x0, local copies, waits for them, and re-layouts: 25.3 us -> none  [the longest x1 23.9 us: local(): band_blocks = jnp.zeros((band_rows, block_size, block_size), owned_blocks...]
    unnamed x58 -> x9, local copies, waits for them, and re-layouts: 25.7 us -> 3.07 us
  transfers between devices with their start and end apart: 13 -> 12, of which waited for: 8 -> 7; matrix products, arithmetic and copies ran while one was open for 13% -> 5% of each run, Pallas kernels for 0% -> 0%
where the time goes in v1:
time: 340 us; the launch traced here: 337 us
  waiting for transfers between devices  253 us (74%)
  starting transfers between devices  29.9 us (9%)
  Pallas kernels  20.1 us (6%)
  local copies, waits for them, and re-layouts  17.7 us (5%)
  between operations  13.7 us (4%)
    all_to_all x1, waiting for transfers between devices, local(): lax.all_to_all(outgoing.reshape(ROWS * COLS, 2, B, B), AXES, split_axis=0...  105 us
    ppermute x7, waiting for transfers between devices, send_row(): return lax.ppermute(value, 'row', moved(by_y, flip_z))  90 us
    all_to_all x1, waiting for transfers between devices, local(): lax.all_to_all(inner.reshape(ROWS, 4, B, B), 'row', split_axis=0, concat_...  55.8 us
    pallas_call x1, Pallas kernels, cubed(): pl.pallas_call(cubed_kernel, grid_spec=pltpu.PrefetchScalarGridSpec(num_s...  14 us
    all_to_all x1, starting transfers between devices, local(): lax.all_to_all(jnp.broadcast_to(tags.reshape(1, 8, 128), (ROWS * COLS, 8,...  10.5 us
    transpose x1, local copies, waits for them, and re-layouts, local(): owned_blocks.reshape(ROWS, 2, COLS, B, B).transpose(0, 2, 1, 3, 4)  10.3 us
    all_to_all x1, starting transfers between devices, local(): lax.all_to_all(outgoing.reshape(ROWS * COLS, 2, B, B), AXES, split_axis=0...  7.99 us
  transfers between devices with their start and end apart: 12, of which 7 were waited for; matrix products, arithmetic and copies ran while one was open for 5% of the time, Pallas kernels for 0%

profile of v1, /device:TPU:6, one launch (start us, length us, event | category | flops | bytes accessed | tf_op | source)
XLA Modules:
  0.0 337.5 jit_solution(2536971817378289955)
XLA Ops:
  6.5 0.8 reshape.167
  7.3 0.7 add_bitcast_fusion
  8.0 0.8 broadcast_in_dim.91
  8.9 10.5 %all-to-all-start = ((s32[128,8,128]{2,1,0:T(8,128)}), s32[128,8,128]{2,1,0:T(8,128)S(1)}, u32[]{:S(2)}, u32[]{:S(2)}) async-start(s32[128,8,128]{2,1,0:T(8,128)} %broadcast_in_dim.91), calls=%async_computation | async-start | bytes 1048576 | tf_op jit(solution)/shard_map/all_to_all | solution.py:191
  19.4 10.3 %copy.16 = bf16[8,16,2,128,128]{4,3,2,1,0:T(8,128)(2,1)} copy(bf16[8,16,2,128,128]{4,3,1,2,0:T(8,128)(2,1)} %bitcast.45) | data formatting | bytes 16777216 | tf_op jit(solution)/shard_map/transpose | solution.py:185
  29.7 2.2 all-to-all-done
  31.9 8.0 %all-to-all-start.1 = ((bf16[128,2,128,128]{3,2,1,0:T(8,128)(2,1)}), bf16[128,2,128,128]{3,2,1,0:T(8,128)(2,1)}, u32[]{:S(2)}, u32[]{:S(2)}) async-start(bf16[128,2,128,128]{3,2,1,0:T(8,128)(2,1)} %bitcast.43), calls=%async_computation.1 | async-start | bytes 16777216 | tf_op jit(solution)/shard_map/all_to_all | solution.py:186
  40.9 0.4 convert_element_type.15
  41.3 0.8 fusion.2
  43.3 104.7 %all-to-all-done.1 = bf16[128,2,128,128]{3,2,1,0:T(8,128)(2,1)} async-done(((bf16[128,2,128,128]{3,2,1,0:T(8,128)(2,1)}), bf16[128,2,128,128]{3,2,1,0:T(8,128)(2,1)}, u32[]{:S(2)}, u32[]{:S(2)}) %all-to-all-start.1) | async-done | bytes 8388640 | tf_op jit(solution)/shard_map/all_to_all | solution.py:186
  148.0 3.8 %pack.1 = (bf16[64,128,128]{2,1,0:T(8,128)(2,1)}, bf16[32,128,128]{2,1,0:T(8,128)(2,1)S(1)}, bf16[2,128,128]{2,1,0:T(8,128)(2,1)}) custom-call(s32[96]{0:T(128)S(1)} %pad_add_fusion.where, bf16[256,128,128]{2,1,0:T(8,128)(2,1)} %bitcast.23.arrived), custom_call_target="tpu_custom_call" | custom-call | bytes 6291456 | tf_op jit(solution)/shard_map/pack/pallas_call | solution.py:53
  151.8 1.0 copy-done.2
  152.9 3.2 collective-permute-start
  156.2 4.7 %all-to-all-start.2 = ((bf16[8,4,128,128]{3,2,1,0:T(8,128)(2,1)}), bf16[8,4,128,128]{3,2,1,0:T(8,128)(2,1)S(1)}, u32[]{:S(2)}, u32[]{:S(2)}) async-start(bf16[8,4,128,128]{3,2,1,0:T(8,128)(2,1)} %bitcast.42), calls=%async_computation.2 | async-start | bytes 2097152 | tf_op jit(solution)/shard_map/all_to_all | solution.py:259
  162.1 55.8 %all-to-all-done.2 = bf16[8,4,128,128]{3,2,1,0:T(8,128)(2,1)S(1)} async-done(((bf16[8,4,128,128]{3,2,1,0:T(8,128)(2,1)}), bf16[8,4,128,128]{3,2,1,0:T(8,128)(2,1)S(1)}, u32[]{:S(2)}, u32[]{:S(2)}) %all-to-all-start.2) | async-done | bytes 1048608 | tf_op jit(solution)/shard_map/all_to_all | solution.py:259
  217.9 2.0 copy-done.1
  219.9 2.2 square.1
  222.2 3.2 collective-permute-start.5
  225.4 44.3 %collective-permute-done.4.refs_6_ = bf16[64,128,128]{2,1,0:T(8,128)(2,1)} collective-permute-done((bf16[64,128,128]{2,1,0:T(8,128)(2,1)S(1)}, bf16[64,128,128]{2,1,0:T(8,128)(2,1)}, u32[]{:S(2)}, u32[]{:S(2)}) %collective-permute-start.4) | collective-permute-done | bytes 2097184 | tf_op jit(solution)/shard_map/ppermute | solution.py:26
  270.0 0.8 select_reduce_fusion
  270.9 0.6 collective-permute-done.5.refs_7_
  271.5 42.5 %collective-permute-done.3.refs_5_ = bf16[64,128,128]{2,1,0:T(8,128)(2,1)} collective-permute-done((bf16[64,128,128]{2,1,0:T(8,128)(2,1)}, bf16[64,128,128]{2,1,0:T(8,128)(2,1)}, u32[]{:S(2)}, u32[]{:S(2)}) %collective-permute-start.3) | collective-permute-done | bytes 2097184 | tf_op jit(solution)/shard_map/ppermute | solution.py:26
  313.9 2.7 collective-permute-done.6.refs_8_
  316.6 14.0 %cubed.1 = bf16[256,4096]{1,0:T(8,128)(2,1)} custom-call(s32[17]{0:T(128)S(1)} %stack.71.groups, s32[512]{0:T(512)S(1)} %reshape.170.inner_at, s32[512]{0:T(512)S(1)} %reshape.171.target, bf16[16,32,128,128]{3,2,1,0:T(8,128)(2,1)} %bitcast.44, bf16[64,128,128]{2,1,0:T(8,128)(2,1)} %get-tuple-element.10.refs_1_, ...), custom_call_target="tpu_custom_call" | custom-call | flops 8589934592 | bytes 37748736 | tf_op jit(solution)/shard_map/cubed/pallas_call | solution.py:151
  (65 shorter events, 3.8 us)
Async XLA Ops:
  8.9 23.0 %all-to-all-start = ((s32[128,8,128]{2,1,0:T(8,128)}), s32[128,8,128]{2,1,0:T(8,128)S(1)}, u32[]{:S(2)}, u32[]{:S(2)}) async-start(s32[128,8,128]{2,1,0:T(8,128)} %broadcast_in_dim.91), calls=%async_computation | async-start | bytes 1048576 | tf_op jit(solution)/shard_map/all_to_all | solution.py:191
  31.9 116.1 %all-to-all-start.1 = ((bf16[128,2,128,128]{3,2,1,0:T(8,128)(2,1)}), bf16[128,2,128,128]{3,2,1,0:T(8,128)(2,1)}, u32[]{:S(2)}, u32[]{:S(2)}) async-start(bf16[128,2,128,128]{3,2,1,0:T(8,128)(2,1)} %bitcast.43), calls=%async_computation.1 | async-start | bytes 16777216 | tf_op jit(solution)/shard_map/all_to_all | solution.py:186
  39.9 177.9 %all-gather.4.cloned.1.call-start = ((), (), s32[]{:S(2)}) async-start(), calls=%async_computation.3 | async-start | bytes 1114112 | tf_op jit(solution)/shard_map/all_gather | solution.py:258
  151.8 1.0 copy-start.2
  152.8 9.0 %copy-start.3 = (s32[2,32]{1,0:T(2,128)S(1)}, s32[2,32]{1,0:T(2,128)}, u32[]{:S(2)}) copy-start(s32[2,32]{1,0:T(2,128)} %param.7) | copy-start | bytes 772
  152.8 65.0 %collective-permute-start.2 = (bf16[64,128,128]{2,1,0:T(8,128)(2,1)}, bf16[64,128,128]{2,1,0:T(8,128)(2,1)S(1)}, u32[]{:S(2)}, u32[]{:S(2)}) collective-permute-start(bf16[64,128,128]{2,1,0:T(8,128)(2,1)} %get-tuple-element.10.refs_1_), channel_id=1, source_target_pairs={{0,16},{16,0},{32,48},{48,32},{64,80},{80,64},{96,112},{112,96},{1... | collective-permute-start | bytes 6291464 | tf_op jit(solution)/shard_map/ppermute | solution.py:26
  152.9 64.9 %collective-permute-start.1 = (bf16[64,128,128]{2,1,0:T(8,128)(2,1)}, bf16[64,128,128]{2,1,0:T(8,128)(2,1)}, u32[]{:S(2)}, u32[]{:S(2)}) collective-permute-start(bf16[64,128,128]{2,1,0:T(8,128)(2,1)} %get-tuple-element.10.refs_1_), channel_id=1, source_target_pairs={{0,32},{16,48},{32,64},{48,80},{64,96},{80,112},{96,0},{112,16},{1... | collective-permute-start | bytes 6291464 | tf_op jit(solution)/shard_map/ppermute | solution.py:26
  152.9 64.9 %collective-permute-start = (bf16[64,128,128]{2,1,0:T(8,128)(2,1)}, bf16[64,128,128]{2,1,0:T(8,128)(2,1)}, u32[]{:S(2)}, u32[]{:S(2)}) collective-permute-start(bf16[64,128,128]{2,1,0:T(8,128)(2,1)} %get-tuple-element.10.refs_1_), channel_id=1, source_target_pairs={{0,96},{16,112},{32,0},{48,16},{64,32},{80,48},{96,64},{112,80},{1... | collective-permute-start | bytes 6291464 | tf_op jit(solution)/shard_map/ppermute | solution.py:26
  156.2 61.7 %all-to-all-start.2 = ((bf16[8,4,128,128]{3,2,1,0:T(8,128)(2,1)}), bf16[8,4,128,128]{3,2,1,0:T(8,128)(2,1)S(1)}, u32[]{:S(2)}, u32[]{:S(2)}) async-start(bf16[8,4,128,128]{3,2,1,0:T(8,128)(2,1)} %bitcast.42), calls=%async_computation.2 | async-start | bytes 2097152 | tf_op jit(solution)/shard_map/all_to_all | solution.py:259
  160.9 155.7 %all-gather.6.cloned.1.call-start = ((), (), s32[]{:S(2)}) async-start(), calls=%async_computation.4 | async-start | bytes 17825792 | tf_op jit(solution)/shard_map/all_gather | solution.py:269
  217.8 4.3 %copy-start = (bf16[64,128,128]{2,1,0:T(8,128)(2,1)}, bf16[64,128,128]{2,1,0:T(8,128)(2,1)S(1)}, u32[]{:S(2)}) copy-start(bf16[64,128,128]{2,1,0:T(8,128)(2,1)S(1)} %collective-permute-done.2.refs_2_.refs_4_) | copy-start | bytes 6291460
  217.9 2.0 copy-start.1
  222.1 47.7 %collective-permute-start.4 = (bf16[64,128,128]{2,1,0:T(8,128)(2,1)S(1)}, bf16[64,128,128]{2,1,0:T(8,128)(2,1)}, u32[]{:S(2)}, u32[]{:S(2)}) collective-permute-start(bf16[64,128,128]{2,1,0:T(8,128)(2,1)S(1)} %collective-permute-done.2.refs_2_.refs_4_), channel_id=1, source_target_pairs={{0,32},{16,48},{32,64},{48,80},{64,96},{80,112},{96,0},{112,16},{1... | collective-permute-start | bytes 6291464 | tf_op jit(solution)/shard_map/ppermute | solution.py:26
  222.2 49.3 %collective-permute-start.5 = (bf16[64,128,128]{2,1,0:T(8,128)(2,1)S(1)}, bf16[64,128,128]{2,1,0:T(8,128)(2,1)}, u32[]{:S(2)}, u32[]{:S(2)}) collective-permute-start(bf16[64,128,128]{2,1,0:T(8,128)(2,1)S(1)} %collective-permute-done.2.refs_2_.refs_4_), channel_id=1, source_target_pairs={{0,96},{16,112},{32,0},{48,16},{64,32},{80,48},{96,64},{112,80},{1... | collective-permute-start | bytes 6291464 | tf_op jit(solution)/shard_map/ppermute | solution.py:26
  225.4 88.6 %collective-permute-start.3 = (bf16[64,128,128]{2,1,0:T(8,128)(2,1)}, bf16[64,128,128]{2,1,0:T(8,128)(2,1)}, u32[]{:S(2)}, u32[]{:S(2)}) collective-permute-start(bf16[64,128,128]{2,1,0:T(8,128)(2,1)} %collective-permute-done.refs_0_.refs_2_), channel_id=1, source_target_pairs={{0,96},{16,112},{32,0},{48,16},{64,32},{80,48},{96,64},{112,80},{1... | collective-permute-start | bytes 6291464 | tf_op jit(solution)/shard_map/ppermute | solution.py:26
  269.7 46.9 %collective-permute-start.6 = (bf16[64,128,128]{2,1,0:T(8,128)(2,1)}, bf16[64,128,128]{2,1,0:T(8,128)(2,1)}, u32[]{:S(2)}, u32[]{:S(2)}) collective-permute-start(bf16[64,128,128]{2,1,0:T(8,128)(2,1)} %collective-permute-done.4.refs_6_), channel_id=1, source_target_pairs={{0,32},{16,48},{32,64},{48,80},{64,96},{80,112},{96,0},{112,16},{1... | collective-permute-start | bytes 6291464 | tf_op jit(solution)/shard_map/ppermute | solution.py:26
Sparse Core Ops, SparseCore 0:
  156.3 34.9 all-gather.3
  222.2 90.7 all-gather.5

commit v2 on v1

v2 whole, which is shorter than its diff:
```python
import functools

import jax
import jax.numpy as jnp
from jax import lax
from jax.experimental import pallas as pl
from jax.experimental.pallas import tpu as pltpu
from jax.sharding import PartitionSpec as P

AXES = ("row", "col")
B = 128
ROWS, COLS = 8, 16
GROUP = 32
MIB = 1 << 20
ROOM = 63 * MIB
EARLY = ((0, 0), (0, 1), (1, 0), (1, 1), (3, 0), (3, 1), (2, 0))
LATE = ((2, 1),)


def moved(by_y, flip_z):
    pairs = []
    for r in range(ROWS):
        y, z = r // 2, r % 2
        pairs.append((r, (y + by_y) % 4 * 2 + (z ^ flip_z)))
    return pairs


def send_col(value, by_x, flip_z, flip_core):
    pairs = []
    for n in range(COLS):
        x, z, core = n // 4, n // 2 % 2, n % 2
        pairs.append((n, (x + by_x) % 4 * 4 + (z ^ flip_z) * 2 + (core ^ flip_core)))
    return lax.ppermute(value, "col", pairs)


def send_row(value, by_y, flip_z):
    return lax.ppermute(value, "row", moved(by_y, flip_z))


def spread_kernel(owned, blocks, held, sem_in, sem_out):
    def read(n):
        return pltpu.make_async_copy(
            owned.at[n], held.at[n // 2, :, n % 2], sem_in.at[n]
        )

    def write(h):
        return pltpu.make_async_copy(held.at[h], blocks.at[h], sem_out.at[h])

    for n in range(2 * ROWS):
        read(n).start()
    for h in range(ROWS):
        read(2 * h).wait()
        read(2 * h + 1).wait()
        write(h).start()
    for h in range(ROWS):
        write(h).wait()


def spread(owned):
    return pl.pallas_call(
        spread_kernel,
        in_specs=[pl.BlockSpec(memory_space=pl.ANY)],
        out_specs=pl.BlockSpec(memory_space=pl.ANY),
        scratch_shapes=[
            pltpu.VMEM((ROWS, COLS, 2, B, B), jnp.bfloat16),
            pltpu.SemaphoreType.DMA((2 * ROWS,)),
            pltpu.SemaphoreType.DMA((ROWS,)),
        ],
        out_shape=jax.ShapeDtypeStruct((ROWS, COLS, 2, B, B), jnp.bfloat16),
        compiler_params=pltpu.CompilerParams(vmem_limit_bytes=ROOM),
        cost_estimate=pl.CostEstimate(flops=0, bytes_accessed=16 * MIB, transcendentals=0),
        name="spread",
    )(owned)


def after_kernel(*refs):
    del refs


def after(values, others):
    return pl.pallas_call(
        after_kernel,
        in_specs=[pl.BlockSpec(memory_space=pltpu.HBM)] * (len(values) + len(others)),
        out_specs=[pl.BlockSpec(memory_space=pltpu.HBM)] * len(values),
        out_shape=[jax.ShapeDtypeStruct(v.shape, v.dtype) for v in values],
        input_output_aliases={n: n for n in range(len(values))},
        compiler_params=pltpu.CompilerParams(vmem_limit_bytes=ROOM),
        cost_estimate=pl.CostEstimate(flops=0, bytes_accessed=1024, transcendentals=0),
        name="after",
    )(*values, *others)


def pack_kernel(parts, where, arrived, *refs):
    outs, held, sem, sems = refs[-3 - parts : -3], *refs[-3:]
    count = held.shape[0]

    @pl.loop(0, count)
    def _(n):
        pltpu.make_async_copy(arrived.at[where[n]], held.at[n], sem).start()

    pltpu.make_async_copy(arrived.at[pl.ds(0, count)], held, sem).wait()
    size = count // parts
    writes = [
        pltpu.make_async_copy(held.at[pl.ds(n * size, size)], out, sems.at[n])
        for n, out in enumerate(outs)
    ]
    for write in writes:
        write.start()
    for write in writes:
        write.wait()


def pack(where, arrived, others=(), parts=1):
    count = where.shape[0]
    return pl.pallas_call(
        functools.partial(pack_kernel, parts),
        grid_spec=pltpu.PrefetchScalarGridSpec(
            num_scalar_prefetch=1,
            grid=(),
            in_specs=[pl.BlockSpec(memory_space=pltpu.HBM)] * (1 + len(others)),
            out_specs=[pl.BlockSpec(memory_space=pltpu.HBM)] * parts,
            scratch_shapes=[
                pltpu.VMEM((count, B, B), jnp.bfloat16),
                pltpu.SemaphoreType.DMA,
                pltpu.SemaphoreType.DMA((parts,)),
            ],
        ),
        out_shape=[jax.ShapeDtypeStruct((count // parts, B, B), jnp.bfloat16)] * parts,
        compiler_params=pltpu.CompilerParams(vmem_limit_bytes=ROOM),
        cost_estimate=pl.CostEstimate(
            flops=0, bytes_accessed=4 * count * B * B, transcendentals=0
        ),
        name="pack",
    )(where, arrived, *others)


def square_kernel(groups, leader, mask, left, *refs):
    out, held, done, total, sem_in, sem_out = refs[-6:]
    count = held.shape[0]

    def write(p):
        return pltpu.make_async_copy(done.at[p], out.at[p], sem_out.at[p])

    for p, inner in enumerate(refs[:count]):
        pltpu.make_async_copy(inner, held.at[p], sem_in.at[p]).start()

    @pl.loop(0, count)
    def _(p):
        pltpu.make_async_copy(refs[0], held.at[p], sem_in.at[p]).wait()
        base = groups[p] * 32
        total[...] = jnp.zeros_like(total)
        for g in range(COLS):
            for i in range(2):
                at = leader[base + i * 16 + g]
                total[i * 16 + at] += jnp.dot(
                    left[g, i],
                    held[p, g % ROWS * 4 + i * 2 + g // ROWS],
                    preferred_element_type=jnp.float32,
                )
        for n in range(32):
            kept = mask[base + n].astype(jnp.float32)
            done[p, n] = (total[n] * kept).astype(jnp.bfloat16)
        write(p).start()

    for p in range(count):
        write(p).wait()


def square(groups, leader, mask, left, inners, others):
    count = len(inners)
    hbm = pl.BlockSpec(memory_space=pltpu.HBM)
    return pl.pallas_call(
        square_kernel,
        grid_spec=pltpu.PrefetchScalarGridSpec(
            num_scalar_prefetch=3,
            grid=(),
            in_specs=[pl.BlockSpec(memory_space=pltpu.VMEM)]
            + [hbm] * (count + len(others)),
            out_specs=hbm,
            scratch_shapes=[
                pltpu.VMEM((count, 32, B, B), jnp.bfloat16),
                pltpu.VMEM((count, 32, B, B), jnp.bfloat16),
                pltpu.VMEM((32, B, B), jnp.float32),
                pltpu.SemaphoreType.DMA((count,)),
                pltpu.SemaphoreType.DMA((count,)),
            ],
        ),
        out_shape=jax.ShapeDtypeStruct((count, 32, B, B), jnp.bfloat16),
        compiler_params=pltpu.CompilerParams(vmem_limit_bytes=ROOM),
        cost_estimate=pl.CostEstimate(
            flops=count * 32 * 2 * B**3, bytes_accessed=2 * count * MIB, transcendentals=0
        ),
        name="square",
    )(groups, leader, mask, left, *inners, *others)


def cubed_kernel(is_last, groups, slots, inner_at, target, *refs):
    filtered, refs = refs[:4], refs[4:]
    count = len(refs) - 7
    pieces, (before, out, held_f, held_p, total, sem_f, sem_p) = refs[:count], refs[count:]
    steps, spare = held_f.shape[0] - 1, held_f.shape[0] - 1

    def f_start(m):
        place, core = slots[m] // 2, slots[m] % 2
        for n, blocks in enumerate(filtered):
            first = n // 2 * len(EARLY)
            found = (place >= first) & (place < first + blocks.shape[0])

            @pl.when(found & (core == n % 2))
            def _():
                pltpu.make_async_copy(
                    blocks.at[place - first], held_f.at[m], sem_f.at[m]
                ).start()

    def f_wait(m):
        pltpu.make_async_copy(filtered[0].at[0], held_f.at[m], sem_f.at[m]).wait()

    if is_last:
        last = pltpu.make_async_copy(before, total, sem_f.at[spare])
    else:
        last = pltpu.make_async_copy(filtered[0].at[0], held_f.at[spare], sem_f.at[spare])
    last.start()
    m = 0
    for piece in pieces:
        for first in range(0, piece.shape[0], GROUP):
            f_start(m)
            pltpu.make_async_copy(
                piece.at[pl.ds(first, GROUP)], held_p.at[m], sem_p.at[m]
            ).start()
            m += 1
    if is_last:
        last.wait()
    else:
        total[...] = jnp.zeros_like(total)

    @pl.loop(0, steps)
    def _(m):
        f_wait(m)
        pltpu.make_async_copy(
            pieces[0].at[pl.ds(0, GROUP)], held_p.at[m], sem_p.at[m]
        ).wait()
        base = groups[m] * 32
        for n in range(32):
            at = target[base + n] + n // 16 * GROUP
            total[at] += jnp.dot(
                held_f[m, n],
                held_p[m, inner_at[base + n]],
                preferred_element_type=jnp.float32,
            )

    if is_last:
        for i in range(2):
            for j in range(GROUP):
                out[i * B : (i + 1) * B, j * B : (j + 1) * B] = (
                    -2.0 * total[i * GROUP + j]
                ).astype(jnp.bfloat16)
    else:
        last.wait()
        own = groups[steps] * 32
        for n in range(32):
            at = inner_at[own + n] + n // 16 * GROUP
            total[at] += -1.5 * held_f[spare, n].astype(jnp.float32)
        copy = pltpu.make_async_copy(total, out, sem_f.at[spare])
        copy.start()
        copy.wait()


def cubed(groups, slots, inner_at, target, filtered, pieces, before):
    is_last = before is not None
    steps = sum(piece.shape[0] for piece in pieces) // GROUP
    if is_last:
        shape = jax.ShapeDtypeStruct((2 * B, GROUP * B), jnp.bfloat16)
        spec = pl.BlockSpec(memory_space=pltpu.VMEM)
    else:
        shape = jax.ShapeDtypeStruct((64, B, B), jnp.float32)
        spec = pl.BlockSpec(memory_space=pltpu.HBM)
        before = filtered[0]
    return pl.pallas_call(
        functools.partial(cubed_kernel, is_last),
        grid_spec=pltpu.PrefetchScalarGridSpec(
            num_scalar_prefetch=4,
            grid=(),
            in_specs=[pl.BlockSpec(memory_space=pltpu.HBM)] * (5 + len(pieces)),
            out_specs=spec,
            scratch_shapes=[
                pltpu.VMEM((steps + 1, 32, B, B), jnp.bfloat16),
                pltpu.VMEM((steps, GROUP, B, B), jnp.bfloat16),
                pltpu.VMEM((64, B, B), jnp.float32),
                pltpu.SemaphoreType.DMA((steps + 1,)),
                pltpu.SemaphoreType.DMA((steps,)),
            ],
        ),
        out_shape=shape,
        compiler_params=pltpu.CompilerParams(vmem_limit_bytes=ROOM),
        cost_estimate=pl.CostEstimate(
            flops=4 * steps * 32 * 2 * B**3,
            bytes_accessed=(2 * steps + 5) * MIB,
            transcendentals=0,
        ),
        name="cubed",
    )(groups, slots, inner_at, target, *filtered, *pieces, before)


def is_equal(values, count):
    return values[..., None] == jnp.arange(count, dtype=jnp.int32)


def picked(values, table):
    return jnp.sum(jnp.where(is_equal(values, table.shape[0]), table, 0), axis=-1)


def local(owned_blocks, owned_rows, owned_cols, keep):
    r, c = lax.axis_index("row"), lax.axis_index("col")
    tags = jnp.concatenate(
        [owned_cols.reshape(-1), owned_rows, keep.reshape(-1), jnp.zeros(688, jnp.int32)]
    )
    outgoing = spread(owned_blocks)
    arrived = lax.all_to_all(
        outgoing.reshape(ROWS * COLS, 2, B, B), AXES, split_axis=0, concat_axis=0, tiled=True
    ).reshape(256, B, B)

    tags = lax.all_to_all(
        jnp.broadcast_to(tags.reshape(1, 8, 128), (ROWS * COLS, 8, 128)),
        AXES,
        split_axis=0,
        concat_axis=0,
        tiled=True,
    )
    all_rows = tags[:, 2, :16]
    all_cols = tags[:, :2].reshape(2048, COLS)
    bands = (jnp.arange(16, dtype=jnp.int32) // 2)[None]
    ids = GROUP * (bands + ROWS * (all_rows // GROUP)) + all_rows % GROUP
    ids = jnp.where(all_rows < 64, ids, -1).reshape(2048)
    spots = (ids[None] == jnp.arange(512, dtype=jnp.int32)[:, None]).astype(jnp.bfloat16)
    cols = jnp.dot(
        spots, all_cols.astype(jnp.bfloat16), preferred_element_type=jnp.float32
    ).astype(jnp.int32)

    band_tags = lax.dynamic_slice_in_dim(all_rows, 2 * r, 2, 1).reshape(256)
    place = jnp.sum(
        jnp.where(
            band_tags[None] == jnp.arange(64, dtype=jnp.int32)[:, None],
            jnp.arange(256, dtype=jnp.int32)[None],
            0,
        ),
        axis=1,
    )
    window_cols = cols.reshape(16, GROUP, COLS)[:ROWS, :2]
    wanted = lax.dynamic_slice_in_dim(
        window_cols.reshape(ROWS, 2, 2, ROWS), r, 1, 3
    )[..., 0]
    wanted = wanted + GROUP * jnp.arange(2, dtype=jnp.int32)
    where = jnp.concatenate([picked(wanted.reshape(32), place), place[:2]])

    mine = lax.dynamic_index_in_dim(window_cols, r, 0, keepdims=False)
    rows_in = (mine + GROUP * jnp.arange(COLS, dtype=jnp.int32)[None]).reshape(32)
    tcol = (
        jnp.dot(
            is_equal(rows_in, 512).astype(jnp.bfloat16),
            cols.astype(jnp.bfloat16),
            preferred_element_type=jnp.float32,
        )
        .astype(jnp.int32)
        .reshape(2, 16, COLS)
    )
    my_cols = lax.dynamic_slice_in_dim(cols, c, 1, 1).reshape(COLS, GROUP)
    inner_at = tcol.transpose(2, 0, 1)
    target = jnp.sum(
        jnp.where(is_equal(inner_at, GROUP), my_cols[:, None, None, :], 0), axis=-1
    )
    same = inner_at[:, :, :, None] == inner_at[:, :, None, :]
    order = jnp.arange(16, dtype=jnp.int32)
    leader = jnp.min(jnp.where(same, order, 16), axis=-1)
    keep = lax.dynamic_slice_in_dim(tags[:, 2, 16:80], r * COLS, COLS, 0)
    keep = keep.reshape(COLS, 2, 1, GROUP)
    kept = jnp.sum(jnp.where(is_equal(inner_at, GROUP), keep, 0), axis=-1)
    mask = jnp.where(leader == order, kept, 0)
    leader, mask = leader.reshape(512), mask.reshape(512)

    inner, window = pack(where[:32], arrived)[0], pack(where[32:], arrived)[0]
    band = pack(place, arrived, [inner, window], 2)
    left = lax.all_gather(window, "col", axis=0, tiled=True).reshape(COLS, 2, B, B)
    inner = lax.all_to_all(
        inner.reshape(ROWS, 4, B, B), "row", split_axis=0, concat_axis=0, tiled=True
    ).reshape(32, B, B)

    p, f = {(0, 0, 0): band[0]}, {}
    p[1, 0, 0] = send_row(band[0], -1, 0)
    p[3, 0, 0] = send_row(band[0], 1, 0)
    p[0, 1, 0] = send_row(band[0], 0, 1)
    f[1, 0] = send_col(inner, -1, 0, 0)
    f[3, 0] = send_col(inner, 1, 0, 0)

    keys = [(1, 0, 0), (3, 0, 0), (0, 1, 0)]
    second, f[0, 0], f[1, 0], f[3, 0], *held = after(
        [band[1], inner, f[1, 0], f[3, 0]] + [p[key] for key in keys], []
    )
    p.update(zip(keys, held))
    p[1, 0, 1] = send_row(second, -1, 0)
    p[3, 0, 1] = send_row(second, 1, 0)
    f[0, 1] = send_col(f[0, 0], 0, 1, 0)
    f[2, 0] = send_col(f[1, 0], -1, 0, 0)

    p[0, 0, 1], p[1, 0, 0], p[3, 0, 1], f[0, 1], f[2, 0] = after(
        [second, p[1, 0, 0], p[3, 0, 1], f[0, 1], f[2, 0]], [p[1, 0, 1]]
    )
    p[2, 0, 0] = send_row(p[1, 0, 0], -1, 0)
    p[2, 0, 1] = send_row(p[3, 0, 1], 1, 0)
    p[0, 1, 1] = send_row(p[0, 0, 1], 0, 1)
    f[1, 1] = send_col(f[0, 1], -1, 0, 0)
    f[3, 1] = send_col(f[0, 1], 1, 0, 0)

    p[0, 1, 0], p[2, 0, 0], f[3, 1], f[1, 1] = after(
        [p[0, 1, 0], p[2, 0, 0], f[3, 1], f[1, 1]], [p[2, 0, 1], p[0, 1, 1]]
    )
    p[1, 1, 0] = send_row(p[0, 1, 0], -1, 0)
    p[3, 1, 0] = send_row(p[0, 1, 0], 1, 0)
    p[2, 1, 0] = send_row(p[2, 0, 0], 0, 1)
    f[2, 1] = send_col(f[3, 1], 1, 0, 0)

    def squares(keys, others):
        ids = [(c // 4 + dx) % 4 * 4 + ((c % 4) ^ (2 * dz)) for dx, dz in keys]
        ids = jnp.stack(ids).astype(jnp.int32)
        return square(ids, leader, mask, left, [f[key] for key in keys], others)

    early, p[0, 1, 1], p[2, 0, 1], f[2, 1] = after(
        [squares(EARLY, []), p[0, 1, 1], p[2, 0, 1], f[2, 1]],
        [p[1, 1, 0], p[3, 1, 0], p[2, 1, 0]],
    )
    p[1, 1, 1] = send_row(p[0, 1, 1], -1, 0)
    p[3, 1, 1] = send_row(p[0, 1, 1], 1, 0)
    p[2, 1, 1] = send_row(p[2, 0, 1], 0, 1)
    filtered = [early, send_col(early, 0, 0, 1)]
    late = squares(LATE, [])
    filtered += [late, send_col(late, 0, 0, 1)]

    def products(keys, before):
        groups, slots = [], []
        for dy, dz, half in keys:
            group = (r // 2 + dy) % 4 * 2 + (r % 2 + dz) % 2 + ROWS * half
            groups.append(group)
            dx = (group // 4 - c // 4) % 4
            slots.append((dx ^ (dx // 2)) * 4 + ((group % 4) ^ (c % 4)))
        return cubed(
            jnp.stack(groups + [c]).astype(jnp.int32),
            jnp.stack(slots).astype(jnp.int32),
            inner_at.reshape(512),
            target.reshape(512),
            filtered,
            [p[key] for key in keys],
            before,
        )

    last = [(1, 1, 1), (3, 1, 1), (2, 1, 1)]
    total = products([key for key in p if key not in last], None)
    return products(last, total)


def solution(mesh):
    placed = (P(AXES, None, None, None), P(AXES), P(AXES, None), P("row", "col"))
    return jax.shard_map(
        local, mesh=mesh, in_specs=placed, out_specs=P("row", "col"), check_vma=False
    )
```

time: 340 us -> 333 us (0.979)
  waiting for transfers between devices: 253 us -> 203 us
  Pallas kernels: 20.1 us -> 50.4 us
  starting transfers between devices: 29.9 us -> 49.8 us
  local copies, waits for them, and re-layouts: 17.7 us -> 8.6 us
    all_to_all x1, waiting for transfers between devices: 55.8 us -> 5.42 us  [local(): lax.all_to_all(inner.reshape(ROWS, 4, B, B), 'row', split_axis=0, concat_...]
    ppermute x7 -> x14, waiting for transfers between devices: 90 us -> 56.5 us  [send_row(): return lax.ppermute(value, 'row', moved(by_y, flip_z))]
    ppermute x0 -> x9, waiting for transfers between devices: none -> 30.9 us  [send_col(): return lax.ppermute(value, 'col', pairs)]
    pallas_call x2 -> x10, Pallas kernels: 17.9 us -> 36.4 us  [the longest x2 21.4 us: cubed(): pl.pallas_call(functools.partial(cubed_kernel, is_last), grid_spec=pltpu....]
    pallas_call x1 -> x2, Pallas kernels: 2.19 us -> 14 us  [square(): pl.pallas_call(square_kernel, grid_spec=pltpu.PrefetchScalarGridSpec(num_...]
    ppermute x7 -> x14, starting transfers between devices: 6.67 us -> 18.2 us  [send_row(): return lax.ppermute(value, 'row', moved(by_y, flip_z))]
    transpose x1 -> x0, local copies, waits for them, and re-layouts: 10.3 us -> none  [local(): owned_blocks.reshape(ROWS, 2, COLS, B, B).transpose(0, 2, 1, 3, 4)]
    ppermute x0 -> x9, starting transfers between devices: none -> 10.3 us  [send_col(): return lax.ppermute(value, 'col', pairs)]
  transfers between devices with their start and end apart: 12 -> 27, of which waited for: 7 -> 21; matrix products, arithmetic and copies ran while one was open for 5% -> 4% of each run, Pallas kernels for 0% -> 12%
where the time goes in v2:
time: 333 us; the launch traced here: 332 us
  waiting for transfers between devices  203 us (61%)
  Pallas kernels  50.4 us (15%)
  starting transfers between devices  49.8 us (15%)
  between operations  13.7 us (4%)
  local copies, waits for them, and re-layouts  8.6 us (3%)
  other arithmetic  5.51 us (2%)
    all_to_all x1, waiting for transfers between devices, local(): lax.all_to_all(outgoing.reshape(ROWS * COLS, 2, B, B), AXES, split_axis=0...  104 us
    ppermute x14, waiting for transfers between devices, send_row(): return lax.ppermute(value, 'row', moved(by_y, flip_z))  56.5 us
    ppermute x9, waiting for transfers between devices, send_col(): return lax.ppermute(value, 'col', pairs)  30.9 us
    pallas_call x2, Pallas kernels, cubed(): pl.pallas_call(functools.partial(cubed_kernel, is_last), grid_spec=pltpu....  21.4 us
    ppermute x14, starting transfers between devices, send_row(): return lax.ppermute(value, 'row', moved(by_y, flip_z))  18.2 us
    pallas_call x2, Pallas kernels, square(): pl.pallas_call(square_kernel, grid_spec=pltpu.PrefetchScalarGridSpec(num_...  14 us
    all_to_all x1, starting transfers between devices, local(): lax.all_to_all(jnp.broadcast_to(tags.reshape(1, 8, 128), (ROWS * COLS, 8,...  10.5 us
    ppermute x9, starting transfers between devices, send_col(): return lax.ppermute(value, 'col', pairs)  10.3 us
  transfers between devices with their start and end apart: 27, of which 21 were waited for; matrix products, arithmetic and copies ran while one was open for 4% of the time, Pallas kernels for 12%

profile of v2, /device:TPU:6, one launch (start us, length us, event | category | flops | bytes accessed | tf_op | source)
XLA Modules:
  0.0 331.6 jit_solution(8746898738367892108)
XLA Ops:
  9.6 10.5 %all-to-all-start = ((s32[128,8,128]{2,1,0:T(8,128)}), s32[128,8,128]{2,1,0:T(8,128)S(1)}, u32[]{:S(2)}, u32[]{:S(2)}) async-start(s32[128,8,128]{2,1,0:T(8,128)} %broadcast_in_dim.87), calls=%async_computation | async-start | bytes 1048576 | tf_op jit(solution)/shard_map/all_to_all | solution.py:322
  20.1 6.5 %spread.1 = bf16[8,16,2,128,128]{4,3,2,1,0:T(8,128)(2,1)} custom-call(bf16[16,16,128,128]{3,2,1,0:T(8,128)(2,1)} %owned.1), custom_call_target="tpu_custom_call" | custom-call | bytes 16777216 | tf_op jit(solution)/shard_map/spread/pallas_call | solution.py:60
  26.7 6.0 %all-to-all-done = s32[128,8,128]{2,1,0:T(8,128)S(1)} async-done(((s32[128,8,128]{2,1,0:T(8,128)}), s32[128,8,128]{2,1,0:T(8,128)S(1)}, u32[]{:S(2)}, u32[]{:S(2)}) %all-to-all-start) | async-done | bytes 524320 | tf_op jit(solution)/shard_map/all_to_all | solution.py:322
  32.7 6.5 %all-to-all-start.1 = ((bf16[128,2,128,128]{3,2,1,0:T(8,128)(2,1)}), bf16[128,2,128,128]{3,2,1,0:T(8,128)(2,1)}, u32[]{:S(2)}, u32[]{:S(2)}) async-start(bf16[128,2,128,128]{3,2,1,0:T(8,128)(2,1)} %bitcast.59), calls=%async_computation.1 | async-start | bytes 16777216 | tf_op jit(solution)/shard_map/all_to_all | solution.py:318
  43.0 103.6 %all-to-all-done.1 = bf16[128,2,128,128]{3,2,1,0:T(8,128)(2,1)} async-done(((bf16[128,2,128,128]{3,2,1,0:T(8,128)(2,1)}), bf16[128,2,128,128]{3,2,1,0:T(8,128)(2,1)}, u32[]{:S(2)}, u32[]{:S(2)}) %all-to-all-start.1) | async-done | bytes 8388640 | tf_op jit(solution)/shard_map/all_to_all | solution.py:318
  149.5 4.2 %all-to-all-start.2 = ((bf16[8,4,128,128]{3,2,1,0:T(8,128)(2,1)}), bf16[8,4,128,128]{3,2,1,0:T(8,128)(2,1)}, u32[]{:S(2)}, u32[]{:S(2)}) async-start(bf16[8,4,128,128]{3,2,1,0:T(8,128)(2,1)} %bitcast.60), calls=%async_computation.2 | async-start | bytes 2097152 | tf_op jit(solution)/shard_map/all_to_all | solution.py:383
  155.8 3.6 %pack.5 = (bf16[32,128,128]{2,1,0:T(8,128)(2,1)}, bf16[32,128,128]{2,1,0:T(8,128)(2,1)}) custom-call(s32[64]{0:T(128)} %copy-done.1, bf16[256,128,128]{2,1,0:T(8,128)(2,1)} %bitcast.17.arrived, bf16[32,128,128]{2,1,0:T(8,128)(2,1)} %pack.4.refs_0_, bf16[2,128,128]{2,1,0:T(8,128)(2,1)} %pack.3.refs_1_), custom_call_target="tpu_custom_call" | custom-call | bytes 4194304 | tf_op jit(solution)/shard_map/pack/pallas_call | solution.py:115
  159.4 3.2 collective-permute-start.2
  165.5 5.4 %all-to-all-done.2 = bf16[8,4,128,128]{3,2,1,0:T(8,128)(2,1)} async-done(((bf16[8,4,128,128]{3,2,1,0:T(8,128)(2,1)}), bf16[8,4,128,128]{3,2,1,0:T(8,128)(2,1)}, u32[]{:S(2)}, u32[]{:S(2)}) %all-to-all-start.2) | async-done | bytes 1048608 | tf_op jit(solution)/shard_map/all_to_all | solution.py:383
  171.0 4.8 %collective-permute-start = (bf16[32,128,128]{2,1,0:T(8,128)(2,1)}, bf16[32,128,128]{2,1,0:T(8,128)(2,1)}, u32[]{:S(2)}, u32[]{:S(2)}) collective-permute-start(bf16[32,128,128]{2,1,0:T(8,128)(2,1)} %bitcast.20.refs_1_), channel_id=1, source_target_pairs={{0,12},{1,13},{2,14},{3,15},{4,0},{5,1},{6,2},{7,3},{8,4},{9,5},{1... | collective-permute-start | bytes 3145736 | tf_op jit(solution)/shard_map/ppermute | solution.py:33
  175.8 14.2 %collective-permute-done.2.refs_4_ = bf16[32,128,128]{2,1,0:T(8,128)(2,1)} collective-permute-done((bf16[32,128,128]{2,1,0:T(8,128)(2,1)}, bf16[32,128,128]{2,1,0:T(8,128)(2,1)}, u32[]{:S(2)}, u32[]{:S(2)}) %collective-permute-start.2) | collective-permute-done | bytes 1048608 | tf_op jit(solution)/shard_map/ppermute | solution.py:37
  192.2 4.4 %collective-permute-done.refs_2_ = bf16[32,128,128]{2,1,0:T(8,128)(2,1)} collective-permute-done((bf16[32,128,128]{2,1,0:T(8,128)(2,1)}, bf16[32,128,128]{2,1,0:T(8,128)(2,1)}, u32[]{:S(2)}, u32[]{:S(2)}) %collective-permute-start) | collective-permute-done | bytes 1048608 | tf_op jit(solution)/shard_map/ppermute | solution.py:33
  201.3 19.7 %collective-permute-done.8.refs_5_.refs_8_ = bf16[32,128,128]{2,1,0:T(8,128)(2,1)} collective-permute-done((bf16[32,128,128]{2,1,0:T(8,128)(2,1)}, bf16[32,128,128]{2,1,0:T(8,128)(2,1)}, u32[]{:S(2)}, u32[]{:S(2)}) %collective-permute-start.8) | collective-permute-done | bytes 1048608 | tf_op jit(solution)/shard_map/ppermute | solution.py:37
  221.0 3.5 %collective-permute-done.5.refs_2_ = bf16[32,128,128]{2,1,0:T(8,128)(2,1)} collective-permute-done((bf16[32,128,128]{2,1,0:T(8,128)(2,1)}, bf16[32,128,128]{2,1,0:T(8,128)(2,1)}, u32[]{:S(2)}, u32[]{:S(2)}) %collective-permute-start.5) | collective-permute-done | bytes 1048608 | tf_op jit(solution)/shard_map/ppermute | solution.py:37
  230.2 19.3 %collective-permute-done.10.refs_2_ = bf16[32,128,128]{2,1,0:T(8,128)(2,1)} collective-permute-done((bf16[32,128,128]{2,1,0:T(8,128)(2,1)}, bf16[32,128,128]{2,1,0:T(8,128)(2,1)}, u32[]{:S(2)}, u32[]{:S(2)}) %collective-permute-start.10) | collective-permute-done | bytes 1048608 | tf_op jit(solution)/shard_map/ppermute | solution.py:33
  250.8 4.4 %collective-permute-done.13.refs_5_.refs_1_ = bf16[32,128,128]{2,1,0:T(8,128)(2,1)} collective-permute-done((bf16[32,128,128]{2,1,0:T(8,128)(2,1)}, bf16[32,128,128]{2,1,0:T(8,128)(2,1)}, u32[]{:S(2)}, u32[]{:S(2)}) %collective-permute-start.13) | collective-permute-done | bytes 1048608 | tf_op jit(solution)/shard_map/ppermute | solution.py:37
  264.7 9.1 %square.2.refs_0_ = bf16[7,32,128,128]{3,2,1,0:T(8,128)(2,1)} custom-call(s32[7]{0:T(128)} %stack.155.groups, s32[512]{0:T(512)} %copy-done, s32[512]{0:T(512)} %compare_select_fusion.mask, bf16[16,2,128,128]{3,2,1,0:T(8,128)(2,1)} %bitcast.61, bf16[32,128,128]{2,1,0:T(8,128)(2,1)} %get-tuple-element.29.refs_0_, ...), custom_call_target="tpu_custom_call" | custom-call | flops 939524096 | bytes 14680064 | tf_op jit(solution)/shard_map/square/pallas_call | solution.py:172
  273.8 3.6 %collective-permute-done.14.refs_3_ = bf16[32,128,128]{2,1,0:T(8,128)(2,1)} collective-permute-done((bf16[32,128,128]{2,1,0:T(8,128)(2,1)}, bf16[32,128,128]{2,1,0:T(8,128)(2,1)}, u32[]{:S(2)}, u32[]{:S(2)}) %collective-permute-start.14) | collective-permute-done | bytes 1048608 | tf_op jit(solution)/shard_map/ppermute | solution.py:33
  277.6 3.4 %collective-permute-done.16.refs_5_.refs_15_ = bf16[32,128,128]{2,1,0:T(8,128)(2,1)} collective-permute-done((bf16[32,128,128]{2,1,0:T(8,128)(2,1)}, bf16[32,128,128]{2,1,0:T(8,128)(2,1)}, u32[]{:S(2)}, u32[]{:S(2)}) %collective-permute-start.16) | collective-permute-done | bytes 1048608 | tf_op jit(solution)/shard_map/ppermute | solution.py:37
  282.4 4.9 %square.3.refs_2_ = bf16[1,32,128,128]{3,2,1,0:T(8,128)(2,1)} custom-call(s32[1]{0:T(128)} %bitcast.21.groups, s32[512]{0:T(512)} %copy-done, s32[512]{0:T(512)} %compare_select_fusion.mask, bf16[16,2,128,128]{3,2,1,0:T(8,128)(2,1)} %bitcast.62, bf16[32,128,128]{2,1,0:T(8,128)(2,1)} %get-tuple-element.45.refs_0_), custom_call_target="tpu_custom_call" | custom-call | flops 134217728 | bytes 2097152 | tf_op jit(solution)/shard_map/square/pallas_call | solution.py:172
  295.9 14.1 %cubed.2.refs_7_ = f32[64,128,128]{2,1,0:T(8,128)} custom-call(s32[14]{0:T(128)} %stack.170.groups, s32[13]{0:T(128)} %stack.184.slots, s32[512]{0:T(512)} %reshape.170.inner_at, s32[512]{0:T(512)} %reshape.171.target, bf16[7,32,128,128]{3,2,1,0:T(8,128)(2,1)} %get-tuple-element.44.refs_0_.refs_17_, ...), custom_call_target="tpu_custom_call" | custom-call | flops 6979321856 | bytes 32505856 | tf_op jit(solution)/shard_map/cubed/pallas_call | solution.py:278
  310.0 3.8 %collective-permute-done.20.refs_4_ = bf16[32,128,128]{2,1,0:T(8,128)(2,1)} collective-permute-done((bf16[32,128,128]{2,1,0:T(8,128)(2,1)}, bf16[32,128,128]{2,1,0:T(8,128)(2,1)}, u32[]{:S(2)}, u32[]{:S(2)}) %collective-permute-start.20) | collective-permute-done | bytes 1048608 | tf_op jit(solution)/shard_map/ppermute | solution.py:37
  313.8 3.4 %collective-permute-done.21.refs_5_ = bf16[32,128,128]{2,1,0:T(8,128)(2,1)} collective-permute-done((bf16[32,128,128]{2,1,0:T(8,128)(2,1)}, bf16[32,128,128]{2,1,0:T(8,128)(2,1)}, u32[]{:S(2)}, u32[]{:S(2)}) %collective-permute-start.21) | collective-permute-done | bytes 1048608 | tf_op jit(solution)/shard_map/ppermute | solution.py:37
  317.5 7.3 %cubed.3 = bf16[256,4096]{1,0:T(8,128)(2,1)} custom-call(s32[4]{0:T(128)} %pad_add_fusion.groups, s32[3]{0:T(128)} %pad_add_fusion.1.slots, s32[512]{0:T(512)} %reshape.170.inner_at, s32[512]{0:T(512)} %reshape.171.target, bf16[7,32,128,128]{3,2,1,0:T(8,128)(2,1)} %get-tuple-element.44.refs_0_.refs_17_, ...), custom_call_target="tpu_custom_call" | custom-call | flops 1610612736 | bytes 11534336 | tf_op jit(solution)/shard_map/cubed/pallas_call | solution.py:278
  (103 shorter events, 48.6 us)
Async XLA Ops:
  9.6 23.0 %all-to-all-start = ((s32[128,8,128]{2,1,0:T(8,128)}), s32[128,8,128]{2,1,0:T(8,128)S(1)}, u32[]{:S(2)}, u32[]{:S(2)}) async-start(s32[128,8,128]{2,1,0:T(8,128)} %broadcast_in_dim.87), calls=%async_computation | async-start | bytes 1048576 | tf_op jit(solution)/shard_map/all_to_all | solution.py:322
  32.7 113.9 %all-to-all-start.1 = ((bf16[128,2,128,128]{3,2,1,0:T(8,128)(2,1)}), bf16[128,2,128,128]{3,2,1,0:T(8,128)(2,1)}, u32[]{:S(2)}, u32[]{:S(2)}) async-start(bf16[128,2,128,128]{3,2,1,0:T(8,128)(2,1)} %bitcast.59), calls=%async_computation.1 | async-start | bytes 16777216 | tf_op jit(solution)/shard_map/all_to_all | solution.py:318
  149.5 21.5 %all-to-all-start.2 = ((bf16[8,4,128,128]{3,2,1,0:T(8,128)(2,1)}), bf16[8,4,128,128]{3,2,1,0:T(8,128)(2,1)}, u32[]{:S(2)}, u32[]{:S(2)}) async-start(bf16[8,4,128,128]{3,2,1,0:T(8,128)(2,1)} %bitcast.60), calls=%async_computation.2 | async-start | bytes 2097152 | tf_op jit(solution)/shard_map/all_to_all | solution.py:383
  153.7 111.0 %all-gather.2.cloned.1.call-start = ((), (), s32[]{:S(2)}) async-start(), calls=%async_computation.3 | async-start | bytes 1114112 | tf_op jit(solution)/shard_map/all_gather | solution.py:382
  159.4 30.5 %collective-permute-start.2 = (bf16[32,128,128]{2,1,0:T(8,128)(2,1)}, bf16[32,128,128]{2,1,0:T(8,128)(2,1)}, u32[]{:S(2)}, u32[]{:S(2)}) collective-permute-start(bf16[32,128,128]{2,1,0:T(8,128)(2,1)} %get-tuple-element.28.refs_4_), channel_id=1, source_target_pairs={{0,96},{16,112},{32,0},{48,16},{64,32},{80,48},{96,64},{112,80},{1... | collective-permute-start | bytes 3145736 | tf_op jit(solution)/shard_map/ppermute | solution.py:37
  162.6 29.6 %collective-permute-start.3 = (bf16[32,128,128]{2,1,0:T(8,128)(2,1)}, bf16[32,128,128]{2,1,0:T(8,128)(2,1)}, u32[]{:S(2)}, u32[]{:S(2)}) collective-permute-start(bf16[32,128,128]{2,1,0:T(8,128)(2,1)} %get-tuple-element.28.refs_4_), channel_id=1, source_target_pairs={{0,32},{16,48},{32,64},{48,80},{64,96},{80,112},{96,0},{112,16},{1... | collective-permute-start | bytes 3145736 | tf_op jit(solution)/shard_map/ppermute | solution.py:37
  162.6 29.6 %collective-permute-start.4 = (bf16[32,128,128]{2,1,0:T(8,128)(2,1)}, bf16[32,128,128]{2,1,0:T(8,128)(2,1)}, u32[]{:S(2)}, u32[]{:S(2)}) collective-permute-start(bf16[32,128,128]{2,1,0:T(8,128)(2,1)} %get-tuple-element.28.refs_4_), channel_id=1, source_target_pairs={{0,16},{16,0},{32,48},{48,32},{64,80},{80,64},{96,112},{112,96},{1... | collective-permute-start | bytes 3145736 | tf_op jit(solution)/shard_map/ppermute | solution.py:37
  171.0 25.7 %collective-permute-start = (bf16[32,128,128]{2,1,0:T(8,128)(2,1)}, bf16[32,128,128]{2,1,0:T(8,128)(2,1)}, u32[]{:S(2)}, u32[]{:S(2)}) collective-permute-start(bf16[32,128,128]{2,1,0:T(8,128)(2,1)} %bitcast.20.refs_1_), channel_id=1, source_target_pairs={{0,12},{1,13},{2,14},{3,15},{4,0},{5,1},{6,2},{7,3},{8,4},{9,5},{1... | collective-permute-start | bytes 3145736 | tf_op jit(solution)/shard_map/ppermute | solution.py:33
  175.8 23.1 %collective-permute-start.1 = (bf16[32,128,128]{2,1,0:T(8,128)(2,1)}, bf16[32,128,128]{2,1,0:T(8,128)(2,1)}, u32[]{:S(2)}, u32[]{:S(2)}) collective-permute-start(bf16[32,128,128]{2,1,0:T(8,128)(2,1)} %bitcast.20.refs_1_), channel_id=1, source_target_pairs={{0,4},{1,5},{2,6},{3,7},{4,8},{5,9},{6,10},{7,11},{8,12},{9,13},{1... | collective-permute-start | bytes 3145736 | tf_op jit(solution)/shard_map/ppermute | solution.py:33
  198.8 22.1 %collective-permute-start.8 = (bf16[32,128,128]{2,1,0:T(8,128)(2,1)}, bf16[32,128,128]{2,1,0:T(8,128)(2,1)}, u32[]{:S(2)}, u32[]{:S(2)}) collective-permute-start(bf16[32,128,128]{2,1,0:T(8,128)(2,1)} %get-tuple-element.30.refs_0_), channel_id=1, source_target_pairs={{0,96},{16,112},{32,0},{48,16},{64,32},{80,48},{96,64},{112,80},{1... | collective-permute-start | bytes 3145736 | tf_op jit(solution)/shard_map/ppermute | solution.py:37
  198.8 25.6 %collective-permute-start.5 = (bf16[32,128,128]{2,1,0:T(8,128)(2,1)}, bf16[32,128,128]{2,1,0:T(8,128)(2,1)}, u32[]{:S(2)}, u32[]{:S(2)}) collective-permute-start(bf16[32,128,128]{2,1,0:T(8,128)(2,1)} %get-tuple-element.30.refs_0_), channel_id=1, source_target_pairs={{0,32},{16,48},{32,64},{48,80},{64,96},{80,112},{96,0},{112,16},{1... | collective-permute-start | bytes 3145736 | tf_op jit(solution)/shard_map/ppermute | solution.py:37
  200.9 23.6 %collective-permute-start.6 = (bf16[32,128,128]{2,1,0:T(8,128)(2,1)}, bf16[32,128,128]{2,1,0:T(8,128)(2,1)}, u32[]{:S(2)}, u32[]{:S(2)}) collective-permute-start(bf16[32,128,128]{2,1,0:T(8,128)(2,1)} %get-tuple-element.29.refs_0_), channel_id=1, source_target_pairs={{0,2},{1,3},{2,0},{3,1},{4,6},{5,7},{6,4},{7,5},{8,10},{9,11},{10,... | collective-permute-start | bytes 3145736 | tf_op jit(solution)/shard_map/ppermute | solution.py:33
  200.9 23.6 %collective-permute-start.7 = (bf16[32,128,128]{2,1,0:T(8,128)(2,1)}, bf16[32,128,128]{2,1,0:T(8,128)(2,1)}, u32[]{:S(2)}, u32[]{:S(2)}) collective-permute-start(bf16[32,128,128]{2,1,0:T(8,128)(2,1)} %get-tuple-element.32.refs_2_), channel_id=1, source_target_pairs={{0,12},{1,13},{2,14},{3,15},{4,0},{5,1},{6,2},{7,3},{8,4},{9,5},{1... | collective-permute-start | bytes 3145736 | tf_op jit(solution)/shard_map/ppermute | solution.py:33
  224.4 25.0 %collective-permute-start.10 = (bf16[32,128,128]{2,1,0:T(8,128)(2,1)}, bf16[32,128,128]{2,1,0:T(8,128)(2,1)}, u32[]{:S(2)}, u32[]{:S(2)}) collective-permute-start(bf16[32,128,128]{2,1,0:T(8,128)(2,1)} %get-tuple-element.33.refs_1_), channel_id=1, source_target_pairs={{0,4},{1,5},{2,6},{3,7},{4,8},{5,9},{6,10},{7,11},{8,12},{9,13},{1... | collective-permute-start | bytes 3145736 | tf_op jit(solution)/shard_map/ppermute | solution.py:33
  226.3 24.5 %collective-permute-start.11 = (bf16[32,128,128]{2,1,0:T(8,128)(2,1)}, bf16[32,128,128]{2,1,0:T(8,128)(2,1)}, u32[]{:S(2)}, u32[]{:S(2)}) collective-permute-start(bf16[32,128,128]{2,1,0:T(8,128)(2,1)} %get-tuple-element.33.refs_1_), channel_id=1, source_target_pairs={{0,12},{1,13},{2,14},{3,15},{4,0},{5,1},{6,2},{7,3},{8,4},{9,5},{1... | collective-permute-start | bytes 3145736 | tf_op jit(solution)/shard_map/ppermute | solution.py:33
  226.5 24.3 %collective-permute-start.12 = (bf16[32,128,128]{2,1,0:T(8,128)(2,1)}, bf16[32,128,128]{2,1,0:T(8,128)(2,1)}, u32[]{:S(2)}, u32[]{:S(2)}) collective-permute-start(bf16[32,128,128]{2,1,0:T(8,128)(2,1)} %get-tuple-element.36.refs_9_), channel_id=1, source_target_pairs={{0,32},{16,48},{32,64},{48,80},{64,96},{80,112},{96,0},{112,16},{1... | collective-permute-start | bytes 3145736 | tf_op jit(solution)/shard_map/ppermute | solution.py:37
  228.8 26.4 %collective-permute-start.13 = (bf16[32,128,128]{2,1,0:T(8,128)(2,1)}, bf16[32,128,128]{2,1,0:T(8,128)(2,1)}, u32[]{:S(2)}, u32[]{:S(2)}) collective-permute-start(bf16[32,128,128]{2,1,0:T(8,128)(2,1)} %get-tuple-element.37.refs_10_), channel_id=1, source_target_pairs={{0,16},{16,0},{32,48},{48,32},{64,80},{80,64},{96,112},{112,96},{1... | collective-permute-start | bytes 3145736 | tf_op jit(solution)/shard_map/ppermute | solution.py:37
  228.8 26.4 %collective-permute-start.9 = (bf16[32,128,128]{2,1,0:T(8,128)(2,1)}, bf16[32,128,128]{2,1,0:T(8,128)(2,1)}, u32[]{:S(2)}, u32[]{:S(2)}) collective-permute-start(bf16[32,128,128]{2,1,0:T(8,128)(2,1)} %get-tuple-element.35.refs_5_), channel_id=1, source_target_pairs={{0,96},{16,112},{32,0},{48,16},{64,32},{80,48},{96,64},{112,80},{1... | collective-permute-start | bytes 3145736 | tf_op jit(solution)/shard_map/ppermute | solution.py:37
  255.2 22.2 %collective-permute-start.14 = (bf16[32,128,128]{2,1,0:T(8,128)(2,1)}, bf16[32,128,128]{2,1,0:T(8,128)(2,1)}, u32[]{:S(2)}, u32[]{:S(2)}) collective-permute-start(bf16[32,128,128]{2,1,0:T(8,128)(2,1)} %get-tuple-element.40.refs_5_), channel_id=1, source_target_pairs={{0,4},{1,5},{2,6},{3,7},{4,8},{5,9},{6,10},{7,11},{8,12},{9,13},{1... | collective-permute-start | bytes 3145736 | tf_op jit(solution)/shard_map/ppermute | solution.py:33
  259.9 21.1 %collective-permute-start.16 = (bf16[32,128,128]{2,1,0:T(8,128)(2,1)}, bf16[32,128,128]{2,1,0:T(8,128)(2,1)}, u32[]{:S(2)}, u32[]{:S(2)}) collective-permute-start(bf16[32,128,128]{2,1,0:T(8,128)(2,1)} %get-tuple-element.42.refs_7_), channel_id=1, source_target_pairs={{0,32},{16,48},{32,64},{48,80},{64,96},{80,112},{96,0},{112,16},{1... | collective-permute-start | bytes 3145736 | tf_op jit(solution)/shard_map/ppermute | solution.py:37
  259.9 22.4 %collective-permute-start.17 = (bf16[32,128,128]{2,1,0:T(8,128)(2,1)}, bf16[32,128,128]{2,1,0:T(8,128)(2,1)}, u32[]{:S(2)}, u32[]{:S(2)}) collective-permute-start(bf16[32,128,128]{2,1,0:T(8,128)(2,1)} %get-tuple-element.43.refs_11_), channel_id=1, source_target_pairs={{0,16},{16,0},{32,48},{48,32},{64,80},{80,64},{96,112},{112,96},{1... | collective-permute-start | bytes 3145736 | tf_op jit(solution)/shard_map/ppermute | solution.py:37
  287.8 25.9 %collective-permute-start.20 = (bf16[32,128,128]{2,1,0:T(8,128)(2,1)}, bf16[32,128,128]{2,1,0:T(8,128)(2,1)}, u32[]{:S(2)}, u32[]{:S(2)}) collective-permute-start(bf16[32,128,128]{2,1,0:T(8,128)(2,1)} %get-tuple-element.46.refs_13_), channel_id=1, source_target_pairs={{0,96},{16,112},{32,0},{48,16},{64,32},{80,48},{96,64},{112,80},{1... | collective-permute-start | bytes 3145736 | tf_op jit(solution)/shard_map/ppermute | solution.py:37
  290.8 26.4 %collective-permute-start.21 = (bf16[32,128,128]{2,1,0:T(8,128)(2,1)}, bf16[32,128,128]{2,1,0:T(8,128)(2,1)}, u32[]{:S(2)}, u32[]{:S(2)}) collective-permute-start(bf16[32,128,128]{2,1,0:T(8,128)(2,1)} %get-tuple-element.46.refs_13_), channel_id=1, source_target_pairs={{0,32},{16,48},{32,64},{48,80},{64,96},{80,112},{96,0},{112,16},{1... | collective-permute-start | bytes 3145736 | tf_op jit(solution)/shard_map/ppermute | solution.py:37
  290.8 26.7 %collective-permute-start.22 = (bf16[32,128,128]{2,1,0:T(8,128)(2,1)}, bf16[32,128,128]{2,1,0:T(8,128)(2,1)}, u32[]{:S(2)}, u32[]{:S(2)}) collective-permute-start(bf16[32,128,128]{2,1,0:T(8,128)(2,1)} %get-tuple-element.47.refs_12_), channel_id=1, source_target_pairs={{0,16},{16,0},{32,48},{48,32},{64,80},{80,64},{96,112},{112,96},{1... | collective-permute-start | bytes 3145736 | tf_op jit(solution)/shard_map/ppermute | solution.py:37
  (5 other events, 154.3 us)
Sparse Core Ops, SparseCore 0:
  230.3 34.3 all-gather.1

commit v3 on v2

--- a/solution.py
+++ b/solution.py
@@ -14,7 +14,7 @@
 MIB = 1 << 20
 ROOM = 63 * MIB
 EARLY = ((0, 0), (0, 1), (1, 0), (1, 1), (3, 0), (3, 1), (2, 0))
-LATE = ((2, 1),)
+LATE = (2, 1)
 
 
 def moved(by_y, flip_z):
@@ -195,21 +195,22 @@
 
 
 def cubed_kernel(is_last, groups, slots, inner_at, target, *refs):
-    filtered, refs = refs[:4], refs[4:]
+    filtered, refs = refs[:3], refs[3:]
     count = len(refs) - 7
     pieces, (before, out, held_f, held_p, total, sem_f, sem_p) = refs[:count], refs[count:]
     steps, spare = held_f.shape[0] - 1, held_f.shape[0] - 1
 
     def f_start(m):
         place, core = slots[m] // 2, slots[m] % 2
+        late = place == len(EARLY)
         for n, blocks in enumerate(filtered):
-            first = n // 2 * len(EARLY)
-            found = (place >= first) & (place < first + blocks.shape[0])
-
-            @pl.when(found & (core == n % 2))
+            found = late if n == 2 else (core == n) & ~late
+            where = core if n == 2 else place
+
+            @pl.when(found)
             def _():
                 pltpu.make_async_copy(
-                    blocks.at[place - first], held_f.at[m], sem_f.at[m]
+                    blocks.at[where], held_f.at[m], sem_f.at[m]
                 ).start()
 
     def f_wait(m):
@@ -280,7 +281,7 @@
         grid_spec=pltpu.PrefetchScalarGridSpec(
             num_scalar_prefetch=4,
             grid=(),
-            in_specs=[pl.BlockSpec(memory_space=pltpu.HBM)] * (5 + len(pieces)),
+            in_specs=[pl.BlockSpec(memory_space=pltpu.HBM)] * (4 + len(pieces)),
             out_specs=spec,
             scratch_shapes=[
                 pltpu.VMEM((steps + 1, 32, B, B), jnp.bfloat16),
@@ -378,7 +379,7 @@
     leader, mask = leader.reshape(512), mask.reshape(512)
 
     inner, window = pack(where[:32], arrived)[0], pack(where[32:], arrived)[0]
-    band = pack(place, arrived, [inner, window], 2)
+    band = pack(place, arrived, [inner], 2)
     left = lax.all_gather(window, "col", axis=0, tiled=True).reshape(COLS, 2, B, B)
     inner = lax.all_to_all(
         inner.reshape(ROWS, 4, B, B), "row", split_axis=0, concat_axis=0, tiled=True
@@ -392,17 +393,16 @@
     f[3, 0] = send_col(inner, 1, 0, 0)
 
     keys = [(1, 0, 0), (3, 0, 0), (0, 1, 0)]
-    second, f[0, 0], f[1, 0], f[3, 0], *held = after(
-        [band[1], inner, f[1, 0], f[3, 0]] + [p[key] for key in keys], []
-    )
+    second, *held = after([band[1]] + [p[key] for key in keys], [])
     p.update(zip(keys, held))
     p[1, 0, 1] = send_row(second, -1, 0)
     p[3, 0, 1] = send_row(second, 1, 0)
-    f[0, 1] = send_col(f[0, 0], 0, 1, 0)
+    f[0, 0] = inner
+    f[0, 1] = send_col(inner, 0, 1, 0)
     f[2, 0] = send_col(f[1, 0], -1, 0, 0)
 
-    p[0, 0, 1], p[1, 0, 0], p[3, 0, 1], f[0, 1], f[2, 0] = after(
-        [second, p[1, 0, 0], p[3, 0, 1], f[0, 1], f[2, 0]], [p[1, 0, 1]]
+    p[0, 0, 1], p[1, 0, 0], p[3, 0, 1], f[0, 1], f[2, 0], f[3, 0] = after(
+        [second, p[1, 0, 0], p[3, 0, 1], f[0, 1], f[2, 0], f[3, 0]], [p[1, 0, 1]]
     )
     p[2, 0, 0] = send_row(p[1, 0, 0], -1, 0)
     p[2, 0, 1] = send_row(p[3, 0, 1], 1, 0)
@@ -418,21 +418,23 @@
     p[2, 1, 0] = send_row(p[2, 0, 0], 0, 1)
     f[2, 1] = send_col(f[3, 1], 1, 0, 0)
 
-    def squares(keys, others):
-        ids = [(c // 4 + dx) % 4 * 4 + ((c % 4) ^ (2 * dz)) for dx, dz in keys]
+    def squares(blocks):
+        ids = [
+            (c // 4 + dx) % 4 * 4 + ((c % 4) ^ (2 * dz + core)) for dx, dz, core in blocks
+        ]
         ids = jnp.stack(ids).astype(jnp.int32)
-        return square(ids, leader, mask, left, [f[key] for key in keys], others)
+        return square(ids, leader, mask, left, list(blocks.values()), [])
 
     early, p[0, 1, 1], p[2, 0, 1], f[2, 1] = after(
-        [squares(EARLY, []), p[0, 1, 1], p[2, 0, 1], f[2, 1]],
+        [squares({(*key, 0): f[key] for key in EARLY}), p[0, 1, 1], p[2, 0, 1], f[2, 1]],
         [p[1, 1, 0], p[3, 1, 0], p[2, 1, 0]],
     )
     p[1, 1, 1] = send_row(p[0, 1, 1], -1, 0)
     p[3, 1, 1] = send_row(p[0, 1, 1], 1, 0)
     p[2, 1, 1] = send_row(p[2, 0, 1], 0, 1)
-    filtered = [early, send_col(early, 0, 0, 1)]
-    late = squares(LATE, [])
-    filtered += [late, send_col(late, 0, 0, 1)]
+    other = send_col(f[LATE], 0, 0, 1)
+    late = squares({(*LATE, 0): f[LATE], (*LATE, 1): other})
+    filtered = [early, send_col(early, 0, 0, 1), late]
 
     def products(keys, before):
         groups, slots = [], []

time: 333 us -> 329 us (0.988)
  waiting for transfers between devices: 203 us -> 190 us
  starting transfers between devices: 49.8 us -> 57 us
    ppermute x14, waiting for transfers between devices: 56.5 us -> 28.6 us  [send_row(): return lax.ppermute(value, 'row', moved(by_y, flip_z))]
    ppermute x9, waiting for transfers between devices: 30.9 us -> 43.4 us  [send_col(): return lax.ppermute(value, 'col', pairs)]
    ppermute x9, starting transfers between devices: 10.3 us -> 14 us  [send_col(): return lax.ppermute(value, 'col', pairs)]
    ppermute x14, starting transfers between devices: 18.2 us -> 21.8 us  [send_row(): return lax.ppermute(value, 'row', moved(by_y, flip_z))]
  transfers between devices with their start and end apart: 27 -> 27, of which waited for: 21 -> 20; matrix products, arithmetic and copies ran while one was open for 4% -> 4% of each run, Pallas kernels for 12% -> 12%
where the time goes in v3:
time: 329 us; the launch traced here: 327 us
  waiting for transfers between devices  190 us (58%)
  starting transfers between devices  57 us (17%)
  Pallas kernels  50.6 us (15%)
  between operations  13.7 us (4%)
  local copies, waits for them, and re-layouts  8.53 us (3%)
  other arithmetic  6.06 us (2%)
    all_to_all x1, waiting for transfers between devices, local(): lax.all_to_all(outgoing.reshape(ROWS * COLS, 2, B, B), AXES, split_axis=0...  104 us
    ppermute x9, waiting for transfers between devices, send_col(): return lax.ppermute(value, 'col', pairs)  43.4 us
    ppermute x14, waiting for transfers between devices, send_row(): return lax.ppermute(value, 'row', moved(by_y, flip_z))  28.6 us
    ppermute x14, starting transfers between devices, send_row(): return lax.ppermute(value, 'row', moved(by_y, flip_z))  21.8 us
    pallas_call x2, Pallas kernels, cubed(): pl.pallas_call(functools.partial(cubed_kernel, is_last), grid_spec=pltpu....  20.9 us
    pallas_call x2, Pallas kernels, square(): pl.pallas_call(square_kernel, grid_spec=pltpu.PrefetchScalarGridSpec(num_...  14.7 us
    ppermute x9, starting transfers between devices, send_col(): return lax.ppermute(value, 'col', pairs)  14 us
    all_to_all x1, starting transfers between devices, local(): lax.all_to_all(jnp.broadcast_to(tags.reshape(1, 8, 128), (ROWS * COLS, 8,...  10.5 us
  transfers between devices with their start and end apart: 27, of which 20 were waited for; matrix products, arithmetic and copies ran while one was open for 4% of the time, Pallas kernels for 12%

profile of v3, /device:TPU:6, one launch (start us, length us, event | category | flops | bytes accessed | tf_op | source)
XLA Modules:
  0.0 327.1 jit_solution(14946890574873188366)
XLA Ops:
  9.6 10.5 %all-to-all-start = ((s32[128,8,128]{2,1,0:T(8,128)}), s32[128,8,128]{2,1,0:T(8,128)S(1)}, u32[]{:S(2)}, u32[]{:S(2)}) async-start(s32[128,8,128]{2,1,0:T(8,128)} %broadcast_in_dim.87), calls=%async_computation | async-start | bytes 1048576 | tf_op jit(solution)/shard_map/all_to_all | solution.py:323
  20.1 6.5 %spread.1 = bf16[8,16,2,128,128]{4,3,2,1,0:T(8,128)(2,1)} custom-call(bf16[16,16,128,128]{3,2,1,0:T(8,128)(2,1)} %owned.1), custom_call_target="tpu_custom_call" | custom-call | bytes 16777216 | tf_op jit(solution)/shard_map/spread/pallas_call | solution.py:60
  26.7 6.0 %all-to-all-done = s32[128,8,128]{2,1,0:T(8,128)S(1)} async-done(((s32[128,8,128]{2,1,0:T(8,128)}), s32[128,8,128]{2,1,0:T(8,128)S(1)}, u32[]{:S(2)}, u32[]{:S(2)}) %all-to-all-start) | async-done | bytes 524320 | tf_op jit(solution)/shard_map/all_to_all | solution.py:323
  32.7 6.5 %all-to-all-start.1 = ((bf16[128,2,128,128]{3,2,1,0:T(8,128)(2,1)}), bf16[128,2,128,128]{3,2,1,0:T(8,128)(2,1)}, u32[]{:S(2)}, u32[]{:S(2)}) async-start(bf16[128,2,128,128]{3,2,1,0:T(8,128)(2,1)} %bitcast.60), calls=%async_computation.1 | async-start | bytes 16777216 | tf_op jit(solution)/shard_map/all_to_all | solution.py:319
  43.0 103.6 %all-to-all-done.1 = bf16[128,2,128,128]{3,2,1,0:T(8,128)(2,1)} async-done(((bf16[128,2,128,128]{3,2,1,0:T(8,128)(2,1)}), bf16[128,2,128,128]{3,2,1,0:T(8,128)(2,1)}, u32[]{:S(2)}, u32[]{:S(2)}) %all-to-all-start.1) | async-done | bytes 8388640 | tf_op jit(solution)/shard_map/all_to_all | solution.py:319
  149.5 4.2 %all-to-all-start.2 = ((bf16[8,4,128,128]{3,2,1,0:T(8,128)(2,1)}), bf16[8,4,128,128]{3,2,1,0:T(8,128)(2,1)}, u32[]{:S(2)}, u32[]{:S(2)}) async-start(bf16[8,4,128,128]{3,2,1,0:T(8,128)(2,1)} %bitcast.61), calls=%async_computation.2 | async-start | bytes 2097152 | tf_op jit(solution)/shard_map/all_to_all | solution.py:384
  153.8 3.5 %pack.5 = (bf16[32,128,128]{2,1,0:T(8,128)(2,1)}, bf16[32,128,128]{2,1,0:T(8,128)(2,1)}) custom-call(s32[64]{0:T(128)} %copy-done.1, bf16[256,128,128]{2,1,0:T(8,128)(2,1)} %bitcast.17.arrived, bf16[32,128,128]{2,1,0:T(8,128)(2,1)} %pack.4.refs_0_), custom_call_target="tpu_custom_call" | custom-call | bytes 4194304 | tf_op jit(solution)/shard_map/pack/pallas_call | solution.py:115
  157.3 3.2 collective-permute-start
  160.5 3.0 collective-permute-start.2
  163.4 7.5 %all-to-all-done.2 = bf16[8,4,128,128]{3,2,1,0:T(8,128)(2,1)} async-done(((bf16[8,4,128,128]{3,2,1,0:T(8,128)(2,1)}), bf16[8,4,128,128]{3,2,1,0:T(8,128)(2,1)}, u32[]{:S(2)}, u32[]{:S(2)}) %all-to-all-start.2) | async-done | bytes 1048608 | tf_op jit(solution)/shard_map/all_to_all | solution.py:384
  171.0 4.8 %collective-permute-start.5 = (bf16[32,128,128]{2,1,0:T(8,128)(2,1)}, bf16[32,128,128]{2,1,0:T(8,128)(2,1)}, u32[]{:S(2)}, u32[]{:S(2)}) collective-permute-start(bf16[32,128,128]{2,1,0:T(8,128)(2,1)} %bitcast.20.refs_0_), channel_id=1, source_target_pairs={{0,12},{1,13},{2,14},{3,15},{4,0},{5,1},{6,2},{7,3},{8,4},{9,5},{1... | collective-permute-start | bytes 3145736 | tf_op jit(solution)/shard_map/ppermute | solution.py:33
  175.8 14.2 %collective-permute-done.refs_1_ = bf16[32,128,128]{2,1,0:T(8,128)(2,1)} collective-permute-done((bf16[32,128,128]{2,1,0:T(8,128)(2,1)}, bf16[32,128,128]{2,1,0:T(8,128)(2,1)}, u32[]{:S(2)}, u32[]{:S(2)}) %collective-permute-start) | collective-permute-done | bytes 1048608 | tf_op jit(solution)/shard_map/ppermute | solution.py:37
  192.1 2.8 collective-permute-start.8
  196.6 3.1 collective-permute-start.6
  199.7 11.5 %collective-permute-done.4.refs_3_ = bf16[32,128,128]{2,1,0:T(8,128)(2,1)} collective-permute-done((bf16[32,128,128]{2,1,0:T(8,128)(2,1)}, bf16[32,128,128]{2,1,0:T(8,128)(2,1)}, u32[]{:S(2)}, u32[]{:S(2)}) %collective-permute-start.4) | collective-permute-done | bytes 1048608 | tf_op jit(solution)/shard_map/ppermute | solution.py:33
  211.2 6.0 %collective-permute-done.7.refs_5_ = bf16[32,128,128]{2,1,0:T(8,128)(2,1)} collective-permute-done((bf16[32,128,128]{2,1,0:T(8,128)(2,1)}, bf16[32,128,128]{2,1,0:T(8,128)(2,1)}, u32[]{:S(2)}, u32[]{:S(2)}) %collective-permute-start.7) | collective-permute-done | bytes 1048608 | tf_op jit(solution)/shard_map/ppermute | solution.py:33
  221.5 2.9 collective-permute-start.11
  230.7 16.0 %collective-permute-done.10.refs_2_ = bf16[32,128,128]{2,1,0:T(8,128)(2,1)} collective-permute-done((bf16[32,128,128]{2,1,0:T(8,128)(2,1)}, bf16[32,128,128]{2,1,0:T(8,128)(2,1)}, u32[]{:S(2)}, u32[]{:S(2)}) %collective-permute-start.10) | collective-permute-done | bytes 1048608 | tf_op jit(solution)/shard_map/ppermute | solution.py:33
  263.4 9.1 %square.2.refs_0_ = bf16[7,32,128,128]{3,2,1,0:T(8,128)(2,1)} custom-call(s32[7]{0:T(128)} %stack.161.groups, s32[512]{0:T(512)} %copy-done, s32[512]{0:T(512)} %compare_select_fusion.mask, bf16[16,2,128,128]{3,2,1,0:T(8,128)(2,1)} %bitcast.62, bf16[32,128,128]{2,1,0:T(8,128)(2,1)} %bitcast.20.refs_0_, bf16[32,128,128]{2,1,0:T(8,128)(2,1)} %get-tuple-element.29.refs_1_, ...), custom_call_target="tpu_custom_call" | custom-call | flops 939524096 | bytes 14680064 | tf_op jit(solution)/shard_map/square/pallas_call | solution.py:172
  276.6 3.6 %collective-permute-done.17.refs_6_.refs_15_ = bf16[32,128,128]{2,1,0:T(8,128)(2,1)} collective-permute-done((bf16[32,128,128]{2,1,0:T(8,128)(2,1)}, bf16[32,128,128]{2,1,0:T(8,128)(2,1)}, u32[]{:S(2)}, u32[]{:S(2)}) %collective-permute-start.17) | collective-permute-done | bytes 1048608 | tf_op jit(solution)/shard_map/ppermute | solution.py:37
  287.7 6.0 %collective-permute-done.19.refs_1_ = bf16[32,128,128]{2,1,0:T(8,128)(2,1)} collective-permute-done((bf16[32,128,128]{2,1,0:T(8,128)(2,1)}, bf16[32,128,128]{2,1,0:T(8,128)(2,1)}, u32[]{:S(2)}, u32[]{:S(2)}) %collective-permute-start.19) | collective-permute-done | bytes 1048608 | tf_op jit(solution)/shard_map/ppermute | solution.py:33
  293.7 5.6 %square.3.refs_2_ = bf16[2,32,128,128]{3,2,1,0:T(8,128)(2,1)} custom-call(s32[2]{0:T(128)} %pad_add_fusion.2.groups, s32[512]{0:T(512)} %copy-done, s32[512]{0:T(512)} %compare_select_fusion.mask, bf16[16,2,128,128]{3,2,1,0:T(8,128)(2,1)} %bitcast.63, bf16[32,128,128]{2,1,0:T(8,128)(2,1)} %get-tuple-element.41.refs_0_, ...), custom_call_target="tpu_custom_call" | custom-call | flops 268435456 | bytes 4194304 | tf_op jit(solution)/shard_map/square/pallas_call | solution.py:172
  299.3 13.7 %cubed.2.refs_6_ = f32[64,128,128]{2,1,0:T(8,128)} custom-call(s32[14]{0:T(128)} %stack.178.groups, s32[13]{0:T(128)} %stack.192.slots, s32[512]{0:T(512)} %reshape.170.inner_at, s32[512]{0:T(512)} %reshape.171.target, bf16[7,32,128,128]{3,2,1,0:T(8,128)(2,1)} %get-tuple-element.40.refs_0_.refs_16_, ...), custom_call_target="tpu_custom_call" | custom-call | flops 6979321856 | bytes 32505856 | tf_op jit(solution)/shard_map/cubed/pallas_call | solution.py:279
  313.1 7.2 %cubed.3 = bf16[256,4096]{1,0:T(8,128)(2,1)} custom-call(s32[4]{0:T(128)} %pad_add_fusion.groups, s32[3]{0:T(128)} %pad_add_fusion.1.slots, s32[512]{0:T(512)} %reshape.170.inner_at, s32[512]{0:T(512)} %reshape.171.target, bf16[7,32,128,128]{3,2,1,0:T(8,128)(2,1)} %get-tuple-element.40.refs_0_.refs_16_, ...), custom_call_target="tpu_custom_call" | custom-call | flops 1610612736 | bytes 11534336 | tf_op jit(solution)/shard_map/cubed/pallas_call | solution.py:279
  (104 shorter events, 52.4 us)
Async XLA Ops:
  9.6 23.0 %all-to-all-start = ((s32[128,8,128]{2,1,0:T(8,128)}), s32[128,8,128]{2,1,0:T(8,128)S(1)}, u32[]{:S(2)}, u32[]{:S(2)}) async-start(s32[128,8,128]{2,1,0:T(8,128)} %broadcast_in_dim.87), calls=%async_computation | async-start | bytes 1048576 | tf_op jit(solution)/shard_map/all_to_all | solution.py:323
  32.7 113.9 %all-to-all-start.1 = ((bf16[128,2,128,128]{3,2,1,0:T(8,128)(2,1)}), bf16[128,2,128,128]{3,2,1,0:T(8,128)(2,1)}, u32[]{:S(2)}, u32[]{:S(2)}) async-start(bf16[128,2,128,128]{3,2,1,0:T(8,128)(2,1)} %bitcast.60), calls=%async_computation.1 | async-start | bytes 16777216 | tf_op jit(solution)/shard_map/all_to_all | solution.py:319
  153.7 109.7 %all-gather.2.cloned.1.call-start = ((), (), s32[]{:S(2)}) async-start(), calls=%async_computation.3 | async-start | bytes 1114112 | tf_op jit(solution)/shard_map/all_gather | solution.py:383
  157.3 32.6 %collective-permute-start = (bf16[32,128,128]{2,1,0:T(8,128)(2,1)}, bf16[32,128,128]{2,1,0:T(8,128)(2,1)}, u32[]{:S(2)}, u32[]{:S(2)}) collective-permute-start(bf16[32,128,128]{2,1,0:T(8,128)(2,1)} %get-tuple-element.26.refs_3_), channel_id=1, source_target_pairs={{0,96},{16,112},{32,0},{48,16},{64,32},{80,48},{96,64},{112,80},{1... | collective-permute-start | bytes 3145736 | tf_op jit(solution)/shard_map/ppermute | solution.py:37
  160.5 30.9 %collective-permute-start.1 = (bf16[32,128,128]{2,1,0:T(8,128)(2,1)}, bf16[32,128,128]{2,1,0:T(8,128)(2,1)}, u32[]{:S(2)}, u32[]{:S(2)}) collective-permute-start(bf16[32,128,128]{2,1,0:T(8,128)(2,1)} %get-tuple-element.26.refs_3_), channel_id=1, source_target_pairs={{0,32},{16,48},{32,64},{48,80},{64,96},{80,112},{96,0},{112,16},{1... | collective-permute-start | bytes 3145736 | tf_op jit(solution)/shard_map/ppermute | solution.py:37
  160.5 31.6 %collective-permute-start.2 = (bf16[32,128,128]{2,1,0:T(8,128)(2,1)}, bf16[32,128,128]{2,1,0:T(8,128)(2,1)}, u32[]{:S(2)}, u32[]{:S(2)}) collective-permute-start(bf16[32,128,128]{2,1,0:T(8,128)(2,1)} %get-tuple-element.26.refs_3_), channel_id=1, source_target_pairs={{0,16},{16,0},{32,48},{48,32},{64,80},{80,64},{96,112},{112,96},{1... | collective-permute-start | bytes 3145736 | tf_op jit(solution)/shard_map/ppermute | solution.py:37
  171.0 25.7 %collective-permute-start.5 = (bf16[32,128,128]{2,1,0:T(8,128)(2,1)}, bf16[32,128,128]{2,1,0:T(8,128)(2,1)}, u32[]{:S(2)}, u32[]{:S(2)}) collective-permute-start(bf16[32,128,128]{2,1,0:T(8,128)(2,1)} %bitcast.20.refs_0_), channel_id=1, source_target_pairs={{0,12},{1,13},{2,14},{3,15},{4,0},{5,1},{6,2},{7,3},{8,4},{9,5},{1... | collective-permute-start | bytes 3145736 | tf_op jit(solution)/shard_map/ppermute | solution.py:33
  175.8 35.4 %collective-permute-start.4 = (bf16[32,128,128]{2,1,0:T(8,128)(2,1)}, bf16[32,128,128]{2,1,0:T(8,128)(2,1)}, u32[]{:S(2)}, u32[]{:S(2)}) collective-permute-start(bf16[32,128,128]{2,1,0:T(8,128)(2,1)} %bitcast.20.refs_0_), channel_id=1, source_target_pairs={{0,2},{1,3},{2,0},{3,1},{4,6},{5,7},{6,4},{7,5},{8,10},{9,11},{10,... | collective-permute-start | bytes 3145736 | tf_op jit(solution)/shard_map/ppermute | solution.py:33
  189.9 27.2 %collective-permute-start.7 = (bf16[32,128,128]{2,1,0:T(8,128)(2,1)}, bf16[32,128,128]{2,1,0:T(8,128)(2,1)}, u32[]{:S(2)}, u32[]{:S(2)}) collective-permute-start(bf16[32,128,128]{2,1,0:T(8,128)(2,1)} %bitcast.20.refs_0_), channel_id=1, source_target_pairs={{0,4},{1,5},{2,6},{3,7},{4,8},{5,9},{6,10},{7,11},{8,12},{9,13},{1... | collective-permute-start | bytes 3145736 | tf_op jit(solution)/shard_map/ppermute | solution.py:33
  192.1 25.1 %collective-permute-start.8 = (bf16[32,128,128]{2,1,0:T(8,128)(2,1)}, bf16[32,128,128]{2,1,0:T(8,128)(2,1)}, u32[]{:S(2)}, u32[]{:S(2)}) collective-permute-start(bf16[32,128,128]{2,1,0:T(8,128)(2,1)} %get-tuple-element.27.refs_0_), channel_id=1, source_target_pairs={{0,96},{16,112},{32,0},{48,16},{64,32},{80,48},{96,64},{112,80},{1... | collective-permute-start | bytes 3145736 | tf_op jit(solution)/shard_map/ppermute | solution.py:37
  194.9 24.7 %collective-permute-start.3 = (bf16[32,128,128]{2,1,0:T(8,128)(2,1)}, bf16[32,128,128]{2,1,0:T(8,128)(2,1)}, u32[]{:S(2)}, u32[]{:S(2)}) collective-permute-start(bf16[32,128,128]{2,1,0:T(8,128)(2,1)} %get-tuple-element.27.refs_0_), channel_id=1, source_target_pairs={{0,32},{16,48},{32,64},{48,80},{64,96},{80,112},{96,0},{112,16},{1... | collective-permute-start | bytes 3145736 | tf_op jit(solution)/shard_map/ppermute | solution.py:37
  196.6 24.1 %collective-permute-start.6 = (bf16[32,128,128]{2,1,0:T(8,128)(2,1)}, bf16[32,128,128]{2,1,0:T(8,128)(2,1)}, u32[]{:S(2)}, u32[]{:S(2)}) collective-permute-start(bf16[32,128,128]{2,1,0:T(8,128)(2,1)} %collective-permute-done.5.refs_2_), channel_id=1, source_target_pairs={{0,12},{1,13},{2,14},{3,15},{4,0},{5,1},{6,2},{7,3},{8,4},{9,5},{1... | collective-permute-start | bytes 3145736 | tf_op jit(solution)/shard_map/ppermute | solution.py:33
  220.7 26.1 %collective-permute-start.10 = (bf16[32,128,128]{2,1,0:T(8,128)(2,1)}, bf16[32,128,128]{2,1,0:T(8,128)(2,1)}, u32[]{:S(2)}, u32[]{:S(2)}) collective-permute-start(bf16[32,128,128]{2,1,0:T(8,128)(2,1)} %get-tuple-element.29.refs_1_), channel_id=1, source_target_pairs={{0,4},{1,5},{2,6},{3,7},{4,8},{5,9},{6,10},{7,11},{8,12},{9,13},{1... | collective-permute-start | bytes 3145736 | tf_op jit(solution)/shard_map/ppermute | solution.py:33
  221.5 25.2 %collective-permute-start.11 = (bf16[32,128,128]{2,1,0:T(8,128)(2,1)}, bf16[32,128,128]{2,1,0:T(8,128)(2,1)}, u32[]{:S(2)}, u32[]{:S(2)}) collective-permute-start(bf16[32,128,128]{2,1,0:T(8,128)(2,1)} %get-tuple-element.29.refs_1_), channel_id=1, source_target_pairs={{0,12},{1,13},{2,14},{3,15},{4,0},{5,1},{6,2},{7,3},{8,4},{9,5},{1... | collective-permute-start | bytes 3145736 | tf_op jit(solution)/shard_map/ppermute | solution.py:33
  224.5 23.5 %collective-permute-start.12 = (bf16[32,128,128]{2,1,0:T(8,128)(2,1)}, bf16[32,128,128]{2,1,0:T(8,128)(2,1)}, u32[]{:S(2)}, u32[]{:S(2)}) collective-permute-start(bf16[32,128,128]{2,1,0:T(8,128)(2,1)} %get-tuple-element.32.refs_8_), channel_id=1, source_target_pairs={{0,32},{16,48},{32,64},{48,80},{64,96},{80,112},{96,0},{112,16},{1... | collective-permute-start | bytes 3145736 | tf_op jit(solution)/shard_map/ppermute | solution.py:37
  224.5 25.6 %collective-permute-start.13 = (bf16[32,128,128]{2,1,0:T(8,128)(2,1)}, bf16[32,128,128]{2,1,0:T(8,128)(2,1)}, u32[]{:S(2)}, u32[]{:S(2)}) collective-permute-start(bf16[32,128,128]{2,1,0:T(8,128)(2,1)} %get-tuple-element.33.refs_9_), channel_id=1, source_target_pairs={{0,16},{16,0},{32,48},{48,32},{64,80},{80,64},{96,112},{112,96},{1... | collective-permute-start | bytes 3145736 | tf_op jit(solution)/shard_map/ppermute | solution.py:37
  226.0 24.0 %collective-permute-start.9 = (bf16[32,128,128]{2,1,0:T(8,128)(2,1)}, bf16[32,128,128]{2,1,0:T(8,128)(2,1)}, u32[]{:S(2)}, u32[]{:S(2)}) collective-permute-start(bf16[32,128,128]{2,1,0:T(8,128)(2,1)} %get-tuple-element.31.refs_4_), channel_id=1, source_target_pairs={{0,96},{16,112},{32,0},{48,16},{64,32},{80,48},{96,64},{112,80},{1... | collective-permute-start | bytes 3145736 | tf_op jit(solution)/shard_map/ppermute | solution.py:37
  250.1 23.6 %collective-permute-start.14 = (bf16[32,128,128]{2,1,0:T(8,128)(2,1)}, bf16[32,128,128]{2,1,0:T(8,128)(2,1)}, u32[]{:S(2)}, u32[]{:S(2)}) collective-permute-start(bf16[32,128,128]{2,1,0:T(8,128)(2,1)} %get-tuple-element.36.refs_5_), channel_id=1, source_target_pairs={{0,4},{1,5},{2,6},{3,7},{4,8},{5,9},{6,10},{7,11},{8,12},{9,13},{1... | collective-permute-start | bytes 3145736 | tf_op jit(solution)/shard_map/ppermute | solution.py:33
  251.9 23.9 %collective-permute-start.15 = (bf16[32,128,128]{2,1,0:T(8,128)(2,1)}, bf16[32,128,128]{2,1,0:T(8,128)(2,1)}, u32[]{:S(2)}, u32[]{:S(2)}) collective-permute-start(bf16[32,128,128]{2,1,0:T(8,128)(2,1)} %get-tuple-element.38.refs_6_), channel_id=1, source_target_pairs={{0,96},{16,112},{32,0},{48,16},{64,32},{80,48},{96,64},{112,80},{1... | collective-permute-start | bytes 3145736 | tf_op jit(solution)/shard_map/ppermute | solution.py:37
  254.1 22.6 %collective-permute-start.16 = (bf16[32,128,128]{2,1,0:T(8,128)(2,1)}, bf16[32,128,128]{2,1,0:T(8,128)(2,1)}, u32[]{:S(2)}, u32[]{:S(2)}) collective-permute-start(bf16[32,128,128]{2,1,0:T(8,128)(2,1)} %get-tuple-element.38.refs_6_), channel_id=1, source_target_pairs={{0,32},{16,48},{32,64},{48,80},{64,96},{80,112},{96,0},{112,16},{1... | collective-permute-start | bytes 3145736 | tf_op jit(solution)/shard_map/ppermute | solution.py:37
  256.7 23.6 %collective-permute-start.17 = (bf16[32,128,128]{2,1,0:T(8,128)(2,1)}, bf16[32,128,128]{2,1,0:T(8,128)(2,1)}, u32[]{:S(2)}, u32[]{:S(2)}) collective-permute-start(bf16[32,128,128]{2,1,0:T(8,128)(2,1)} %get-tuple-element.39.refs_10_), channel_id=1, source_target_pairs={{0,16},{16,0},{32,48},{48,32},{64,80},{80,64},{96,112},{112,96},{1... | collective-permute-start | bytes 3145736 | tf_op jit(solution)/shard_map/ppermute | solution.py:37
  280.7 32.4 %collective-permute-start.20 = (bf16[32,128,128]{2,1,0:T(8,128)(2,1)}, bf16[32,128,128]{2,1,0:T(8,128)(2,1)}, u32[]{:S(2)}, u32[]{:S(2)}) collective-permute-start(bf16[32,128,128]{2,1,0:T(8,128)(2,1)} %get-tuple-element.42.refs_12_), channel_id=1, source_target_pairs={{0,96},{16,112},{32,0},{48,16},{64,32},{80,48},{96,64},{112,80},{1... | collective-permute-start | bytes 3145736 | tf_op jit(solution)/shard_map/ppermute | solution.py:37
  282.1 31.0 %collective-permute-start.21 = (bf16[32,128,128]{2,1,0:T(8,128)(2,1)}, bf16[32,128,128]{2,1,0:T(8,128)(2,1)}, u32[]{:S(2)}, u32[]{:S(2)}) collective-permute-start(bf16[32,128,128]{2,1,0:T(8,128)(2,1)} %get-tuple-element.42.refs_12_), channel_id=1, source_target_pairs={{0,32},{16,48},{32,64},{48,80},{64,96},{80,112},{96,0},{112,16},{1... | collective-permute-start | bytes 3145736 | tf_op jit(solution)/shard_map/ppermute | solution.py:37
  282.8 30.3 %collective-permute-start.22 = (bf16[32,128,128]{2,1,0:T(8,128)(2,1)}, bf16[32,128,128]{2,1,0:T(8,128)(2,1)}, u32[]{:S(2)}, u32[]{:S(2)}) collective-permute-start(bf16[32,128,128]{2,1,0:T(8,128)(2,1)} %get-tuple-element.43.refs_11_), channel_id=1, source_target_pairs={{0,16},{16,0},{32,48},{48,32},{64,80},{80,64},{96,112},{112,96},{1... | collective-permute-start | bytes 3145736 | tf_op jit(solution)/shard_map/ppermute | solution.py:37
  (5 other events, 167.2 us)
Sparse Core Ops, SparseCore 0:
  230.9 32.5 all-gather.1

commit v4 on v2

--- a/solution.py
+++ b/solution.py
@@ -13,8 +13,8 @@
 GROUP = 32
 MIB = 1 << 20
 ROOM = 63 * MIB
-EARLY = ((0, 0), (0, 1), (1, 0), (1, 1), (3, 0), (3, 1), (2, 0))
-LATE = ((2, 1),)
+EARLY = ((0, 0), (0, 1), (1, 0), (1, 1), (3, 0), (3, 1))
+LATE = ((2, 0), (2, 1))
 
 
 def moved(by_y, flip_z):
@@ -378,60 +378,62 @@
     leader, mask = leader.reshape(512), mask.reshape(512)
 
     inner, window = pack(where[:32], arrived)[0], pack(where[32:], arrived)[0]
-    band = pack(place, arrived, [inner, window], 2)
+    band = pack(place, arrived, [inner], 2)
     left = lax.all_gather(window, "col", axis=0, tiled=True).reshape(COLS, 2, B, B)
     inner = lax.all_to_all(
         inner.reshape(ROWS, 4, B, B), "row", split_axis=0, concat_axis=0, tiled=True
     ).reshape(32, B, B)
 
-    p, f = {(0, 0, 0): band[0]}, {}
+    p, f = {}, {(0, 0): inner}
     p[1, 0, 0] = send_row(band[0], -1, 0)
     p[3, 0, 0] = send_row(band[0], 1, 0)
-    p[0, 1, 0] = send_row(band[0], 0, 1)
     f[1, 0] = send_col(inner, -1, 0, 0)
     f[3, 0] = send_col(inner, 1, 0, 0)
-
-    keys = [(1, 0, 0), (3, 0, 0), (0, 1, 0)]
-    second, f[0, 0], f[1, 0], f[3, 0], *held = after(
-        [band[1], inner, f[1, 0], f[3, 0]] + [p[key] for key in keys], []
-    )
-    p.update(zip(keys, held))
+    f[0, 1] = send_col(inner, 0, 1, 0)
+
+    p[0, 0, 0], second, p[1, 0, 0], p[3, 0, 0] = after(
+        [*band, p[1, 0, 0], p[3, 0, 0]], []
+    )
     p[1, 0, 1] = send_row(second, -1, 0)
     p[3, 0, 1] = send_row(second, 1, 0)
-    f[0, 1] = send_col(f[0, 0], 0, 1, 0)
-    f[2, 0] = send_col(f[1, 0], -1, 0, 0)
-
-    p[0, 0, 1], p[1, 0, 0], p[3, 0, 1], f[0, 1], f[2, 0] = after(
-        [second, p[1, 0, 0], p[3, 0, 1], f[0, 1], f[2, 0]], [p[1, 0, 1]]
-    )
+    p[0, 1, 0] = send_row(p[0, 0, 0], 0, 1)
+    f[1, 1] = send_col(f[0, 1], -1, 0, 0)
+    f[3, 1] = send_col(f[0, 1], 1, 0, 0)
+
+    keys = [(1, 0), (3, 0), (1, 1), (3, 1)]
+    p[0, 0, 1], p[1, 0, 0], p[3, 0, 1], p[0, 1, 0], *held = after(
+        [second, p[1, 0, 0], p[3, 0, 1], p[0, 1, 0]] + [f[key] for key in keys],
+        [p[1, 0, 1]],
+    )
+    f.update(zip(keys, held))
     p[2, 0, 0] = send_row(p[1, 0, 0], -1, 0)
     p[2, 0, 1] = send_row(p[3, 0, 1], 1, 0)
     p[0, 1, 1] = send_row(p[0, 0, 1], 0, 1)
-    f[1, 1] = send_col(f[0, 1], -1, 0, 0)
-    f[3, 1] = send_col(f[0, 1], 1, 0, 0)
-
-    p[0, 1, 0], p[2, 0, 0], f[3, 1], f[1, 1] = after(
-        [p[0, 1, 0], p[2, 0, 0], f[3, 1], f[1, 1]], [p[2, 0, 1], p[0, 1, 1]]
-    )
+    f[2, 0] = send_col(f[1, 0], -1, 0, 0)
+    f[2, 1] = send_col(f[3, 1], 1, 0, 0)
+
+    def squares(keys):
+        ids = [(c // 4 + dx) % 4 * 4 + ((c % 4) ^ (2 * dz)) for dx, dz in keys]
+        ids = jnp.stack(ids).astype(jnp.int32)
+        return square(ids, leader, mask, left, [f[key] for key in keys], [])
+
+    keys = [(0, 1, 0), (0, 1, 1), (2, 0, 0), (2, 0, 1)]
+    early, f[2, 0], f[2, 1], *held = after(
+        [squares(EARLY), f[2, 0], f[2, 1]] + [p[key] for key in keys], []
+    )
+    p.update(zip(keys, held))
     p[1, 1, 0] = send_row(p[0, 1, 0], -1, 0)
     p[3, 1, 0] = send_row(p[0, 1, 0], 1, 0)
     p[2, 1, 0] = send_row(p[2, 0, 0], 0, 1)
-    f[2, 1] = send_col(f[3, 1], 1, 0, 0)
-
-    def squares(keys, others):
-        ids = [(c // 4 + dx) % 4 * 4 + ((c % 4) ^ (2 * dz)) for dx, dz in keys]
-        ids = jnp.stack(ids).astype(jnp.int32)
-        return square(ids, leader, mask, left, [f[key] for key in keys], others)
-
-    early, p[0, 1, 1], p[2, 0, 1], f[2, 1] = after(
-        [squares(EARLY, []), p[0, 1, 1], p[2, 0, 1], f[2, 1]],
+    filtered = [early, send_col(early, 0, 0, 1)]
+
+    late, p[0, 1, 1], p[2, 0, 1] = after(
+        [squares(LATE), p[0, 1, 1], p[2, 0, 1]],
         [p[1, 1, 0], p[3, 1, 0], p[2, 1, 0]],
     )
     p[1, 1, 1] = send_row(p[0, 1, 1], -1, 0)
     p[3, 1, 1] = send_row(p[0, 1, 1], 1, 0)
     p[2, 1, 1] = send_row(p[2, 0, 1], 0, 1)
-    filtered = [early, send_col(early, 0, 0, 1)]
-    late = squares(LATE, [])
     filtered += [late, send_col(late, 0, 0, 1)]
 
     def products(keys, before):

time: 333 us -> 330 us (level)
  waiting for transfers between devices: 203 us -> 198 us
    ppermute x9, waiting for transfers between devices: 30.9 us -> 14.8 us  [send_col(): return lax.ppermute(value, 'col', pairs)]
    ppermute x14, waiting for transfers between devices: 56.5 us -> 62.7 us  [send_row(): return lax.ppermute(value, 'row', moved(by_y, flip_z))]
    all_to_all x1, waiting for transfers between devices: 5.42 us -> 10.5 us  [local(): lax.all_to_all(inner.reshape(ROWS, 4, B, B), 'row', split_axis=0, concat_...]
  transfers between devices with their start and end apart: 27 -> 27, of which waited for: 21 -> 22; matrix products, arithmetic and copies ran while one was open for 4% -> 4% of each run, Pallas kernels for 12% -> 12%
where the time goes in v4:
time: 330 us; the launch traced here: 329 us
  waiting for transfers between devices  198 us (60%)
  starting transfers between devices  51.4 us (16%)
  Pallas kernels  50.3 us (15%)
  between operations  13.7 us (4%)
  local copies, waits for them, and re-layouts  8.59 us (3%)
  other arithmetic  6.21 us (2%)
    all_to_all x1, waiting for transfers between devices, local(): lax.all_to_all(outgoing.reshape(ROWS * COLS, 2, B, B), AXES, split_axis=0...  104 us
    ppermute x14, waiting for transfers between devices, send_row(): return lax.ppermute(value, 'row', moved(by_y, flip_z))  62.7 us
    pallas_call x2, Pallas kernels, cubed(): pl.pallas_call(functools.partial(cubed_kernel, is_last), grid_spec=pltpu....  21.3 us
    ppermute x14, starting transfers between devices, send_row(): return lax.ppermute(value, 'row', moved(by_y, flip_z))  17.9 us
    ppermute x9, waiting for transfers between devices, send_col(): return lax.ppermute(value, 'col', pairs)  14.8 us
    pallas_call x2, Pallas kernels, square(): pl.pallas_call(square_kernel, grid_spec=pltpu.PrefetchScalarGridSpec(num_...  14 us
    ppermute x9, starting transfers between devices, send_col(): return lax.ppermute(value, 'col', pairs)  12.3 us
    all_to_all x1, waiting for transfers between devices, local(): lax.all_to_all(inner.reshape(ROWS, 4, B, B), 'row', split_axis=0, concat_...  10.5 us
  transfers between devices with their start and end apart: 27, of which 22 were waited for; matrix products, arithmetic and copies ran while one was open for 4% of the time, Pallas kernels for 12%

profile of v4, /device:TPU:6, one launch (start us, length us, event | category | flops | bytes accessed | tf_op | source)
XLA Modules:
  0.0 328.9 jit_solution(13606233578055603909)
XLA Ops:
  9.6 10.5 %all-to-all-start = ((s32[128,8,128]{2,1,0:T(8,128)}), s32[128,8,128]{2,1,0:T(8,128)S(1)}, u32[]{:S(2)}, u32[]{:S(2)}) async-start(s32[128,8,128]{2,1,0:T(8,128)} %broadcast_in_dim.87), calls=%async_computation | async-start | bytes 1048576 | tf_op jit(solution)/shard_map/all_to_all | solution.py:322
  20.1 6.5 %spread.1 = bf16[8,16,2,128,128]{4,3,2,1,0:T(8,128)(2,1)} custom-call(bf16[16,16,128,128]{3,2,1,0:T(8,128)(2,1)} %owned.1), custom_call_target="tpu_custom_call" | custom-call | bytes 16777216 | tf_op jit(solution)/shard_map/spread/pallas_call | solution.py:60
  26.7 6.0 %all-to-all-done = s32[128,8,128]{2,1,0:T(8,128)S(1)} async-done(((s32[128,8,128]{2,1,0:T(8,128)}), s32[128,8,128]{2,1,0:T(8,128)S(1)}, u32[]{:S(2)}, u32[]{:S(2)}) %all-to-all-start) | async-done | bytes 524320 | tf_op jit(solution)/shard_map/all_to_all | solution.py:322
  32.7 6.5 %all-to-all-start.1 = ((bf16[128,2,128,128]{3,2,1,0:T(8,128)(2,1)}), bf16[128,2,128,128]{3,2,1,0:T(8,128)(2,1)}, u32[]{:S(2)}, u32[]{:S(2)}) async-start(bf16[128,2,128,128]{3,2,1,0:T(8,128)(2,1)} %bitcast.59), calls=%async_computation.1 | async-start | bytes 16777216 | tf_op jit(solution)/shard_map/all_to_all | solution.py:318
  43.0 103.6 %all-to-all-done.1 = bf16[128,2,128,128]{3,2,1,0:T(8,128)(2,1)} async-done(((bf16[128,2,128,128]{3,2,1,0:T(8,128)(2,1)}), bf16[128,2,128,128]{3,2,1,0:T(8,128)(2,1)}, u32[]{:S(2)}, u32[]{:S(2)}) %all-to-all-start.1) | async-done | bytes 8388640 | tf_op jit(solution)/shard_map/all_to_all | solution.py:318
  149.5 4.3 %all-to-all-start.2 = ((bf16[8,4,128,128]{3,2,1,0:T(8,128)(2,1)}), bf16[8,4,128,128]{3,2,1,0:T(8,128)(2,1)}, u32[]{:S(2)}, u32[]{:S(2)}) async-start(bf16[8,4,128,128]{3,2,1,0:T(8,128)(2,1)} %bitcast.60), calls=%async_computation.2 | async-start | bytes 2097152 | tf_op jit(solution)/shard_map/all_to_all | solution.py:383
  153.8 3.6 %pack.5 = (bf16[32,128,128]{2,1,0:T(8,128)(2,1)}, bf16[32,128,128]{2,1,0:T(8,128)(2,1)}) custom-call(s32[64]{0:T(128)} %copy-done.1, bf16[256,128,128]{2,1,0:T(8,128)(2,1)} %bitcast.16.arrived, bf16[32,128,128]{2,1,0:T(8,128)(2,1)} %pack.4.refs_0_), custom_call_target="tpu_custom_call" | custom-call | bytes 4194304 | tf_op jit(solution)/shard_map/pack/pallas_call | solution.py:115
  157.4 3.2 collective-permute-start.1
  160.5 10.5 %all-to-all-done.2 = bf16[8,4,128,128]{3,2,1,0:T(8,128)(2,1)} async-done(((bf16[8,4,128,128]{3,2,1,0:T(8,128)(2,1)}), bf16[8,4,128,128]{3,2,1,0:T(8,128)(2,1)}, u32[]{:S(2)}, u32[]{:S(2)}) %all-to-all-start.2) | async-done | bytes 1048608 | tf_op jit(solution)/shard_map/all_to_all | solution.py:383
  171.4 4.4 %collective-permute-start.5 = (bf16[32,128,128]{2,1,0:T(8,128)(2,1)}, bf16[32,128,128]{2,1,0:T(8,128)(2,1)}, u32[]{:S(2)}, u32[]{:S(2)}) collective-permute-start(bf16[32,128,128]{2,1,0:T(8,128)(2,1)} %bitcast.19.refs_0_), channel_id=1, source_target_pairs={{0,12},{1,13},{2,14},{3,15},{4,0},{5,1},{6,2},{7,3},{8,4},{9,5},{1... | collective-permute-start | bytes 3145736 | tf_op jit(solution)/shard_map/ppermute | solution.py:33
  175.8 14.2 %collective-permute-done.1.refs_2_ = bf16[32,128,128]{2,1,0:T(8,128)(2,1)} collective-permute-done((bf16[32,128,128]{2,1,0:T(8,128)(2,1)}, bf16[32,128,128]{2,1,0:T(8,128)(2,1)}, u32[]{:S(2)}, u32[]{:S(2)}) %collective-permute-start.1) | collective-permute-done | bytes 1048608 | tf_op jit(solution)/shard_map/ppermute | solution.py:37
  196.7 4.2 %collective-permute-start.7 = (bf16[32,128,128]{2,1,0:T(8,128)(2,1)}, bf16[32,128,128]{2,1,0:T(8,128)(2,1)}, u32[]{:S(2)}, u32[]{:S(2)}) collective-permute-start(bf16[32,128,128]{2,1,0:T(8,128)(2,1)} %collective-permute-done.refs_1_), channel_id=1, source_target_pairs={{0,12},{1,13},{2,14},{3,15},{4,0},{5,1},{6,2},{7,3},{8,4},{9,5},{1... | collective-permute-start | bytes 3145736 | tf_op jit(solution)/shard_map/ppermute | solution.py:33
  203.0 12.9 %collective-permute-done.9.refs_8_.refs_7_ = bf16[32,128,128]{2,1,0:T(8,128)(2,1)} collective-permute-done((bf16[32,128,128]{2,1,0:T(8,128)(2,1)}, bf16[32,128,128]{2,1,0:T(8,128)(2,1)}, u32[]{:S(2)}, u32[]{:S(2)}) %collective-permute-start.9) | collective-permute-done | bytes 1048608 | tf_op jit(solution)/shard_map/ppermute | solution.py:37
  219.9 5.9 %collective-permute-done.7.refs_6_ = bf16[32,128,128]{2,1,0:T(8,128)(2,1)} collective-permute-done((bf16[32,128,128]{2,1,0:T(8,128)(2,1)}, bf16[32,128,128]{2,1,0:T(8,128)(2,1)}, u32[]{:S(2)}, u32[]{:S(2)}) %collective-permute-start.7) | collective-permute-done | bytes 1048608 | tf_op jit(solution)/shard_map/ppermute | solution.py:33
  228.4 3.1 collective-permute-start.11
  238.9 8.4 %square.2.refs_0_ = bf16[6,32,128,128]{3,2,1,0:T(8,128)(2,1)} custom-call(s32[6]{0:T(128)} %stack.157.groups, s32[512]{0:T(512)} %copy-done, s32[512]{0:T(512)} %compare_select_fusion.mask, bf16[16,2,128,128]{3,2,1,0:T(8,128)(2,1)} %bitcast.61, bf16[32,128,128]{2,1,0:T(8,128)(2,1)} %bitcast.19.refs_0_, bf16[32,128,128]{2,1,0:T(8,128)(2,1)} %collective-permute-done.refs_1_, ...), custom_call_target="tpu_custom_call" | custom-call | flops 805306368 | bytes 12582912 | tf_op jit(solution)/shard_map/square/pallas_call | solution.py:172
  247.3 4.5 %collective-permute-done.10.refs_1_ = bf16[32,128,128]{2,1,0:T(8,128)(2,1)} collective-permute-done((bf16[32,128,128]{2,1,0:T(8,128)(2,1)}, bf16[32,128,128]{2,1,0:T(8,128)(2,1)}, u32[]{:S(2)}, u32[]{:S(2)}) %collective-permute-start.10) | collective-permute-done | bytes 1048608 | tf_op jit(solution)/shard_map/ppermute | solution.py:33
  252.2 3.4 %collective-permute-done.12.refs_4_ = bf16[32,128,128]{2,1,0:T(8,128)(2,1)} collective-permute-done((bf16[32,128,128]{2,1,0:T(8,128)(2,1)}, bf16[32,128,128]{2,1,0:T(8,128)(2,1)}, u32[]{:S(2)}, u32[]{:S(2)}) %collective-permute-start.12) | collective-permute-done | bytes 1048608 | tf_op jit(solution)/shard_map/ppermute | solution.py:37
  260.5 5.6 %square.3.refs_0_ = bf16[2,32,128,128]{3,2,1,0:T(8,128)(2,1)} custom-call(s32[2]{0:T(128)} %pad_add_fusion.2.groups, s32[512]{0:T(512)} %copy-done, s32[512]{0:T(512)} %compare_select_fusion.mask, bf16[16,2,128,128]{3,2,1,0:T(8,128)(2,1)} %bitcast.62, bf16[32,128,128]{2,1,0:T(8,128)(2,1)} %get-tuple-element.43.refs_0_, ...), custom_call_target="tpu_custom_call" | custom-call | flops 268435456 | bytes 4194304 | tf_op jit(solution)/shard_map/square/pallas_call | solution.py:172
  266.1 15.6 %collective-permute-done.16.refs_3_.refs_14_ = bf16[32,128,128]{2,1,0:T(8,128)(2,1)} collective-permute-done((bf16[32,128,128]{2,1,0:T(8,128)(2,1)}, bf16[32,128,128]{2,1,0:T(8,128)(2,1)}, u32[]{:S(2)}, u32[]{:S(2)}) %collective-permute-start.16) | collective-permute-done | bytes 1048608 | tf_op jit(solution)/shard_map/ppermute | solution.py:37
  292.6 14.0 %cubed.2.refs_7_ = f32[64,128,128]{2,1,0:T(8,128)} custom-call(s32[14]{0:T(128)} %stack.174.groups, s32[13]{0:T(128)} %stack.188.slots, s32[512]{0:T(512)} %reshape.170.inner_at, s32[512]{0:T(512)} %reshape.171.target, bf16[6,32,128,128]{3,2,1,0:T(8,128)(2,1)} %get-tuple-element.42.refs_0_.refs_17_, ...), custom_call_target="tpu_custom_call" | custom-call | flops 6979321856 | bytes 32505856 | tf_op jit(solution)/shard_map/cubed/pallas_call | solution.py:278
  306.6 4.4 %collective-permute-done.20.refs_4_ = bf16[32,128,128]{2,1,0:T(8,128)(2,1)} collective-permute-done((bf16[32,128,128]{2,1,0:T(8,128)(2,1)}, bf16[32,128,128]{2,1,0:T(8,128)(2,1)}, u32[]{:S(2)}, u32[]{:S(2)}) %collective-permute-start.20) | collective-permute-done | bytes 1048608 | tf_op jit(solution)/shard_map/ppermute | solution.py:37
  311.0 3.4 %collective-permute-done.21.refs_5_ = bf16[32,128,128]{2,1,0:T(8,128)(2,1)} collective-permute-done((bf16[32,128,128]{2,1,0:T(8,128)(2,1)}, bf16[32,128,128]{2,1,0:T(8,128)(2,1)}, u32[]{:S(2)}, u32[]{:S(2)}) %collective-permute-start.21) | collective-permute-done | bytes 1048608 | tf_op jit(solution)/shard_map/ppermute | solution.py:37
  314.7 7.3 %cubed.3 = bf16[256,4096]{1,0:T(8,128)(2,1)} custom-call(s32[4]{0:T(128)} %pad_add_fusion.groups, s32[3]{0:T(128)} %pad_add_fusion.1.slots, s32[512]{0:T(512)} %reshape.170.inner_at, s32[512]{0:T(512)} %reshape.171.target, bf16[6,32,128,128]{3,2,1,0:T(8,128)(2,1)} %get-tuple-element.42.refs_0_.refs_17_, ...), custom_call_target="tpu_custom_call" | custom-call | flops 1610612736 | bytes 11534336 | tf_op jit(solution)/shard_map/cubed/pallas_call | solution.py:278
  (104 shorter events, 49.3 us)
Async XLA Ops:
  9.6 23.0 %all-to-all-start = ((s32[128,8,128]{2,1,0:T(8,128)}), s32[128,8,128]{2,1,0:T(8,128)S(1)}, u32[]{:S(2)}, u32[]{:S(2)}) async-start(s32[128,8,128]{2,1,0:T(8,128)} %broadcast_in_dim.87), calls=%async_computation | async-start | bytes 1048576 | tf_op jit(solution)/shard_map/all_to_all | solution.py:322
  32.7 113.9 %all-to-all-start.1 = ((bf16[128,2,128,128]{3,2,1,0:T(8,128)(2,1)}), bf16[128,2,128,128]{3,2,1,0:T(8,128)(2,1)}, u32[]{:S(2)}, u32[]{:S(2)}) async-start(bf16[128,2,128,128]{3,2,1,0:T(8,128)(2,1)} %bitcast.59), calls=%async_computation.1 | async-start | bytes 16777216 | tf_op jit(solution)/shard_map/all_to_all | solution.py:318
  153.7 85.1 %all-gather.2.cloned.1.call-start = ((), (), s32[]{:S(2)}) async-start(), calls=%async_computation.3 | async-start | bytes 1114112 | tf_op jit(solution)/shard_map/all_gather | solution.py:382
  157.4 32.6 %collective-permute-start.1 = (bf16[32,128,128]{2,1,0:T(8,128)(2,1)}, bf16[32,128,128]{2,1,0:T(8,128)(2,1)}, u32[]{:S(2)}, u32[]{:S(2)}) collective-permute-start(bf16[32,128,128]{2,1,0:T(8,128)(2,1)} %get-tuple-element.29.refs_0_), channel_id=1, source_target_pairs={{0,96},{16,112},{32,0},{48,16},{64,32},{80,48},{96,64},{112,80},{1... | collective-permute-start | bytes 3145736 | tf_op jit(solution)/shard_map/ppermute | solution.py:37
  160.5 30.9 %collective-permute-start.2 = (bf16[32,128,128]{2,1,0:T(8,128)(2,1)}, bf16[32,128,128]{2,1,0:T(8,128)(2,1)}, u32[]{:S(2)}, u32[]{:S(2)}) collective-permute-start(bf16[32,128,128]{2,1,0:T(8,128)(2,1)} %get-tuple-element.29.refs_0_), channel_id=1, source_target_pairs={{0,32},{16,48},{32,64},{48,80},{64,96},{80,112},{96,0},{112,16},{1... | collective-permute-start | bytes 3145736 | tf_op jit(solution)/shard_map/ppermute | solution.py:37
  171.0 23.4 %collective-permute-start = (bf16[32,128,128]{2,1,0:T(8,128)(2,1)}, bf16[32,128,128]{2,1,0:T(8,128)(2,1)}, u32[]{:S(2)}, u32[]{:S(2)}) collective-permute-start(bf16[32,128,128]{2,1,0:T(8,128)(2,1)} %bitcast.19.refs_0_), channel_id=1, source_target_pairs={{0,2},{1,3},{2,0},{3,1},{4,6},{5,7},{6,4},{7,5},{8,10},{9,11},{10,... | collective-permute-start | bytes 3145736 | tf_op jit(solution)/shard_map/ppermute | solution.py:33
  171.4 25.2 %collective-permute-start.5 = (bf16[32,128,128]{2,1,0:T(8,128)(2,1)}, bf16[32,128,128]{2,1,0:T(8,128)(2,1)}, u32[]{:S(2)}, u32[]{:S(2)}) collective-permute-start(bf16[32,128,128]{2,1,0:T(8,128)(2,1)} %bitcast.19.refs_0_), channel_id=1, source_target_pairs={{0,12},{1,13},{2,14},{3,15},{4,0},{5,1},{6,2},{7,3},{8,4},{9,5},{1... | collective-permute-start | bytes 3145736 | tf_op jit(solution)/shard_map/ppermute | solution.py:33
  175.8 25.1 %collective-permute-start.6 = (bf16[32,128,128]{2,1,0:T(8,128)(2,1)}, bf16[32,128,128]{2,1,0:T(8,128)(2,1)}, u32[]{:S(2)}, u32[]{:S(2)}) collective-permute-start(bf16[32,128,128]{2,1,0:T(8,128)(2,1)} %bitcast.19.refs_0_), channel_id=1, source_target_pairs={{0,4},{1,5},{2,6},{3,7},{4,8},{5,9},{6,10},{7,11},{8,12},{9,13},{1... | collective-permute-start | bytes 3145736 | tf_op jit(solution)/shard_map/ppermute | solution.py:33
  191.4 24.5 %collective-permute-start.9 = (bf16[32,128,128]{2,1,0:T(8,128)(2,1)}, bf16[32,128,128]{2,1,0:T(8,128)(2,1)}, u32[]{:S(2)}, u32[]{:S(2)}) collective-permute-start(bf16[32,128,128]{2,1,0:T(8,128)(2,1)} %get-tuple-element.31.refs_0_), channel_id=1, source_target_pairs={{0,96},{16,112},{32,0},{48,16},{64,32},{80,48},{96,64},{112,80},{1... | collective-permute-start | bytes 3145736 | tf_op jit(solution)/shard_map/ppermute | solution.py:37
  192.8 25.2 %collective-permute-start.3 = (bf16[32,128,128]{2,1,0:T(8,128)(2,1)}, bf16[32,128,128]{2,1,0:T(8,128)(2,1)}, u32[]{:S(2)}, u32[]{:S(2)}) collective-permute-start(bf16[32,128,128]{2,1,0:T(8,128)(2,1)} %get-tuple-element.31.refs_0_), channel_id=1, source_target_pairs={{0,32},{16,48},{32,64},{48,80},{64,96},{80,112},{96,0},{112,16},{1... | collective-permute-start | bytes 3145736 | tf_op jit(solution)/shard_map/ppermute | solution.py:37
  194.3 25.5 %collective-permute-start.4 = (bf16[32,128,128]{2,1,0:T(8,128)(2,1)}, bf16[32,128,128]{2,1,0:T(8,128)(2,1)}, u32[]{:S(2)}, u32[]{:S(2)}) collective-permute-start(bf16[32,128,128]{2,1,0:T(8,128)(2,1)} %get-tuple-element.33.refs_6_), channel_id=1, source_target_pairs={{0,16},{16,0},{32,48},{48,32},{64,80},{80,64},{96,112},{112,96},{1... | collective-permute-start | bytes 3145736 | tf_op jit(solution)/shard_map/ppermute | solution.py:37
  196.7 29.2 %collective-permute-start.7 = (bf16[32,128,128]{2,1,0:T(8,128)(2,1)}, bf16[32,128,128]{2,1,0:T(8,128)(2,1)}, u32[]{:S(2)}, u32[]{:S(2)}) collective-permute-start(bf16[32,128,128]{2,1,0:T(8,128)(2,1)} %collective-permute-done.refs_1_), channel_id=1, source_target_pairs={{0,12},{1,13},{2,14},{3,15},{4,0},{5,1},{6,2},{7,3},{8,4},{9,5},{1... | collective-permute-start | bytes 3145736 | tf_op jit(solution)/shard_map/ppermute | solution.py:33
  200.9 27.4 %collective-permute-start.8 = (bf16[32,128,128]{2,1,0:T(8,128)(2,1)}, bf16[32,128,128]{2,1,0:T(8,128)(2,1)}, u32[]{:S(2)}, u32[]{:S(2)}) collective-permute-start(bf16[32,128,128]{2,1,0:T(8,128)(2,1)} %collective-permute-done.refs_1_), channel_id=1, source_target_pairs={{0,4},{1,5},{2,6},{3,7},{4,8},{5,9},{6,10},{7,11},{8,12},{9,13},{1... | collective-permute-start | bytes 3145736 | tf_op jit(solution)/shard_map/ppermute | solution.py:33
  228.3 23.5 %collective-permute-start.10 = (bf16[32,128,128]{2,1,0:T(8,128)(2,1)}, bf16[32,128,128]{2,1,0:T(8,128)(2,1)}, u32[]{:S(2)}, u32[]{:S(2)}) collective-permute-start(bf16[32,128,128]{2,1,0:T(8,128)(2,1)} %get-tuple-element.34.refs_2_), channel_id=1, source_target_pairs={{0,12},{1,13},{2,14},{3,15},{4,0},{5,1},{6,2},{7,3},{8,4},{9,5},{1... | collective-permute-start | bytes 3145736 | tf_op jit(solution)/shard_map/ppermute | solution.py:33
  228.4 23.9 %collective-permute-start.11 = (bf16[32,128,128]{2,1,0:T(8,128)(2,1)}, bf16[32,128,128]{2,1,0:T(8,128)(2,1)}, u32[]{:S(2)}, u32[]{:S(2)}) collective-permute-start(bf16[32,128,128]{2,1,0:T(8,128)(2,1)} %get-tuple-element.37.refs_5_), channel_id=1, source_target_pairs={{0,4},{1,5},{2,6},{3,7},{4,8},{5,9},{6,10},{7,11},{8,12},{9,13},{1... | collective-permute-start | bytes 3145736 | tf_op jit(solution)/shard_map/ppermute | solution.py:33
  231.5 24.1 %collective-permute-start.12 = (bf16[32,128,128]{2,1,0:T(8,128)(2,1)}, bf16[32,128,128]{2,1,0:T(8,128)(2,1)}, u32[]{:S(2)}, u32[]{:S(2)}) collective-permute-start(bf16[32,128,128]{2,1,0:T(8,128)(2,1)} %get-tuple-element.39.refs_10_), channel_id=1, source_target_pairs={{0,16},{16,0},{32,48},{48,32},{64,80},{80,64},{96,112},{112,96},{1... | collective-permute-start | bytes 3145736 | tf_op jit(solution)/shard_map/ppermute | solution.py:37
  231.5 24.1 %collective-permute-start.13 = (bf16[32,128,128]{2,1,0:T(8,128)(2,1)}, bf16[32,128,128]{2,1,0:T(8,128)(2,1)}, u32[]{:S(2)}, u32[]{:S(2)}) collective-permute-start(bf16[32,128,128]{2,1,0:T(8,128)(2,1)} %get-tuple-element.40.refs_4_), channel_id=1, source_target_pairs={{0,96},{16,112},{32,0},{48,16},{64,32},{80,48},{96,64},{112,80},{1... | collective-permute-start | bytes 3145736 | tf_op jit(solution)/shard_map/ppermute | solution.py:37
  255.8 36.8 %collective-permute-start.15 = (bf16[6,32,128,128]{3,2,1,0:T(8,128)(2,1)}, bf16[6,32,128,128]{3,2,1,0:T(8,128)(2,1)}, u32[]{:S(2)}, u32[]{:S(2)}) collective-permute-start(bf16[6,32,128,128]{3,2,1,0:T(8,128)(2,1)} %get-tuple-element.42.refs_0_.refs_17_), channel_id=1, source_target_pairs={{0,1},{1,0},{2,3},{3,2},{4,5},{5,4},{6,7},{7,6},{8,9},{9,8},{10,11... | collective-permute-start | bytes 18874376 | tf_op jit(solution)/shard_map/ppermute | solution.py:33
  255.8 25.9 %collective-permute-start.16 = (bf16[32,128,128]{2,1,0:T(8,128)(2,1)}, bf16[32,128,128]{2,1,0:T(8,128)(2,1)}, u32[]{:S(2)}, u32[]{:S(2)}) collective-permute-start(bf16[32,128,128]{2,1,0:T(8,128)(2,1)} %get-tuple-element.47.refs_9_), channel_id=1, source_target_pairs={{0,96},{16,112},{32,0},{48,16},{64,32},{80,48},{96,64},{112,80},{1... | collective-permute-start | bytes 3145736 | tf_op jit(solution)/shard_map/ppermute | solution.py:37
  257.5 26.8 %collective-permute-start.17 = (bf16[32,128,128]{2,1,0:T(8,128)(2,1)}, bf16[32,128,128]{2,1,0:T(8,128)(2,1)}, u32[]{:S(2)}, u32[]{:S(2)}) collective-permute-start(bf16[32,128,128]{2,1,0:T(8,128)(2,1)} %get-tuple-element.47.refs_9_), channel_id=1, source_target_pairs={{0,32},{16,48},{32,64},{48,80},{64,96},{80,112},{96,0},{112,16},{1... | collective-permute-start | bytes 3145736 | tf_op jit(solution)/shard_map/ppermute | solution.py:37
  257.8 26.8 %collective-permute-start.18 = (bf16[32,128,128]{2,1,0:T(8,128)(2,1)}, bf16[32,128,128]{2,1,0:T(8,128)(2,1)}, u32[]{:S(2)}, u32[]{:S(2)}) collective-permute-start(bf16[32,128,128]{2,1,0:T(8,128)(2,1)} %get-tuple-element.48.refs_11_), channel_id=1, source_target_pairs={{0,16},{16,0},{32,48},{48,32},{64,80},{80,64},{96,112},{112,96},{1... | collective-permute-start | bytes 3145736 | tf_op jit(solution)/shard_map/ppermute | solution.py:37
  284.6 26.4 %collective-permute-start.20 = (bf16[32,128,128]{2,1,0:T(8,128)(2,1)}, bf16[32,128,128]{2,1,0:T(8,128)(2,1)}, u32[]{:S(2)}, u32[]{:S(2)}) collective-permute-start(bf16[32,128,128]{2,1,0:T(8,128)(2,1)} %get-tuple-element.50.refs_13_), channel_id=1, source_target_pairs={{0,96},{16,112},{32,0},{48,16},{64,32},{80,48},{96,64},{112,80},{1... | collective-permute-start | bytes 3145736 | tf_op jit(solution)/shard_map/ppermute | solution.py:37
  287.6 26.8 %collective-permute-start.21 = (bf16[32,128,128]{2,1,0:T(8,128)(2,1)}, bf16[32,128,128]{2,1,0:T(8,128)(2,1)}, u32[]{:S(2)}, u32[]{:S(2)}) collective-permute-start(bf16[32,128,128]{2,1,0:T(8,128)(2,1)} %get-tuple-element.50.refs_13_), channel_id=1, source_target_pairs={{0,32},{16,48},{32,64},{48,80},{64,96},{80,112},{96,0},{112,16},{1... | collective-permute-start | bytes 3145736 | tf_op jit(solution)/shard_map/ppermute | solution.py:37
  287.6 27.1 %collective-permute-start.22 = (bf16[32,128,128]{2,1,0:T(8,128)(2,1)}, bf16[32,128,128]{2,1,0:T(8,128)(2,1)}, u32[]{:S(2)}, u32[]{:S(2)}) collective-permute-start(bf16[32,128,128]{2,1,0:T(8,128)(2,1)} %get-tuple-element.51.refs_12_), channel_id=1, source_target_pairs={{0,16},{16,0},{32,48},{48,32},{64,80},{80,64},{96,112},{112,96},{1... | collective-permute-start | bytes 3145736 | tf_op jit(solution)/shard_map/ppermute | solution.py:37
  (5 other events, 158.8 us)
Sparse Core Ops, SparseCore 0:
  203.1 33.9 all-gather.1

commit v5 on v4

--- a/solution.py
+++ b/solution.py
@@ -400,41 +400,37 @@
     f[1, 1] = send_col(f[0, 1], -1, 0, 0)
     f[3, 1] = send_col(f[0, 1], 1, 0, 0)
 
-    keys = [(1, 0), (3, 0), (1, 1), (3, 1)]
-    p[0, 0, 1], p[1, 0, 0], p[3, 0, 1], p[0, 1, 0], *held = after(
-        [second, p[1, 0, 0], p[3, 0, 1], p[0, 1, 0]] + [f[key] for key in keys],
-        [p[1, 0, 1]],
-    )
-    f.update(zip(keys, held))
+    p[0, 0, 1], p[1, 0, 0], p[3, 0, 1], p[0, 1, 0], f[1, 0], f[3, 0] = after(
+        [second, p[1, 0, 0], p[3, 0, 1], p[0, 1, 0], f[1, 0], f[3, 0]],
+        [p[1, 0, 1], f[0, 1]],
+    )
     p[2, 0, 0] = send_row(p[1, 0, 0], -1, 0)
     p[2, 0, 1] = send_row(p[3, 0, 1], 1, 0)
     p[0, 1, 1] = send_row(p[0, 0, 1], 0, 1)
+
+    f[1, 0], f[3, 1] = after([f[1, 0], f[3, 1]], [f[1, 1], p[0, 0, 1]])
     f[2, 0] = send_col(f[1, 0], -1, 0, 0)
     f[2, 1] = send_col(f[3, 1], 1, 0, 0)
+
+    keys = [(0, 1, 0), (0, 1, 1), (2, 0, 0), (2, 0, 1)]
+    p.update(zip(keys, after([p[key] for key in keys], [])))
+    p[1, 1, 0] = send_row(p[0, 1, 0], -1, 0)
+    p[3, 1, 0] = send_row(p[0, 1, 0], 1, 0)
+    p[2, 1, 0] = send_row(p[2, 0, 0], 0, 1)
 
     def squares(keys):
         ids = [(c // 4 + dx) % 4 * 4 + ((c % 4) ^ (2 * dz)) for dx, dz in keys]
         ids = jnp.stack(ids).astype(jnp.int32)
         return square(ids, leader, mask, left, [f[key] for key in keys], [])
 
-    keys = [(0, 1, 0), (0, 1, 1), (2, 0, 0), (2, 0, 1)]
-    early, f[2, 0], f[2, 1], *held = after(
-        [squares(EARLY), f[2, 0], f[2, 1]] + [p[key] for key in keys], []
-    )
-    p.update(zip(keys, held))
-    p[1, 1, 0] = send_row(p[0, 1, 0], -1, 0)
-    p[3, 1, 0] = send_row(p[0, 1, 0], 1, 0)
-    p[2, 1, 0] = send_row(p[2, 0, 0], 0, 1)
-    filtered = [early, send_col(early, 0, 0, 1)]
-
-    late, p[0, 1, 1], p[2, 0, 1] = after(
-        [squares(LATE), p[0, 1, 1], p[2, 0, 1]],
+    early, late, p[0, 1, 1], p[2, 0, 1] = after(
+        [squares(EARLY), squares(LATE), p[0, 1, 1], p[2, 0, 1]],
         [p[1, 1, 0], p[3, 1, 0], p[2, 1, 0]],
     )
     p[1, 1, 1] = send_row(p[0, 1, 1], -1, 0)
     p[3, 1, 1] = send_row(p[0, 1, 1], 1, 0)
     p[2, 1, 1] = send_row(p[2, 0, 1], 0, 1)
-    filtered += [late, send_col(late, 0, 0, 1)]
+    filtered = [early, send_col(early, 0, 0, 1), late, send_col(late, 0, 0, 1)]
 
     def products(keys, before):
         groups, slots = [], []

time: 330 us -> 324 us (0.982)
  waiting for transfers between devices: 198 us -> 185 us
  starting transfers between devices: 51.4 us -> 57 us
    ppermute x14, waiting for transfers between devices: 62.7 us -> 52.4 us  [send_row(): return lax.ppermute(value, 'row', moved(by_y, flip_z))]
    ppermute x9, waiting for transfers between devices: 14.8 us -> 5.25 us  [send_col(): return lax.ppermute(value, 'col', pairs)]
    all_gather x1, waiting for transfers between devices: 0.01 us -> 7.18 us  [local(): lax.all_gather(window, 'col', axis=0, tiled=True).reshape(COLS, 2, B, B)]
    ppermute x14, starting transfers between devices: 17.9 us -> 21.2 us  [send_row(): return lax.ppermute(value, 'row', moved(by_y, flip_z))]
  transfers between devices with their start and end apart: 27 -> 27, of which waited for: 22 -> 17; matrix products, arithmetic and copies ran while one was open for 4% -> 4% of each run, Pallas kernels for 12% -> 12%
where the time goes in v5:
time: 324 us; the launch traced here: 322 us
  waiting for transfers between devices  185 us (57%)
  starting transfers between devices  57 us (18%)
  Pallas kernels  50.3 us (16%)
  between operations  13.7 us (4%)
  local copies, waits for them, and re-layouts  8.54 us (3%)
  other arithmetic  6.14 us (2%)
    all_to_all x1, waiting for transfers between devices, local(): lax.all_to_all(outgoing.reshape(ROWS * COLS, 2, B, B), AXES, split_axis=0...  104 us
    ppermute x14, waiting for transfers between devices, send_row(): return lax.ppermute(value, 'row', moved(by_y, flip_z))  52.4 us
    ppermute x14, starting transfers between devices, send_row(): return lax.ppermute(value, 'row', moved(by_y, flip_z))  21.2 us
    pallas_call x2, Pallas kernels, cubed(): pl.pallas_call(functools.partial(cubed_kernel, is_last), grid_spec=pltpu....  21.2 us
    ppermute x9, starting transfers between devices, send_col(): return lax.ppermute(value, 'col', pairs)  14.5 us
    pallas_call x2, Pallas kernels, square(): pl.pallas_call(square_kernel, grid_spec=pltpu.PrefetchScalarGridSpec(num_...  14 us
    all_to_all x1, waiting for transfers between devices, local(): lax.all_to_all(inner.reshape(ROWS, 4, B, B), 'row', split_axis=0, concat_...  10.5 us
    all_to_all x1, starting transfers between devices, local(): lax.all_to_all(jnp.broadcast_to(tags.reshape(1, 8, 128), (ROWS * COLS, 8,...  10.5 us
  transfers between devices with their start and end apart: 27, of which 17 were waited for; matrix products, arithmetic and copies ran while one was open for 4% of the time, Pallas kernels for 12%

profile of v5, /device:TPU:6, one launch (start us, length us, event | category | flops | bytes accessed | tf_op | source)
XLA Modules:
  0.0 321.6 jit_solution(17717000572206061427)
XLA Ops:
  9.6 10.5 %all-to-all-start = ((s32[128,8,128]{2,1,0:T(8,128)}), s32[128,8,128]{2,1,0:T(8,128)S(1)}, u32[]{:S(2)}, u32[]{:S(2)}) async-start(s32[128,8,128]{2,1,0:T(8,128)} %broadcast_in_dim.87), calls=%async_computation | async-start | bytes 1048576 | tf_op jit(solution)/shard_map/all_to_all | solution.py:322
  20.1 6.5 %spread.1 = bf16[8,16,2,128,128]{4,3,2,1,0:T(8,128)(2,1)} custom-call(bf16[16,16,128,128]{3,2,1,0:T(8,128)(2,1)} %owned.1), custom_call_target="tpu_custom_call" | custom-call | bytes 16777216 | tf_op jit(solution)/shard_map/spread/pallas_call | solution.py:60
  26.7 6.0 %all-to-all-done = s32[128,8,128]{2,1,0:T(8,128)S(1)} async-done(((s32[128,8,128]{2,1,0:T(8,128)}), s32[128,8,128]{2,1,0:T(8,128)S(1)}, u32[]{:S(2)}, u32[]{:S(2)}) %all-to-all-start) | async-done | bytes 524320 | tf_op jit(solution)/shard_map/all_to_all | solution.py:322
  32.7 6.5 %all-to-all-start.1 = ((bf16[128,2,128,128]{3,2,1,0:T(8,128)(2,1)}), bf16[128,2,128,128]{3,2,1,0:T(8,128)(2,1)}, u32[]{:S(2)}, u32[]{:S(2)}) async-start(bf16[128,2,128,128]{3,2,1,0:T(8,128)(2,1)} %bitcast.59), calls=%async_computation.1 | async-start | bytes 16777216 | tf_op jit(solution)/shard_map/all_to_all | solution.py:318
  43.0 103.6 %all-to-all-done.1 = bf16[128,2,128,128]{3,2,1,0:T(8,128)(2,1)} async-done(((bf16[128,2,128,128]{3,2,1,0:T(8,128)(2,1)}), bf16[128,2,128,128]{3,2,1,0:T(8,128)(2,1)}, u32[]{:S(2)}, u32[]{:S(2)}) %all-to-all-start.1) | async-done | bytes 8388640 | tf_op jit(solution)/shard_map/all_to_all | solution.py:318
  146.6 2.9 pack.4.refs_0_
  149.5 4.3 %all-to-all-start.2 = ((bf16[8,4,128,128]{3,2,1,0:T(8,128)(2,1)}), bf16[8,4,128,128]{3,2,1,0:T(8,128)(2,1)}, u32[]{:S(2)}, u32[]{:S(2)}) async-start(bf16[8,4,128,128]{3,2,1,0:T(8,128)(2,1)} %bitcast.60), calls=%async_computation.2 | async-start | bytes 2097152 | tf_op jit(solution)/shard_map/all_to_all | solution.py:383
  153.9 3.6 %pack.5 = (bf16[32,128,128]{2,1,0:T(8,128)(2,1)}, bf16[32,128,128]{2,1,0:T(8,128)(2,1)}) custom-call(s32[64]{0:T(128)} %copy-done.1, bf16[256,128,128]{2,1,0:T(8,128)(2,1)} %bitcast.16.arrived, bf16[32,128,128]{2,1,0:T(8,128)(2,1)} %pack.4.refs_0_), custom_call_target="tpu_custom_call" | custom-call | bytes 4194304 | tf_op jit(solution)/shard_map/pack/pallas_call | solution.py:115
  157.4 3.2 collective-permute-start.1
  160.6 10.5 %all-to-all-done.2 = bf16[8,4,128,128]{3,2,1,0:T(8,128)(2,1)} async-done(((bf16[8,4,128,128]{3,2,1,0:T(8,128)(2,1)}), bf16[8,4,128,128]{3,2,1,0:T(8,128)(2,1)}, u32[]{:S(2)}, u32[]{:S(2)}) %all-to-all-start.2) | async-done | bytes 1048608 | tf_op jit(solution)/shard_map/all_to_all | solution.py:383
  171.4 4.4 %collective-permute-start.5 = (bf16[32,128,128]{2,1,0:T(8,128)(2,1)}, bf16[32,128,128]{2,1,0:T(8,128)(2,1)}, u32[]{:S(2)}, u32[]{:S(2)}) collective-permute-start(bf16[32,128,128]{2,1,0:T(8,128)(2,1)} %bitcast.19.refs_0_), channel_id=1, source_target_pairs={{0,12},{1,13},{2,14},{3,15},{4,0},{5,1},{6,2},{7,3},{8,4},{9,5},{1... | collective-permute-start | bytes 3145736 | tf_op jit(solution)/shard_map/ppermute | solution.py:33
  175.9 14.2 %collective-permute-done.1.refs_2_ = bf16[32,128,128]{2,1,0:T(8,128)(2,1)} collective-permute-done((bf16[32,128,128]{2,1,0:T(8,128)(2,1)}, bf16[32,128,128]{2,1,0:T(8,128)(2,1)}, u32[]{:S(2)}, u32[]{:S(2)}) %collective-permute-start.1) | collective-permute-done | bytes 1048608 | tf_op jit(solution)/shard_map/ppermute | solution.py:37
  196.7 4.2 %collective-permute-start.9 = (bf16[32,128,128]{2,1,0:T(8,128)(2,1)}, bf16[32,128,128]{2,1,0:T(8,128)(2,1)}, u32[]{:S(2)}, u32[]{:S(2)}) collective-permute-start(bf16[32,128,128]{2,1,0:T(8,128)(2,1)} %collective-permute-done.refs_7_.refs_1_), channel_id=1, source_target_pairs={{0,12},{1,13},{2,14},{3,15},{4,0},{5,1},{6,2},{7,3},{8,4},{9,5},{1... | collective-permute-start | bytes 3145736 | tf_op jit(solution)/shard_map/ppermute | solution.py:33
  201.0 15.0 %collective-permute-done.7.refs_6_.refs_7_ = bf16[32,128,128]{2,1,0:T(8,128)(2,1)} collective-permute-done((bf16[32,128,128]{2,1,0:T(8,128)(2,1)}, bf16[32,128,128]{2,1,0:T(8,128)(2,1)}, u32[]{:S(2)}, u32[]{:S(2)}) %collective-permute-start.7) | collective-permute-done | bytes 1048608 | tf_op jit(solution)/shard_map/ppermute | solution.py:37
  219.0 3.2 collective-permute-start.12
  226.4 4.9 %collective-permute-start.10 = (bf16[32,128,128]{2,1,0:T(8,128)(2,1)}, bf16[32,128,128]{2,1,0:T(8,128)(2,1)}, u32[]{:S(2)}, u32[]{:S(2)}) collective-permute-start(bf16[32,128,128]{2,1,0:T(8,128)(2,1)} %get-tuple-element.34.refs_2_), channel_id=1, source_target_pairs={{0,12},{1,13},{2,14},{3,15},{4,0},{5,1},{6,2},{7,3},{8,4},{9,5},{1... | collective-permute-start | bytes 3145736 | tf_op jit(solution)/shard_map/ppermute | solution.py:33
  231.2 13.6 %collective-permute-done.12.refs_1_ = bf16[32,128,128]{2,1,0:T(8,128)(2,1)} collective-permute-done((bf16[32,128,128]{2,1,0:T(8,128)(2,1)}, bf16[32,128,128]{2,1,0:T(8,128)(2,1)}, u32[]{:S(2)}, u32[]{:S(2)}) %collective-permute-start.12) | collective-permute-done | bytes 1048608 | tf_op jit(solution)/shard_map/ppermute | solution.py:37
  256.1 7.2 %all-gather.2.cloned.1.call-done = bf16[32,128,128]{2,1,0:T(8,128)(2,1)} async-done(((bf16[2,128,128]{2,1,0:T(8,128)(2,1)}), bf16[32,128,128]{2,1,0:T(8,128)(2,1)}) %all-gather.2.cloned.1.call-update) | async-done | bytes 1048592 | tf_op jit(solution)/shard_map/all_gather | solution.py:382
  263.3 8.4 %square.2.refs_0_ = bf16[6,32,128,128]{3,2,1,0:T(8,128)(2,1)} custom-call(s32[6]{0:T(128)} %stack.157.groups, s32[512]{0:T(512)} %copy-done, s32[512]{0:T(512)} %compare_select_fusion.mask, bf16[16,2,128,128]{3,2,1,0:T(8,128)(2,1)} %bitcast.61, bf16[32,128,128]{2,1,0:T(8,128)(2,1)} %bitcast.19.refs_0_, ...), custom_call_target="tpu_custom_call" | custom-call | flops 805306368 | bytes 12582912 | tf_op jit(solution)/shard_map/square/pallas_call | solution.py:172
  271.7 5.6 %square.3.refs_1_ = bf16[2,32,128,128]{3,2,1,0:T(8,128)(2,1)} custom-call(s32[2]{0:T(128)} %pad_add_fusion.2.groups, s32[512]{0:T(512)} %copy-done, s32[512]{0:T(512)} %compare_select_fusion.mask, bf16[16,2,128,128]{3,2,1,0:T(8,128)(2,1)} %bitcast.62, bf16[32,128,128]{2,1,0:T(8,128)(2,1)} %collective-permute-done.10.refs_0_, ...), custom_call_target="tpu_custom_call" | custom-call | flops 268435456 | bytes 4194304 | tf_op jit(solution)/shard_map/square/pallas_call | solution.py:172
  280.7 2.7 collective-permute-start.22
  287.2 3.8 %collective-permute-done.19.refs_3_ = bf16[2,32,128,128]{3,2,1,0:T(8,128)(2,1)} collective-permute-done((bf16[2,32,128,128]{3,2,1,0:T(8,128)(2,1)}, bf16[2,32,128,128]{3,2,1,0:T(8,128)(2,1)}, u32[]{:S(2)}, u32[]{:S(2)}) %collective-permute-start.19) | collective-permute-done | bytes 2097184 | tf_op jit(solution)/shard_map/ppermute | solution.py:33
  290.9 13.9 %cubed.2.refs_7_ = f32[64,128,128]{2,1,0:T(8,128)} custom-call(s32[14]{0:T(128)} %stack.174.groups, s32[13]{0:T(128)} %stack.188.slots, s32[512]{0:T(512)} %reshape.170.inner_at, s32[512]{0:T(512)} %reshape.171.target, bf16[6,32,128,128]{3,2,1,0:T(8,128)(2,1)} %get-tuple-element.44.refs_0_.refs_17_, ...), custom_call_target="tpu_custom_call" | custom-call | flops 6979321856 | bytes 32505856 | tf_op jit(solution)/shard_map/cubed/pallas_call | solution.py:278
  307.5 7.3 %cubed.3 = bf16[256,4096]{1,0:T(8,128)(2,1)} custom-call(s32[4]{0:T(128)} %pad_add_fusion.groups, s32[3]{0:T(128)} %pad_add_fusion.1.slots, s32[512]{0:T(512)} %reshape.170.inner_at, s32[512]{0:T(512)} %reshape.171.target, bf16[6,32,128,128]{3,2,1,0:T(8,128)(2,1)} %get-tuple-element.44.refs_0_.refs_17_, ...), custom_call_target="tpu_custom_call" | custom-call | flops 1610612736 | bytes 11534336 | tf_op jit(solution)/shard_map/cubed/pallas_call | solution.py:278
  (105 shorter events, 42.0 us)
Async XLA Ops:
  9.6 23.0 %all-to-all-start = ((s32[128,8,128]{2,1,0:T(8,128)}), s32[128,8,128]{2,1,0:T(8,128)S(1)}, u32[]{:S(2)}, u32[]{:S(2)}) async-start(s32[128,8,128]{2,1,0:T(8,128)} %broadcast_in_dim.87), calls=%async_computation | async-start | bytes 1048576 | tf_op jit(solution)/shard_map/all_to_all | solution.py:322
  32.7 113.9 %all-to-all-start.1 = ((bf16[128,2,128,128]{3,2,1,0:T(8,128)(2,1)}), bf16[128,2,128,128]{3,2,1,0:T(8,128)(2,1)}, u32[]{:S(2)}, u32[]{:S(2)}) async-start(bf16[128,2,128,128]{3,2,1,0:T(8,128)(2,1)} %bitcast.59), calls=%async_computation.1 | async-start | bytes 16777216 | tf_op jit(solution)/shard_map/all_to_all | solution.py:318
  153.8 109.5 %all-gather.2.cloned.1.call-start = ((), (), s32[]{:S(2)}) async-start(), calls=%async_computation.3 | async-start | bytes 1114112 | tf_op jit(solution)/shard_map/all_gather | solution.py:382
  157.4 32.6 %collective-permute-start.1 = (bf16[32,128,128]{2,1,0:T(8,128)(2,1)}, bf16[32,128,128]{2,1,0:T(8,128)(2,1)}, u32[]{:S(2)}, u32[]{:S(2)}) collective-permute-start(bf16[32,128,128]{2,1,0:T(8,128)(2,1)} %get-tuple-element.27.refs_0_), channel_id=1, source_target_pairs={{0,96},{16,112},{32,0},{48,16},{64,32},{80,48},{96,64},{112,80},{1... | collective-permute-start | bytes 3145736 | tf_op jit(solution)/shard_map/ppermute | solution.py:37
  160.6 30.9 %collective-permute-start.2 = (bf16[32,128,128]{2,1,0:T(8,128)(2,1)}, bf16[32,128,128]{2,1,0:T(8,128)(2,1)}, u32[]{:S(2)}, u32[]{:S(2)}) collective-permute-start(bf16[32,128,128]{2,1,0:T(8,128)(2,1)} %get-tuple-element.27.refs_0_), channel_id=1, source_target_pairs={{0,32},{16,48},{32,64},{48,80},{64,96},{80,112},{96,0},{112,16},{1... | collective-permute-start | bytes 3145736 | tf_op jit(solution)/shard_map/ppermute | solution.py:37
  171.1 23.4 %collective-permute-start = (bf16[32,128,128]{2,1,0:T(8,128)(2,1)}, bf16[32,128,128]{2,1,0:T(8,128)(2,1)}, u32[]{:S(2)}, u32[]{:S(2)}) collective-permute-start(bf16[32,128,128]{2,1,0:T(8,128)(2,1)} %bitcast.19.refs_0_), channel_id=1, source_target_pairs={{0,2},{1,3},{2,0},{3,1},{4,6},{5,7},{6,4},{7,5},{8,10},{9,11},{10,... | collective-permute-start | bytes 3145736 | tf_op jit(solution)/shard_map/ppermute | solution.py:33
  171.4 25.3 %collective-permute-start.5 = (bf16[32,128,128]{2,1,0:T(8,128)(2,1)}, bf16[32,128,128]{2,1,0:T(8,128)(2,1)}, u32[]{:S(2)}, u32[]{:S(2)}) collective-permute-start(bf16[32,128,128]{2,1,0:T(8,128)(2,1)} %bitcast.19.refs_0_), channel_id=1, source_target_pairs={{0,12},{1,13},{2,14},{3,15},{4,0},{5,1},{6,2},{7,3},{8,4},{9,5},{1... | collective-permute-start | bytes 3145736 | tf_op jit(solution)/shard_map/ppermute | solution.py:33
  175.9 25.1 %collective-permute-start.6 = (bf16[32,128,128]{2,1,0:T(8,128)(2,1)}, bf16[32,128,128]{2,1,0:T(8,128)(2,1)}, u32[]{:S(2)}, u32[]{:S(2)}) collective-permute-start(bf16[32,128,128]{2,1,0:T(8,128)(2,1)} %bitcast.19.refs_0_), channel_id=1, source_target_pairs={{0,4},{1,5},{2,6},{3,7},{4,8},{5,9},{6,10},{7,11},{8,12},{9,13},{1... | collective-permute-start | bytes 3145736 | tf_op jit(solution)/shard_map/ppermute | solution.py:33
  191.5 24.5 %collective-permute-start.7 = (bf16[32,128,128]{2,1,0:T(8,128)(2,1)}, bf16[32,128,128]{2,1,0:T(8,128)(2,1)}, u32[]{:S(2)}, u32[]{:S(2)}) collective-permute-start(bf16[32,128,128]{2,1,0:T(8,128)(2,1)} %get-tuple-element.29.refs_0_), channel_id=1, source_target_pairs={{0,96},{16,112},{32,0},{48,16},{64,32},{80,48},{96,64},{112,80},{1... | collective-permute-start | bytes 3145736 | tf_op jit(solution)/shard_map/ppermute | solution.py:37
  192.9 25.2 %collective-permute-start.3 = (bf16[32,128,128]{2,1,0:T(8,128)(2,1)}, bf16[32,128,128]{2,1,0:T(8,128)(2,1)}, u32[]{:S(2)}, u32[]{:S(2)}) collective-permute-start(bf16[32,128,128]{2,1,0:T(8,128)(2,1)} %get-tuple-element.29.refs_0_), channel_id=1, source_target_pairs={{0,32},{16,48},{32,64},{48,80},{64,96},{80,112},{96,0},{112,16},{1... | collective-permute-start | bytes 3145736 | tf_op jit(solution)/shard_map/ppermute | solution.py:37
  194.4 24.6 %collective-permute-start.4 = (bf16[32,128,128]{2,1,0:T(8,128)(2,1)}, bf16[32,128,128]{2,1,0:T(8,128)(2,1)}, u32[]{:S(2)}, u32[]{:S(2)}) collective-permute-start(bf16[32,128,128]{2,1,0:T(8,128)(2,1)} %get-tuple-element.31.refs_6_), channel_id=1, source_target_pairs={{0,16},{16,0},{32,48},{48,32},{64,80},{80,64},{96,112},{112,96},{1... | collective-permute-start | bytes 3145736 | tf_op jit(solution)/shard_map/ppermute | solution.py:37
  196.7 29.6 %collective-permute-start.9 = (bf16[32,128,128]{2,1,0:T(8,128)(2,1)}, bf16[32,128,128]{2,1,0:T(8,128)(2,1)}, u32[]{:S(2)}, u32[]{:S(2)}) collective-permute-start(bf16[32,128,128]{2,1,0:T(8,128)(2,1)} %collective-permute-done.refs_7_.refs_1_), channel_id=1, source_target_pairs={{0,12},{1,13},{2,14},{3,15},{4,0},{5,1},{6,2},{7,3},{8,4},{9,5},{1... | collective-permute-start | bytes 3145736 | tf_op jit(solution)/shard_map/ppermute | solution.py:33
  201.0 25.4 %collective-permute-start.8 = (bf16[32,128,128]{2,1,0:T(8,128)(2,1)}, bf16[32,128,128]{2,1,0:T(8,128)(2,1)}, u32[]{:S(2)}, u32[]{:S(2)}) collective-permute-start(bf16[32,128,128]{2,1,0:T(8,128)(2,1)} %collective-permute-done.refs_7_.refs_1_), channel_id=1, source_target_pairs={{0,4},{1,5},{2,6},{3,7},{4,8},{5,9},{6,10},{7,11},{8,12},{9,13},{1... | collective-permute-start | bytes 3145736 | tf_op jit(solution)/shard_map/ppermute | solution.py:33
  219.0 25.8 %collective-permute-start.12 = (bf16[32,128,128]{2,1,0:T(8,128)(2,1)}, bf16[32,128,128]{2,1,0:T(8,128)(2,1)}, u32[]{:S(2)}, u32[]{:S(2)}) collective-permute-start(bf16[32,128,128]{2,1,0:T(8,128)(2,1)} %get-tuple-element.33.refs_3_.refs_10_), channel_id=1, source_target_pairs={{0,16},{16,0},{32,48},{48,32},{64,80},{80,64},{96,112},{112,96},{1... | collective-permute-start | bytes 3145736 | tf_op jit(solution)/shard_map/ppermute | solution.py:37
  222.2 23.3 %collective-permute-start.13 = (bf16[32,128,128]{2,1,0:T(8,128)(2,1)}, bf16[32,128,128]{2,1,0:T(8,128)(2,1)}, u32[]{:S(2)}, u32[]{:S(2)}) collective-permute-start(bf16[32,128,128]{2,1,0:T(8,128)(2,1)} %get-tuple-element.38.refs_4_), channel_id=1, source_target_pairs={{0,96},{16,112},{32,0},{48,16},{64,32},{80,48},{96,64},{112,80},{1... | collective-permute-start | bytes 3145736 | tf_op jit(solution)/shard_map/ppermute | solution.py:37
  223.7 23.6 %collective-permute-start.14 = (bf16[32,128,128]{2,1,0:T(8,128)(2,1)}, bf16[32,128,128]{2,1,0:T(8,128)(2,1)}, u32[]{:S(2)}, u32[]{:S(2)}) collective-permute-start(bf16[32,128,128]{2,1,0:T(8,128)(2,1)} %get-tuple-element.39.refs_8_), channel_id=1, source_target_pairs={{0,32},{16,48},{32,64},{48,80},{64,96},{80,112},{96,0},{112,16},{1... | collective-permute-start | bytes 3145736 | tf_op jit(solution)/shard_map/ppermute | solution.py:37
  226.4 45.3 %collective-permute-start.10 = (bf16[32,128,128]{2,1,0:T(8,128)(2,1)}, bf16[32,128,128]{2,1,0:T(8,128)(2,1)}, u32[]{:S(2)}, u32[]{:S(2)}) collective-permute-start(bf16[32,128,128]{2,1,0:T(8,128)(2,1)} %get-tuple-element.34.refs_2_), channel_id=1, source_target_pairs={{0,12},{1,13},{2,14},{3,15},{4,0},{5,1},{6,2},{7,3},{8,4},{9,5},{1... | collective-permute-start | bytes 3145736 | tf_op jit(solution)/shard_map/ppermute | solution.py:33
  231.2 40.5 %collective-permute-start.11 = (bf16[32,128,128]{2,1,0:T(8,128)(2,1)}, bf16[32,128,128]{2,1,0:T(8,128)(2,1)}, u32[]{:S(2)}, u32[]{:S(2)}) collective-permute-start(bf16[32,128,128]{2,1,0:T(8,128)(2,1)} %get-tuple-element.36.refs_5_), channel_id=1, source_target_pairs={{0,4},{1,5},{2,6},{3,7},{4,8},{5,9},{6,10},{7,11},{8,12},{9,13},{1... | collective-permute-start | bytes 3145736 | tf_op jit(solution)/shard_map/ppermute | solution.py:33
  247.3 30.0 %collective-permute-start.15 = (bf16[32,128,128]{2,1,0:T(8,128)(2,1)}, bf16[32,128,128]{2,1,0:T(8,128)(2,1)}, u32[]{:S(2)}, u32[]{:S(2)}) collective-permute-start(bf16[32,128,128]{2,1,0:T(8,128)(2,1)} %get-tuple-element.42.refs_9_), channel_id=1, source_target_pairs={{0,96},{16,112},{32,0},{48,16},{64,32},{80,48},{96,64},{112,80},{1... | collective-permute-start | bytes 3145736 | tf_op jit(solution)/shard_map/ppermute | solution.py:37
  247.6 29.7 %collective-permute-start.16 = (bf16[32,128,128]{2,1,0:T(8,128)(2,1)}, bf16[32,128,128]{2,1,0:T(8,128)(2,1)}, u32[]{:S(2)}, u32[]{:S(2)}) collective-permute-start(bf16[32,128,128]{2,1,0:T(8,128)(2,1)} %get-tuple-element.42.refs_9_), channel_id=1, source_target_pairs={{0,32},{16,48},{32,64},{48,80},{64,96},{80,112},{96,0},{112,16},{1... | collective-permute-start | bytes 3145736 | tf_op jit(solution)/shard_map/ppermute | solution.py:37
  249.4 28.0 %collective-permute-start.17 = (bf16[32,128,128]{2,1,0:T(8,128)(2,1)}, bf16[32,128,128]{2,1,0:T(8,128)(2,1)}, u32[]{:S(2)}, u32[]{:S(2)}) collective-permute-start(bf16[32,128,128]{2,1,0:T(8,128)(2,1)} %get-tuple-element.43.refs_11_), channel_id=1, source_target_pairs={{0,16},{16,0},{32,48},{48,32},{64,80},{80,64},{96,112},{112,96},{1... | collective-permute-start | bytes 3145736 | tf_op jit(solution)/shard_map/ppermute | solution.py:37
  278.0 26.9 %collective-permute-start.20 = (bf16[32,128,128]{2,1,0:T(8,128)(2,1)}, bf16[32,128,128]{2,1,0:T(8,128)(2,1)}, u32[]{:S(2)}, u32[]{:S(2)}) collective-permute-start(bf16[32,128,128]{2,1,0:T(8,128)(2,1)} %get-tuple-element.46.refs_13_), channel_id=1, source_target_pairs={{0,96},{16,112},{32,0},{48,16},{64,32},{80,48},{96,64},{112,80},{1... | collective-permute-start | bytes 3145736 | tf_op jit(solution)/shard_map/ppermute | solution.py:37
  280.7 26.5 %collective-permute-start.21 = (bf16[32,128,128]{2,1,0:T(8,128)(2,1)}, bf16[32,128,128]{2,1,0:T(8,128)(2,1)}, u32[]{:S(2)}, u32[]{:S(2)}) collective-permute-start(bf16[32,128,128]{2,1,0:T(8,128)(2,1)} %get-tuple-element.46.refs_13_), channel_id=1, source_target_pairs={{0,32},{16,48},{32,64},{48,80},{64,96},{80,112},{96,0},{112,16},{1... | collective-permute-start | bytes 3145736 | tf_op jit(solution)/shard_map/ppermute | solution.py:37
  280.7 26.8 %collective-permute-start.22 = (bf16[32,128,128]{2,1,0:T(8,128)(2,1)}, bf16[32,128,128]{2,1,0:T(8,128)(2,1)}, u32[]{:S(2)}, u32[]{:S(2)}) collective-permute-start(bf16[32,128,128]{2,1,0:T(8,128)(2,1)} %get-tuple-element.47.refs_12_), channel_id=1, source_target_pairs={{0,16},{16,0},{32,48},{48,32},{64,80},{80,64},{96,112},{112,96},{1... | collective-permute-start | bytes 3145736 | tf_op jit(solution)/shard_map/ppermute | solution.py:37
  (5 other events, 163.4 us)
Sparse Core Ops, SparseCore 0:
  226.5 36.7 all-gather.1

commit v6 on v5

--- a/solution.py
+++ b/solution.py
@@ -378,7 +378,7 @@
     leader, mask = leader.reshape(512), mask.reshape(512)
 
     inner, window = pack(where[:32], arrived)[0], pack(where[32:], arrived)[0]
-    band = pack(place, arrived, [inner], 2)
+    band = pack(place, arrived, [inner, window], 2)
     left = lax.all_gather(window, "col", axis=0, tiled=True).reshape(COLS, 2, B, B)
     inner = lax.all_to_all(
         inner.reshape(ROWS, 4, B, B), "row", split_axis=0, concat_axis=0, tiled=True
@@ -402,7 +402,7 @@
 
     p[0, 0, 1], p[1, 0, 0], p[3, 0, 1], p[0, 1, 0], f[1, 0], f[3, 0] = after(
         [second, p[1, 0, 0], p[3, 0, 1], p[0, 1, 0], f[1, 0], f[3, 0]],
-        [p[1, 0, 1], f[0, 1]],
+        [p[1, 0, 1], f[0, 1], left],
     )
     p[2, 0, 0] = send_row(p[1, 0, 0], -1, 0)
     p[2, 0, 1] = send_row(p[3, 0, 1], 1, 0)

time: 324 us -> 321 us (level)
  starting transfers between devices: 57 us -> 52.5 us
    ppermute x9, waiting for transfers between devices: 5.25 us -> 11.6 us  [send_col(): return lax.ppermute(value, 'col', pairs)]
    all_gather x1, waiting for transfers between devices: 7.18 us -> 2.41 us  [local(): lax.all_gather(window, 'col', axis=0, tiled=True).reshape(COLS, 2, B, B)]
    ppermute x14, waiting for transfers between devices: 52.4 us -> 55.7 us  [send_row(): return lax.ppermute(value, 'row', moved(by_y, flip_z))]
  transfers between devices with their start and end apart: 27 -> 27, of which waited for: 17 -> 20; matrix products, arithmetic and copies ran while one was open for 4% -> 4% of each run, Pallas kernels for 12% -> 13%
where the time goes in v6:
time: 321 us; the launch traced here: 320 us
  waiting for transfers between devices  188 us (59%)
  starting transfers between devices  52.5 us (16%)
  Pallas kernels  50.3 us (16%)
  between operations  13.7 us (4%)
  local copies, waits for them, and re-layouts  8.46 us (3%)
  other arithmetic  6.14 us (2%)
    all_to_all x1, waiting for transfers between devices, local(): lax.all_to_all(outgoing.reshape(ROWS * COLS, 2, B, B), AXES, split_axis=0...  104 us
    ppermute x14, waiting for transfers between devices, send_row(): return lax.ppermute(value, 'row', moved(by_y, flip_z))  55.7 us
    pallas_call x2, Pallas kernels, cubed(): pl.pallas_call(functools.partial(cubed_kernel, is_last), grid_spec=pltpu....  21.3 us
    ppermute x14, starting transfers between devices, send_row(): return lax.ppermute(value, 'row', moved(by_y, flip_z))  19.4 us
    pallas_call x2, Pallas kernels, square(): pl.pallas_call(square_kernel, grid_spec=pltpu.PrefetchScalarGridSpec(num_...  14 us
    ppermute x9, starting transfers between devices, send_col(): return lax.ppermute(value, 'col', pairs)  11.8 us
    ppermute x9, waiting for transfers between devices, send_col(): return lax.ppermute(value, 'col', pairs)  11.6 us
    all_to_all x1, starting transfers between devices, local(): lax.all_to_all(jnp.broadcast_to(tags.reshape(1, 8, 128), (ROWS * COLS, 8,...  10.5 us
  transfers between devices with their start and end apart: 27, of which 20 were waited for; matrix products, arithmetic and copies ran while one was open for 4% of the time, Pallas kernels for 13%

profile of v6, /device:TPU:6, one launch (start us, length us, event | category | flops | bytes accessed | tf_op | source)
XLA Modules:
  0.0 319.8 jit_solution(12283948906601190904)
XLA Ops:
  9.6 10.5 %all-to-all-start = ((s32[128,8,128]{2,1,0:T(8,128)}), s32[128,8,128]{2,1,0:T(8,128)S(1)}, u32[]{:S(2)}, u32[]{:S(2)}) async-start(s32[128,8,128]{2,1,0:T(8,128)} %broadcast_in_dim.87), calls=%async_computation | async-start | bytes 1048576 | tf_op jit(solution)/shard_map/all_to_all | solution.py:322
  20.1 6.5 %spread.1 = bf16[8,16,2,128,128]{4,3,2,1,0:T(8,128)(2,1)} custom-call(bf16[16,16,128,128]{3,2,1,0:T(8,128)(2,1)} %owned.1), custom_call_target="tpu_custom_call" | custom-call | bytes 16777216 | tf_op jit(solution)/shard_map/spread/pallas_call | solution.py:60
  26.7 6.0 %all-to-all-done = s32[128,8,128]{2,1,0:T(8,128)S(1)} async-done(((s32[128,8,128]{2,1,0:T(8,128)}), s32[128,8,128]{2,1,0:T(8,128)S(1)}, u32[]{:S(2)}, u32[]{:S(2)}) %all-to-all-start) | async-done | bytes 524320 | tf_op jit(solution)/shard_map/all_to_all | solution.py:322
  32.7 6.5 %all-to-all-start.1 = ((bf16[128,2,128,128]{3,2,1,0:T(8,128)(2,1)}), bf16[128,2,128,128]{3,2,1,0:T(8,128)(2,1)}, u32[]{:S(2)}, u32[]{:S(2)}) async-start(bf16[128,2,128,128]{3,2,1,0:T(8,128)(2,1)} %bitcast.59), calls=%async_computation.1 | async-start | bytes 16777216 | tf_op jit(solution)/shard_map/all_to_all | solution.py:318
  43.0 103.6 %all-to-all-done.1 = bf16[128,2,128,128]{3,2,1,0:T(8,128)(2,1)} async-done(((bf16[128,2,128,128]{3,2,1,0:T(8,128)(2,1)}), bf16[128,2,128,128]{3,2,1,0:T(8,128)(2,1)}, u32[]{:S(2)}, u32[]{:S(2)}) %all-to-all-start.1) | async-done | bytes 8388640 | tf_op jit(solution)/shard_map/all_to_all | solution.py:318
  149.5 4.3 %all-to-all-start.2 = ((bf16[8,4,128,128]{3,2,1,0:T(8,128)(2,1)}), bf16[8,4,128,128]{3,2,1,0:T(8,128)(2,1)}, u32[]{:S(2)}, u32[]{:S(2)}) async-start(bf16[8,4,128,128]{3,2,1,0:T(8,128)(2,1)} %bitcast.60), calls=%async_computation.2 | async-start | bytes 2097152 | tf_op jit(solution)/shard_map/all_to_all | solution.py:383
  155.9 3.6 %pack.5 = (bf16[32,128,128]{2,1,0:T(8,128)(2,1)}, bf16[32,128,128]{2,1,0:T(8,128)(2,1)}) custom-call(s32[64]{0:T(128)} %copy-done.1, bf16[256,128,128]{2,1,0:T(8,128)(2,1)} %bitcast.16.arrived, bf16[32,128,128]{2,1,0:T(8,128)(2,1)} %pack.4.refs_0_, bf16[2,128,128]{2,1,0:T(8,128)(2,1)} %pack.3.refs_1_), custom_call_target="tpu_custom_call" | custom-call | bytes 4194304 | tf_op jit(solution)/shard_map/pack/pallas_call | solution.py:115
  159.5 3.2 collective-permute-start.1
  162.6 8.4 %all-to-all-done.2 = bf16[8,4,128,128]{3,2,1,0:T(8,128)(2,1)} async-done(((bf16[8,4,128,128]{3,2,1,0:T(8,128)(2,1)}), bf16[8,4,128,128]{3,2,1,0:T(8,128)(2,1)}, u32[]{:S(2)}, u32[]{:S(2)}) %all-to-all-start.2) | async-done | bytes 1048608 | tf_op jit(solution)/shard_map/all_to_all | solution.py:383
  171.5 4.4 %collective-permute-start.5 = (bf16[32,128,128]{2,1,0:T(8,128)(2,1)}, bf16[32,128,128]{2,1,0:T(8,128)(2,1)}, u32[]{:S(2)}, u32[]{:S(2)}) collective-permute-start(bf16[32,128,128]{2,1,0:T(8,128)(2,1)} %bitcast.19.refs_0_), channel_id=1, source_target_pairs={{0,12},{1,13},{2,14},{3,15},{4,0},{5,1},{6,2},{7,3},{8,4},{9,5},{1... | collective-permute-start | bytes 3145736 | tf_op jit(solution)/shard_map/ppermute | solution.py:33
  175.9 14.1 %collective-permute-done.1.refs_2_ = bf16[32,128,128]{2,1,0:T(8,128)(2,1)} collective-permute-done((bf16[32,128,128]{2,1,0:T(8,128)(2,1)}, bf16[32,128,128]{2,1,0:T(8,128)(2,1)}, u32[]{:S(2)}, u32[]{:S(2)}) %collective-permute-start.1) | collective-permute-done | bytes 1048608 | tf_op jit(solution)/shard_map/ppermute | solution.py:37
  194.3 4.2 %collective-permute-done.refs_7_.refs_1_ = bf16[32,128,128]{2,1,0:T(8,128)(2,1)} collective-permute-done((bf16[32,128,128]{2,1,0:T(8,128)(2,1)}, bf16[32,128,128]{2,1,0:T(8,128)(2,1)}, u32[]{:S(2)}, u32[]{:S(2)}) %collective-permute-start) | collective-permute-done | bytes 1048608 | tf_op jit(solution)/shard_map/ppermute | solution.py:33
  198.8 3.2 collective-permute-done.5.refs_4_
  207.7 10.0 %collective-permute-done.7.refs_6_.refs_7_ = bf16[32,128,128]{2,1,0:T(8,128)(2,1)} collective-permute-done((bf16[32,128,128]{2,1,0:T(8,128)(2,1)}, bf16[32,128,128]{2,1,0:T(8,128)(2,1)}, u32[]{:S(2)}, u32[]{:S(2)}) %collective-permute-start.7) | collective-permute-done | bytes 1048608 | tf_op jit(solution)/shard_map/ppermute | solution.py:37
  218.9 3.6 %collective-permute-done.4.refs_3_ = bf16[32,128,128]{2,1,0:T(8,128)(2,1)} collective-permute-done((bf16[32,128,128]{2,1,0:T(8,128)(2,1)}, bf16[32,128,128]{2,1,0:T(8,128)(2,1)}, u32[]{:S(2)}, u32[]{:S(2)}) %collective-permute-start.4) | collective-permute-done | bytes 1048608 | tf_op jit(solution)/shard_map/ppermute | solution.py:37
  229.6 15.6 %collective-permute-done.12.refs_1_ = bf16[32,128,128]{2,1,0:T(8,128)(2,1)} collective-permute-done((bf16[32,128,128]{2,1,0:T(8,128)(2,1)}, bf16[32,128,128]{2,1,0:T(8,128)(2,1)}, u32[]{:S(2)}, u32[]{:S(2)}) %collective-permute-start.12) | collective-permute-done | bytes 1048608 | tf_op jit(solution)/shard_map/ppermute | solution.py:37
  245.7 4.4 %collective-permute-done.14.refs_3_ = bf16[32,128,128]{2,1,0:T(8,128)(2,1)} collective-permute-done((bf16[32,128,128]{2,1,0:T(8,128)(2,1)}, bf16[32,128,128]{2,1,0:T(8,128)(2,1)}, u32[]{:S(2)}, u32[]{:S(2)}) %collective-permute-start.14) | collective-permute-done | bytes 1048608 | tf_op jit(solution)/shard_map/ppermute | solution.py:37
  252.1 2.9 collective-permute-start.17
  260.1 8.4 %square.2.refs_0_ = bf16[6,32,128,128]{3,2,1,0:T(8,128)(2,1)} custom-call(s32[6]{0:T(128)} %stack.157.groups, s32[512]{0:T(512)} %copy-done, s32[512]{0:T(512)} %compare_select_fusion.mask, bf16[16,2,128,128]{3,2,1,0:T(8,128)(2,1)} %bitcast.62, bf16[32,128,128]{2,1,0:T(8,128)(2,1)} %bitcast.19.refs_0_, ...), custom_call_target="tpu_custom_call" | custom-call | flops 805306368 | bytes 12582912 | tf_op jit(solution)/shard_map/square/pallas_call | solution.py:172
  268.6 5.6 %square.3.refs_1_ = bf16[2,32,128,128]{3,2,1,0:T(8,128)(2,1)} custom-call(s32[2]{0:T(128)} %pad_add_fusion.2.groups, s32[512]{0:T(512)} %copy-done, s32[512]{0:T(512)} %compare_select_fusion.mask, bf16[16,2,128,128]{3,2,1,0:T(8,128)(2,1)} %bitcast.63, bf16[32,128,128]{2,1,0:T(8,128)(2,1)} %collective-permute-done.10.refs_0_, ...), custom_call_target="tpu_custom_call" | custom-call | flops 268435456 | bytes 4194304 | tf_op jit(solution)/shard_map/square/pallas_call | solution.py:172
  276.1 3.0 collective-permute-start.20
  285.4 3.6 %collective-permute-done.19.refs_3_ = bf16[2,32,128,128]{3,2,1,0:T(8,128)(2,1)} collective-permute-done((bf16[2,32,128,128]{3,2,1,0:T(8,128)(2,1)}, bf16[2,32,128,128]{3,2,1,0:T(8,128)(2,1)}, u32[]{:S(2)}, u32[]{:S(2)}) %collective-permute-start.19) | collective-permute-done | bytes 2097184 | tf_op jit(solution)/shard_map/ppermute | solution.py:33
  289.1 14.0 %cubed.2.refs_7_ = f32[64,128,128]{2,1,0:T(8,128)} custom-call(s32[14]{0:T(128)} %stack.174.groups, s32[13]{0:T(128)} %stack.188.slots, s32[512]{0:T(512)} %reshape.170.inner_at, s32[512]{0:T(512)} %reshape.171.target, bf16[6,32,128,128]{3,2,1,0:T(8,128)(2,1)} %get-tuple-element.44.refs_0_.refs_17_, ...), custom_call_target="tpu_custom_call" | custom-call | flops 6979321856 | bytes 32505856 | tf_op jit(solution)/shard_map/cubed/pallas_call | solution.py:278
  305.6 7.3 %cubed.3 = bf16[256,4096]{1,0:T(8,128)(2,1)} custom-call(s32[4]{0:T(128)} %pad_add_fusion.groups, s32[3]{0:T(128)} %pad_add_fusion.1.slots, s32[512]{0:T(512)} %reshape.170.inner_at, s32[512]{0:T(512)} %reshape.171.target, bf16[6,32,128,128]{3,2,1,0:T(8,128)(2,1)} %get-tuple-element.44.refs_0_.refs_17_, ...), custom_call_target="tpu_custom_call" | custom-call | flops 1610612736 | bytes 11534336 | tf_op jit(solution)/shard_map/cubed/pallas_call | solution.py:278
  (105 shorter events, 49.3 us)
Async XLA Ops:
  9.6 23.0 %all-to-all-start = ((s32[128,8,128]{2,1,0:T(8,128)}), s32[128,8,128]{2,1,0:T(8,128)S(1)}, u32[]{:S(2)}, u32[]{:S(2)}) async-start(s32[128,8,128]{2,1,0:T(8,128)} %broadcast_in_dim.87), calls=%async_computation | async-start | bytes 1048576 | tf_op jit(solution)/shard_map/all_to_all | solution.py:322
  32.7 113.9 %all-to-all-start.1 = ((bf16[128,2,128,128]{3,2,1,0:T(8,128)(2,1)}), bf16[128,2,128,128]{3,2,1,0:T(8,128)(2,1)}, u32[]{:S(2)}, u32[]{:S(2)}) async-start(bf16[128,2,128,128]{3,2,1,0:T(8,128)(2,1)} %bitcast.59), calls=%async_computation.1 | async-start | bytes 16777216 | tf_op jit(solution)/shard_map/all_to_all | solution.py:318
  153.8 53.9 %all-gather.2.cloned.1.call-start = ((), (), s32[]{:S(2)}) async-start(), calls=%async_computation.3 | async-start | bytes 1114112 | tf_op jit(solution)/shard_map/all_gather | solution.py:382
  159.5 30.5 %collective-permute-start.1 = (bf16[32,128,128]{2,1,0:T(8,128)(2,1)}, bf16[32,128,128]{2,1,0:T(8,128)(2,1)}, u32[]{:S(2)}, u32[]{:S(2)}) collective-permute-start(bf16[32,128,128]{2,1,0:T(8,128)(2,1)} %get-tuple-element.27.refs_0_), channel_id=1, source_target_pairs={{0,96},{16,112},{32,0},{48,16},{64,32},{80,48},{96,64},{112,80},{1... | collective-permute-start | bytes 3145736 | tf_op jit(solution)/shard_map/ppermute | solution.py:37
  162.6 29.6 %collective-permute-start.2 = (bf16[32,128,128]{2,1,0:T(8,128)(2,1)}, bf16[32,128,128]{2,1,0:T(8,128)(2,1)}, u32[]{:S(2)}, u32[]{:S(2)}) collective-permute-start(bf16[32,128,128]{2,1,0:T(8,128)(2,1)} %get-tuple-element.27.refs_0_), channel_id=1, source_target_pairs={{0,32},{16,48},{32,64},{48,80},{64,96},{80,112},{96,0},{112,16},{1... | collective-permute-start | bytes 3145736 | tf_op jit(solution)/shard_map/ppermute | solution.py:37
  171.0 27.5 %collective-permute-start = (bf16[32,128,128]{2,1,0:T(8,128)(2,1)}, bf16[32,128,128]{2,1,0:T(8,128)(2,1)}, u32[]{:S(2)}, u32[]{:S(2)}) collective-permute-start(bf16[32,128,128]{2,1,0:T(8,128)(2,1)} %bitcast.19.refs_0_), channel_id=1, source_target_pairs={{0,2},{1,3},{2,0},{3,1},{4,6},{5,7},{6,4},{7,5},{8,10},{9,11},{10,... | collective-permute-start | bytes 3145736 | tf_op jit(solution)/shard_map/ppermute | solution.py:33
  171.5 30.6 %collective-permute-start.5 = (bf16[32,128,128]{2,1,0:T(8,128)(2,1)}, bf16[32,128,128]{2,1,0:T(8,128)(2,1)}, u32[]{:S(2)}, u32[]{:S(2)}) collective-permute-start(bf16[32,128,128]{2,1,0:T(8,128)(2,1)} %bitcast.19.refs_0_), channel_id=1, source_target_pairs={{0,12},{1,13},{2,14},{3,15},{4,0},{5,1},{6,2},{7,3},{8,4},{9,5},{1... | collective-permute-start | bytes 3145736 | tf_op jit(solution)/shard_map/ppermute | solution.py:33
  175.9 28.6 %collective-permute-start.6 = (bf16[32,128,128]{2,1,0:T(8,128)(2,1)}, bf16[32,128,128]{2,1,0:T(8,128)(2,1)}, u32[]{:S(2)}, u32[]{:S(2)}) collective-permute-start(bf16[32,128,128]{2,1,0:T(8,128)(2,1)} %bitcast.19.refs_0_), channel_id=1, source_target_pairs={{0,4},{1,5},{2,6},{3,7},{4,8},{5,9},{6,10},{7,11},{8,12},{9,13},{1... | collective-permute-start | bytes 3145736 | tf_op jit(solution)/shard_map/ppermute | solution.py:33
  192.3 25.4 %collective-permute-start.7 = (bf16[32,128,128]{2,1,0:T(8,128)(2,1)}, bf16[32,128,128]{2,1,0:T(8,128)(2,1)}, u32[]{:S(2)}, u32[]{:S(2)}) collective-permute-start(bf16[32,128,128]{2,1,0:T(8,128)(2,1)} %get-tuple-element.29.refs_0_), channel_id=1, source_target_pairs={{0,96},{16,112},{32,0},{48,16},{64,32},{80,48},{96,64},{112,80},{1... | collective-permute-start | bytes 3145736 | tf_op jit(solution)/shard_map/ppermute | solution.py:37
  192.9 26.1 %collective-permute-start.3 = (bf16[32,128,128]{2,1,0:T(8,128)(2,1)}, bf16[32,128,128]{2,1,0:T(8,128)(2,1)}, u32[]{:S(2)}, u32[]{:S(2)}) collective-permute-start(bf16[32,128,128]{2,1,0:T(8,128)(2,1)} %get-tuple-element.29.refs_0_), channel_id=1, source_target_pairs={{0,32},{16,48},{32,64},{48,80},{64,96},{80,112},{96,0},{112,16},{1... | collective-permute-start | bytes 3145736 | tf_op jit(solution)/shard_map/ppermute | solution.py:37
  198.5 24.0 %collective-permute-start.4 = (bf16[32,128,128]{2,1,0:T(8,128)(2,1)}, bf16[32,128,128]{2,1,0:T(8,128)(2,1)}, u32[]{:S(2)}, u32[]{:S(2)}) collective-permute-start(bf16[32,128,128]{2,1,0:T(8,128)(2,1)} %get-tuple-element.31.refs_6_), channel_id=1, source_target_pairs={{0,16},{16,0},{32,48},{48,32},{64,80},{80,64},{96,112},{112,96},{1... | collective-permute-start | bytes 3145736 | tf_op jit(solution)/shard_map/ppermute | solution.py:37
  202.0 23.9 %collective-permute-start.9 = (bf16[32,128,128]{2,1,0:T(8,128)(2,1)}, bf16[32,128,128]{2,1,0:T(8,128)(2,1)}, u32[]{:S(2)}, u32[]{:S(2)}) collective-permute-start(bf16[32,128,128]{2,1,0:T(8,128)(2,1)} %collective-permute-done.refs_7_.refs_1_), channel_id=1, source_target_pairs={{0,12},{1,13},{2,14},{3,15},{4,0},{5,1},{6,2},{7,3},{8,4},{9,5},{1... | collective-permute-start | bytes 3145736 | tf_op jit(solution)/shard_map/ppermute | solution.py:33
  204.5 21.8 %collective-permute-start.8 = (bf16[32,128,128]{2,1,0:T(8,128)(2,1)}, bf16[32,128,128]{2,1,0:T(8,128)(2,1)}, u32[]{:S(2)}, u32[]{:S(2)}) collective-permute-start(bf16[32,128,128]{2,1,0:T(8,128)(2,1)} %collective-permute-done.refs_7_.refs_1_), channel_id=1, source_target_pairs={{0,4},{1,5},{2,6},{3,7},{4,8},{5,9},{6,10},{7,11},{8,12},{9,13},{1... | collective-permute-start | bytes 3145736 | tf_op jit(solution)/shard_map/ppermute | solution.py:33
  222.6 22.6 %collective-permute-start.12 = (bf16[32,128,128]{2,1,0:T(8,128)(2,1)}, bf16[32,128,128]{2,1,0:T(8,128)(2,1)}, u32[]{:S(2)}, u32[]{:S(2)}) collective-permute-start(bf16[32,128,128]{2,1,0:T(8,128)(2,1)} %get-tuple-element.33.refs_3_.refs_10_), channel_id=1, source_target_pairs={{0,16},{16,0},{32,48},{48,32},{64,80},{80,64},{96,112},{112,96},{1... | collective-permute-start | bytes 3145736 | tf_op jit(solution)/shard_map/ppermute | solution.py:37
  223.9 21.8 %collective-permute-start.13 = (bf16[32,128,128]{2,1,0:T(8,128)(2,1)}, bf16[32,128,128]{2,1,0:T(8,128)(2,1)}, u32[]{:S(2)}, u32[]{:S(2)}) collective-permute-start(bf16[32,128,128]{2,1,0:T(8,128)(2,1)} %get-tuple-element.38.refs_4_), channel_id=1, source_target_pairs={{0,96},{16,112},{32,0},{48,16},{64,32},{80,48},{96,64},{112,80},{1... | collective-permute-start | bytes 3145736 | tf_op jit(solution)/shard_map/ppermute | solution.py:37
  225.8 24.3 %collective-permute-start.14 = (bf16[32,128,128]{2,1,0:T(8,128)(2,1)}, bf16[32,128,128]{2,1,0:T(8,128)(2,1)}, u32[]{:S(2)}, u32[]{:S(2)}) collective-permute-start(bf16[32,128,128]{2,1,0:T(8,128)(2,1)} %get-tuple-element.39.refs_8_), channel_id=1, source_target_pairs={{0,32},{16,48},{32,64},{48,80},{64,96},{80,112},{96,0},{112,16},{1... | collective-permute-start | bytes 3145736 | tf_op jit(solution)/shard_map/ppermute | solution.py:37
  226.4 42.2 %collective-permute-start.10 = (bf16[32,128,128]{2,1,0:T(8,128)(2,1)}, bf16[32,128,128]{2,1,0:T(8,128)(2,1)}, u32[]{:S(2)}, u32[]{:S(2)}) collective-permute-start(bf16[32,128,128]{2,1,0:T(8,128)(2,1)} %get-tuple-element.34.refs_2_), channel_id=1, source_target_pairs={{0,12},{1,13},{2,14},{3,15},{4,0},{5,1},{6,2},{7,3},{8,4},{9,5},{1... | collective-permute-start | bytes 3145736 | tf_op jit(solution)/shard_map/ppermute | solution.py:33
  228.9 39.7 %collective-permute-start.11 = (bf16[32,128,128]{2,1,0:T(8,128)(2,1)}, bf16[32,128,128]{2,1,0:T(8,128)(2,1)}, u32[]{:S(2)}, u32[]{:S(2)}) collective-permute-start(bf16[32,128,128]{2,1,0:T(8,128)(2,1)} %get-tuple-element.36.refs_5_), channel_id=1, source_target_pairs={{0,4},{1,5},{2,6},{3,7},{4,8},{5,9},{6,10},{7,11},{8,12},{9,13},{1... | collective-permute-start | bytes 3145736 | tf_op jit(solution)/shard_map/ppermute | solution.py:33
  250.1 24.1 %collective-permute-start.15 = (bf16[32,128,128]{2,1,0:T(8,128)(2,1)}, bf16[32,128,128]{2,1,0:T(8,128)(2,1)}, u32[]{:S(2)}, u32[]{:S(2)}) collective-permute-start(bf16[32,128,128]{2,1,0:T(8,128)(2,1)} %get-tuple-element.42.refs_9_), channel_id=1, source_target_pairs={{0,96},{16,112},{32,0},{48,16},{64,32},{80,48},{96,64},{112,80},{1... | collective-permute-start | bytes 3145736 | tf_op jit(solution)/shard_map/ppermute | solution.py:37
  251.8 23.4 %collective-permute-start.16 = (bf16[32,128,128]{2,1,0:T(8,128)(2,1)}, bf16[32,128,128]{2,1,0:T(8,128)(2,1)}, u32[]{:S(2)}, u32[]{:S(2)}) collective-permute-start(bf16[32,128,128]{2,1,0:T(8,128)(2,1)} %get-tuple-element.42.refs_9_), channel_id=1, source_target_pairs={{0,32},{16,48},{32,64},{48,80},{64,96},{80,112},{96,0},{112,16},{1... | collective-permute-start | bytes 3145736 | tf_op jit(solution)/shard_map/ppermute | solution.py:37
  252.1 23.5 %collective-permute-start.17 = (bf16[32,128,128]{2,1,0:T(8,128)(2,1)}, bf16[32,128,128]{2,1,0:T(8,128)(2,1)}, u32[]{:S(2)}, u32[]{:S(2)}) collective-permute-start(bf16[32,128,128]{2,1,0:T(8,128)(2,1)} %get-tuple-element.43.refs_11_), channel_id=1, source_target_pairs={{0,16},{16,0},{32,48},{48,32},{64,80},{80,64},{96,112},{112,96},{1... | collective-permute-start | bytes 3145736 | tf_op jit(solution)/shard_map/ppermute | solution.py:37
  276.1 27.0 %collective-permute-start.20 = (bf16[32,128,128]{2,1,0:T(8,128)(2,1)}, bf16[32,128,128]{2,1,0:T(8,128)(2,1)}, u32[]{:S(2)}, u32[]{:S(2)}) collective-permute-start(bf16[32,128,128]{2,1,0:T(8,128)(2,1)} %get-tuple-element.46.refs_13_), channel_id=1, source_target_pairs={{0,96},{16,112},{32,0},{48,16},{64,32},{80,48},{96,64},{112,80},{1... | collective-permute-start | bytes 3145736 | tf_op jit(solution)/shard_map/ppermute | solution.py:37
  279.0 26.3 %collective-permute-start.21 = (bf16[32,128,128]{2,1,0:T(8,128)(2,1)}, bf16[32,128,128]{2,1,0:T(8,128)(2,1)}, u32[]{:S(2)}, u32[]{:S(2)}) collective-permute-start(bf16[32,128,128]{2,1,0:T(8,128)(2,1)} %get-tuple-element.46.refs_13_), channel_id=1, source_target_pairs={{0,32},{16,48},{32,64},{48,80},{64,96},{80,112},{96,0},{112,16},{1... | collective-permute-start | bytes 3145736 | tf_op jit(solution)/shard_map/ppermute | solution.py:37
  279.0 26.6 %collective-permute-start.22 = (bf16[32,128,128]{2,1,0:T(8,128)(2,1)}, bf16[32,128,128]{2,1,0:T(8,128)(2,1)}, u32[]{:S(2)}, u32[]{:S(2)}) collective-permute-start(bf16[32,128,128]{2,1,0:T(8,128)(2,1)} %get-tuple-element.47.refs_12_), channel_id=1, source_target_pairs={{0,16},{16,0},{32,48},{48,32},{64,80},{80,64},{96,112},{112,96},{1... | collective-permute-start | bytes 3145736 | tf_op jit(solution)/shard_map/ppermute | solution.py:37
  (5 other events, 156.3 us)
Sparse Core Ops, SparseCore 0:
  171.6 36.0 all-gather.1

commit v7 on v6

--- a/solution.py
+++ b/solution.py
@@ -378,7 +378,7 @@
     leader, mask = leader.reshape(512), mask.reshape(512)
 
     inner, window = pack(where[:32], arrived)[0], pack(where[32:], arrived)[0]
-    band = pack(place, arrived, [inner, window], 2)
+    band = pack(place, arrived, [inner], 2)
     left = lax.all_gather(window, "col", axis=0, tiled=True).reshape(COLS, 2, B, B)
     inner = lax.all_to_all(
         inner.reshape(ROWS, 4, B, B), "row", split_axis=0, concat_axis=0, tiled=True

time: 321 us -> 320 us (level)
    ppermute x14, waiting for transfers between devices: 55.7 us -> 48.2 us  [send_row(): return lax.ppermute(value, 'row', moved(by_y, flip_z))]
    ppermute x9, waiting for transfers between devices: 11.6 us -> 15 us  [send_col(): return lax.ppermute(value, 'col', pairs)]
  transfers between devices with their start and end apart: 27 -> 27, of which waited for: 20 -> 21; matrix products, arithmetic and copies ran while one was open for 4% -> 4% of each run, Pallas kernels for 13% -> 13%
where the time goes in v7:
time: 320 us
  waiting for transfers between devices  186 us (58%)
  starting transfers between devices  54.4 us (17%)
  Pallas kernels  50.2 us (16%)
  between operations  13.7 us (4%)
  local copies, waits for them, and re-layouts  8.46 us (3%)
  other arithmetic  6.14 us (2%)
    all_to_all x1, waiting for transfers between devices, local(): lax.all_to_all(outgoing.reshape(ROWS * COLS, 2, B, B), AXES, split_axis=0...  104 us
    ppermute x14, waiting for transfers between devices, send_row(): return lax.ppermute(value, 'row', moved(by_y, flip_z))  48.2 us
    ppermute x14, starting transfers between devices, send_row(): return lax.ppermute(value, 'row', moved(by_y, flip_z))  21.4 us
    pallas_call x2, Pallas kernels, cubed(): pl.pallas_call(functools.partial(cubed_kernel, is_last), grid_spec=pltpu....  21.2 us
    ppermute x9, waiting for transfers between devices, send_col(): return lax.ppermute(value, 'col', pairs)  15 us
    pallas_call x2, Pallas kernels, square(): pl.pallas_call(square_kernel, grid_spec=pltpu.PrefetchScalarGridSpec(num_...  14 us
    ppermute x9, starting transfers between devices, send_col(): return lax.ppermute(value, 'col', pairs)  11.7 us
    all_to_all x1, waiting for transfers between devices, local(): lax.all_to_all(inner.reshape(ROWS, 4, B, B), 'row', split_axis=0, concat_...  10.5 us
  transfers between devices with their start and end apart: 27, of which 21 were waited for; matrix products, arithmetic and copies ran while one was open for 4% of the time, Pallas kernels for 13%

profile of v7, /device:TPU:6, one launch (start us, length us, event | category | flops | bytes accessed | tf_op | source)
XLA Modules:
  0.0 319.6 jit_solution(15603439369884872567)
XLA Ops:
  9.6 10.5 %all-to-all-start = ((s32[128,8,128]{2,1,0:T(8,128)}), s32[128,8,128]{2,1,0:T(8,128)S(1)}, u32[]{:S(2)}, u32[]{:S(2)}) async-start(s32[128,8,128]{2,1,0:T(8,128)} %broadcast_in_dim.87), calls=%async_computation | async-start | bytes 1048576 | tf_op jit(solution)/shard_map/all_to_all | solution.py:322
  20.1 6.5 %spread.1 = bf16[8,16,2,128,128]{4,3,2,1,0:T(8,128)(2,1)} custom-call(bf16[16,16,128,128]{3,2,1,0:T(8,128)(2,1)} %owned.1), custom_call_target="tpu_custom_call" | custom-call | bytes 16777216 | tf_op jit(solution)/shard_map/spread/pallas_call | solution.py:60
  26.7 6.0 %all-to-all-done = s32[128,8,128]{2,1,0:T(8,128)S(1)} async-done(((s32[128,8,128]{2,1,0:T(8,128)}), s32[128,8,128]{2,1,0:T(8,128)S(1)}, u32[]{:S(2)}, u32[]{:S(2)}) %all-to-all-start) | async-done | bytes 524320 | tf_op jit(solution)/shard_map/all_to_all | solution.py:322
  32.7 6.5 %all-to-all-start.1 = ((bf16[128,2,128,128]{3,2,1,0:T(8,128)(2,1)}), bf16[128,2,128,128]{3,2,1,0:T(8,128)(2,1)}, u32[]{:S(2)}, u32[]{:S(2)}) async-start(bf16[128,2,128,128]{3,2,1,0:T(8,128)(2,1)} %bitcast.59), calls=%async_computation.1 | async-start | bytes 16777216 | tf_op jit(solution)/shard_map/all_to_all | solution.py:318
  43.0 103.6 %all-to-all-done.1 = bf16[128,2,128,128]{3,2,1,0:T(8,128)(2,1)} async-done(((bf16[128,2,128,128]{3,2,1,0:T(8,128)(2,1)}), bf16[128,2,128,128]{3,2,1,0:T(8,128)(2,1)}, u32[]{:S(2)}, u32[]{:S(2)}) %all-to-all-start.1) | async-done | bytes 8388640 | tf_op jit(solution)/shard_map/all_to_all | solution.py:318
  149.5 4.3 %all-to-all-start.2 = ((bf16[8,4,128,128]{3,2,1,0:T(8,128)(2,1)}), bf16[8,4,128,128]{3,2,1,0:T(8,128)(2,1)}, u32[]{:S(2)}, u32[]{:S(2)}) async-start(bf16[8,4,128,128]{3,2,1,0:T(8,128)(2,1)} %bitcast.60), calls=%async_computation.2 | async-start | bytes 2097152 | tf_op jit(solution)/shard_map/all_to_all | solution.py:383
  153.8 3.5 %pack.5 = (bf16[32,128,128]{2,1,0:T(8,128)(2,1)}, bf16[32,128,128]{2,1,0:T(8,128)(2,1)}) custom-call(s32[64]{0:T(128)} %copy-done.1, bf16[256,128,128]{2,1,0:T(8,128)(2,1)} %bitcast.16.arrived, bf16[32,128,128]{2,1,0:T(8,128)(2,1)} %pack.4.refs_0_), custom_call_target="tpu_custom_call" | custom-call | bytes 4194304 | tf_op jit(solution)/shard_map/pack/pallas_call | solution.py:115
  157.3 3.2 collective-permute-start.1
  160.5 10.5 %all-to-all-done.2 = bf16[8,4,128,128]{3,2,1,0:T(8,128)(2,1)} async-done(((bf16[8,4,128,128]{3,2,1,0:T(8,128)(2,1)}), bf16[8,4,128,128]{3,2,1,0:T(8,128)(2,1)}, u32[]{:S(2)}, u32[]{:S(2)}) %all-to-all-start.2) | async-done | bytes 1048608 | tf_op jit(solution)/shard_map/all_to_all | solution.py:383
  173.6 4.4 %collective-permute-start.5 = (bf16[32,128,128]{2,1,0:T(8,128)(2,1)}, bf16[32,128,128]{2,1,0:T(8,128)(2,1)}, u32[]{:S(2)}, u32[]{:S(2)}) collective-permute-start(bf16[32,128,128]{2,1,0:T(8,128)(2,1)} %bitcast.19.refs_0_), channel_id=1, source_target_pairs={{0,12},{1,13},{2,14},{3,15},{4,0},{5,1},{6,2},{7,3},{8,4},{9,5},{1... | collective-permute-start | bytes 3145736 | tf_op jit(solution)/shard_map/ppermute | solution.py:33
  178.0 12.0 %collective-permute-done.1.refs_2_ = bf16[32,128,128]{2,1,0:T(8,128)(2,1)} collective-permute-done((bf16[32,128,128]{2,1,0:T(8,128)(2,1)}, bf16[32,128,128]{2,1,0:T(8,128)(2,1)}, u32[]{:S(2)}, u32[]{:S(2)}) %collective-permute-start.1) | collective-permute-done | bytes 1048608 | tf_op jit(solution)/shard_map/ppermute | solution.py:37
  193.5 3.4 %collective-permute-done.refs_7_.refs_1_ = bf16[32,128,128]{2,1,0:T(8,128)(2,1)} collective-permute-done((bf16[32,128,128]{2,1,0:T(8,128)(2,1)}, bf16[32,128,128]{2,1,0:T(8,128)(2,1)}, u32[]{:S(2)}, u32[]{:S(2)}) %collective-permute-start) | collective-permute-done | bytes 1048608 | tf_op jit(solution)/shard_map/ppermute | solution.py:33
  198.1 6.1 %collective-permute-done.5.refs_4_ = bf16[32,128,128]{2,1,0:T(8,128)(2,1)} collective-permute-done((bf16[32,128,128]{2,1,0:T(8,128)(2,1)}, bf16[32,128,128]{2,1,0:T(8,128)(2,1)}, u32[]{:S(2)}, u32[]{:S(2)}) %collective-permute-start.5) | collective-permute-done | bytes 1048608 | tf_op jit(solution)/shard_map/ppermute | solution.py:33
  209.7 6.2 %collective-permute-done.7.refs_6_.refs_7_ = bf16[32,128,128]{2,1,0:T(8,128)(2,1)} collective-permute-done((bf16[32,128,128]{2,1,0:T(8,128)(2,1)}, bf16[32,128,128]{2,1,0:T(8,128)(2,1)}, u32[]{:S(2)}, u32[]{:S(2)}) %collective-permute-start.7) | collective-permute-done | bytes 1048608 | tf_op jit(solution)/shard_map/ppermute | solution.py:37
  218.1 4.3 %collective-permute-done.4.refs_3_ = bf16[32,128,128]{2,1,0:T(8,128)(2,1)} collective-permute-done((bf16[32,128,128]{2,1,0:T(8,128)(2,1)}, bf16[32,128,128]{2,1,0:T(8,128)(2,1)}, u32[]{:S(2)}, u32[]{:S(2)}) %collective-permute-start.4) | collective-permute-done | bytes 1048608 | tf_op jit(solution)/shard_map/ppermute | solution.py:37
  231.7 13.9 %collective-permute-done.12.refs_1_ = bf16[32,128,128]{2,1,0:T(8,128)(2,1)} collective-permute-done((bf16[32,128,128]{2,1,0:T(8,128)(2,1)}, bf16[32,128,128]{2,1,0:T(8,128)(2,1)}, u32[]{:S(2)}, u32[]{:S(2)}) %collective-permute-start.12) | collective-permute-done | bytes 1048608 | tf_op jit(solution)/shard_map/ppermute | solution.py:37
  246.7 3.2 %collective-permute-done.14.refs_3_ = bf16[32,128,128]{2,1,0:T(8,128)(2,1)} collective-permute-done((bf16[32,128,128]{2,1,0:T(8,128)(2,1)}, bf16[32,128,128]{2,1,0:T(8,128)(2,1)}, u32[]{:S(2)}, u32[]{:S(2)}) %collective-permute-start.14) | collective-permute-done | bytes 1048608 | tf_op jit(solution)/shard_map/ppermute | solution.py:37
  252.0 3.0 collective-permute-start.17
  260.1 8.4 %square.2.refs_0_ = bf16[6,32,128,128]{3,2,1,0:T(8,128)(2,1)} custom-call(s32[6]{0:T(128)} %stack.157.groups, s32[512]{0:T(512)} %copy-done, s32[512]{0:T(512)} %compare_select_fusion.mask, bf16[16,2,128,128]{3,2,1,0:T(8,128)(2,1)} %bitcast.62, bf16[32,128,128]{2,1,0:T(8,128)(2,1)} %bitcast.19.refs_0_, ...), custom_call_target="tpu_custom_call" | custom-call | flops 805306368 | bytes 12582912 | tf_op jit(solution)/shard_map/square/pallas_call | solution.py:172
  268.6 5.6 %square.3.refs_1_ = bf16[2,32,128,128]{3,2,1,0:T(8,128)(2,1)} custom-call(s32[2]{0:T(128)} %pad_add_fusion.2.groups, s32[512]{0:T(512)} %copy-done, s32[512]{0:T(512)} %compare_select_fusion.mask, bf16[16,2,128,128]{3,2,1,0:T(8,128)(2,1)} %bitcast.63, bf16[32,128,128]{2,1,0:T(8,128)(2,1)} %collective-permute-done.10.refs_0_, ...), custom_call_target="tpu_custom_call" | custom-call | flops 268435456 | bytes 4194304 | tf_op jit(solution)/shard_map/square/pallas_call | solution.py:172
  275.9 3.0 collective-permute-start.20
  285.5 3.4 %collective-permute-done.19.refs_3_ = bf16[2,32,128,128]{3,2,1,0:T(8,128)(2,1)} collective-permute-done((bf16[2,32,128,128]{3,2,1,0:T(8,128)(2,1)}, bf16[2,32,128,128]{3,2,1,0:T(8,128)(2,1)}, u32[]{:S(2)}, u32[]{:S(2)}) %collective-permute-start.19) | collective-permute-done | bytes 2097184 | tf_op jit(solution)/shard_map/ppermute | solution.py:33
  288.9 13.9 %cubed.2.refs_7_ = f32[64,128,128]{2,1,0:T(8,128)} custom-call(s32[14]{0:T(128)} %stack.174.groups, s32[13]{0:T(128)} %stack.188.slots, s32[512]{0:T(512)} %reshape.170.inner_at, s32[512]{0:T(512)} %reshape.171.target, bf16[6,32,128,128]{3,2,1,0:T(8,128)(2,1)} %get-tuple-element.44.refs_0_.refs_17_, ...), custom_call_target="tpu_custom_call" | custom-call | flops 6979321856 | bytes 32505856 | tf_op jit(solution)/shard_map/cubed/pallas_call | solution.py:278
  305.4 7.3 %cubed.3 = bf16[256,4096]{1,0:T(8,128)(2,1)} custom-call(s32[4]{0:T(128)} %pad_add_fusion.groups, s32[3]{0:T(128)} %pad_add_fusion.1.slots, s32[512]{0:T(512)} %reshape.170.inner_at, s32[512]{0:T(512)} %reshape.171.target, bf16[6,32,128,128]{3,2,1,0:T(8,128)(2,1)} %get-tuple-element.44.refs_0_.refs_17_, ...), custom_call_target="tpu_custom_call" | custom-call | flops 1610612736 | bytes 11534336 | tf_op jit(solution)/shard_map/cubed/pallas_call | solution.py:278
  (105 shorter events, 53.1 us)
Async XLA Ops:
  9.6 23.0 %all-to-all-start = ((s32[128,8,128]{2,1,0:T(8,128)}), s32[128,8,128]{2,1,0:T(8,128)S(1)}, u32[]{:S(2)}, u32[]{:S(2)}) async-start(s32[128,8,128]{2,1,0:T(8,128)} %broadcast_in_dim.87), calls=%async_computation | async-start | bytes 1048576 | tf_op jit(solution)/shard_map/all_to_all | solution.py:322
  32.7 113.9 %all-to-all-start.1 = ((bf16[128,2,128,128]{3,2,1,0:T(8,128)(2,1)}), bf16[128,2,128,128]{3,2,1,0:T(8,128)(2,1)}, u32[]{:S(2)}, u32[]{:S(2)}) async-start(bf16[128,2,128,128]{3,2,1,0:T(8,128)(2,1)} %bitcast.59), calls=%async_computation.1 | async-start | bytes 16777216 | tf_op jit(solution)/shard_map/all_to_all | solution.py:318
  153.8 55.9 %all-gather.2.cloned.1.call-start = ((), (), s32[]{:S(2)}) async-start(), calls=%async_computation.3 | async-start | bytes 1114112 | tf_op jit(solution)/shard_map/all_gather | solution.py:382
  157.3 32.6 %collective-permute-start.1 = (bf16[32,128,128]{2,1,0:T(8,128)(2,1)}, bf16[32,128,128]{2,1,0:T(8,128)(2,1)}, u32[]{:S(2)}, u32[]{:S(2)}) collective-permute-start(bf16[32,128,128]{2,1,0:T(8,128)(2,1)} %get-tuple-element.27.refs_0_), channel_id=1, source_target_pairs={{0,96},{16,112},{32,0},{48,16},{64,32},{80,48},{96,64},{112,80},{1... | collective-permute-start | bytes 3145736 | tf_op jit(solution)/shard_map/ppermute | solution.py:37
  160.5 30.9 %collective-permute-start.2 = (bf16[32,128,128]{2,1,0:T(8,128)(2,1)}, bf16[32,128,128]{2,1,0:T(8,128)(2,1)}, u32[]{:S(2)}, u32[]{:S(2)}) collective-permute-start(bf16[32,128,128]{2,1,0:T(8,128)(2,1)} %get-tuple-element.27.refs_0_), channel_id=1, source_target_pairs={{0,32},{16,48},{32,64},{48,80},{64,96},{80,112},{96,0},{112,16},{1... | collective-permute-start | bytes 3145736 | tf_op jit(solution)/shard_map/ppermute | solution.py:37
  171.0 25.9 %collective-permute-start = (bf16[32,128,128]{2,1,0:T(8,128)(2,1)}, bf16[32,128,128]{2,1,0:T(8,128)(2,1)}, u32[]{:S(2)}, u32[]{:S(2)}) collective-permute-start(bf16[32,128,128]{2,1,0:T(8,128)(2,1)} %bitcast.19.refs_0_), channel_id=1, source_target_pairs={{0,2},{1,3},{2,0},{3,1},{4,6},{5,7},{6,4},{7,5},{8,10},{9,11},{10,... | collective-permute-start | bytes 3145736 | tf_op jit(solution)/shard_map/ppermute | solution.py:33
  173.6 30.6 %collective-permute-start.5 = (bf16[32,128,128]{2,1,0:T(8,128)(2,1)}, bf16[32,128,128]{2,1,0:T(8,128)(2,1)}, u32[]{:S(2)}, u32[]{:S(2)}) collective-permute-start(bf16[32,128,128]{2,1,0:T(8,128)(2,1)} %bitcast.19.refs_0_), channel_id=1, source_target_pairs={{0,12},{1,13},{2,14},{3,15},{4,0},{5,1},{6,2},{7,3},{8,4},{9,5},{1... | collective-permute-start | bytes 3145736 | tf_op jit(solution)/shard_map/ppermute | solution.py:33
  178.0 28.8 %collective-permute-start.6 = (bf16[32,128,128]{2,1,0:T(8,128)(2,1)}, bf16[32,128,128]{2,1,0:T(8,128)(2,1)}, u32[]{:S(2)}, u32[]{:S(2)}) collective-permute-start(bf16[32,128,128]{2,1,0:T(8,128)(2,1)} %bitcast.19.refs_0_), channel_id=1, source_target_pairs={{0,4},{1,5},{2,6},{3,7},{4,8},{5,9},{6,10},{7,11},{8,12},{9,13},{1... | collective-permute-start | bytes 3145736 | tf_op jit(solution)/shard_map/ppermute | solution.py:33
  191.4 24.5 %collective-permute-start.7 = (bf16[32,128,128]{2,1,0:T(8,128)(2,1)}, bf16[32,128,128]{2,1,0:T(8,128)(2,1)}, u32[]{:S(2)}, u32[]{:S(2)}) collective-permute-start(bf16[32,128,128]{2,1,0:T(8,128)(2,1)} %get-tuple-element.29.refs_0_), channel_id=1, source_target_pairs={{0,96},{16,112},{32,0},{48,16},{64,32},{80,48},{96,64},{112,80},{1... | collective-permute-start | bytes 3145736 | tf_op jit(solution)/shard_map/ppermute | solution.py:37
  192.9 25.2 %collective-permute-start.3 = (bf16[32,128,128]{2,1,0:T(8,128)(2,1)}, bf16[32,128,128]{2,1,0:T(8,128)(2,1)}, u32[]{:S(2)}, u32[]{:S(2)}) collective-permute-start(bf16[32,128,128]{2,1,0:T(8,128)(2,1)} %get-tuple-element.29.refs_0_), channel_id=1, source_target_pairs={{0,32},{16,48},{32,64},{48,80},{64,96},{80,112},{96,0},{112,16},{1... | collective-permute-start | bytes 3145736 | tf_op jit(solution)/shard_map/ppermute | solution.py:37
  196.9 25.5 %collective-permute-start.4 = (bf16[32,128,128]{2,1,0:T(8,128)(2,1)}, bf16[32,128,128]{2,1,0:T(8,128)(2,1)}, u32[]{:S(2)}, u32[]{:S(2)}) collective-permute-start(bf16[32,128,128]{2,1,0:T(8,128)(2,1)} %get-tuple-element.31.refs_6_), channel_id=1, source_target_pairs={{0,16},{16,0},{32,48},{48,32},{64,80},{80,64},{96,112},{112,96},{1... | collective-permute-start | bytes 3145736 | tf_op jit(solution)/shard_map/ppermute | solution.py:37
  204.2 22.3 %collective-permute-start.9 = (bf16[32,128,128]{2,1,0:T(8,128)(2,1)}, bf16[32,128,128]{2,1,0:T(8,128)(2,1)}, u32[]{:S(2)}, u32[]{:S(2)}) collective-permute-start(bf16[32,128,128]{2,1,0:T(8,128)(2,1)} %collective-permute-done.refs_7_.refs_1_), channel_id=1, source_target_pairs={{0,12},{1,13},{2,14},{3,15},{4,0},{5,1},{6,2},{7,3},{8,4},{9,5},{1... | collective-permute-start | bytes 3145736 | tf_op jit(solution)/shard_map/ppermute | solution.py:33
  206.8 21.6 %collective-permute-start.8 = (bf16[32,128,128]{2,1,0:T(8,128)(2,1)}, bf16[32,128,128]{2,1,0:T(8,128)(2,1)}, u32[]{:S(2)}, u32[]{:S(2)}) collective-permute-start(bf16[32,128,128]{2,1,0:T(8,128)(2,1)} %collective-permute-done.refs_7_.refs_1_), channel_id=1, source_target_pairs={{0,4},{1,5},{2,6},{3,7},{4,8},{5,9},{6,10},{7,11},{8,12},{9,13},{1... | collective-permute-start | bytes 3145736 | tf_op jit(solution)/shard_map/ppermute | solution.py:33
  222.4 23.1 %collective-permute-start.12 = (bf16[32,128,128]{2,1,0:T(8,128)(2,1)}, bf16[32,128,128]{2,1,0:T(8,128)(2,1)}, u32[]{:S(2)}, u32[]{:S(2)}) collective-permute-start(bf16[32,128,128]{2,1,0:T(8,128)(2,1)} %get-tuple-element.33.refs_3_.refs_10_), channel_id=1, source_target_pairs={{0,16},{16,0},{32,48},{48,32},{64,80},{80,64},{96,112},{112,96},{1... | collective-permute-start | bytes 3145736 | tf_op jit(solution)/shard_map/ppermute | solution.py:37
  224.4 22.3 %collective-permute-start.13 = (bf16[32,128,128]{2,1,0:T(8,128)(2,1)}, bf16[32,128,128]{2,1,0:T(8,128)(2,1)}, u32[]{:S(2)}, u32[]{:S(2)}) collective-permute-start(bf16[32,128,128]{2,1,0:T(8,128)(2,1)} %get-tuple-element.38.refs_4_), channel_id=1, source_target_pairs={{0,96},{16,112},{32,0},{48,16},{64,32},{80,48},{96,64},{112,80},{1... | collective-permute-start | bytes 3145736 | tf_op jit(solution)/shard_map/ppermute | solution.py:37
  226.2 23.8 %collective-permute-start.14 = (bf16[32,128,128]{2,1,0:T(8,128)(2,1)}, bf16[32,128,128]{2,1,0:T(8,128)(2,1)}, u32[]{:S(2)}, u32[]{:S(2)}) collective-permute-start(bf16[32,128,128]{2,1,0:T(8,128)(2,1)} %get-tuple-element.39.refs_8_), channel_id=1, source_target_pairs={{0,32},{16,48},{32,64},{48,80},{64,96},{80,112},{96,0},{112,16},{1... | collective-permute-start | bytes 3145736 | tf_op jit(solution)/shard_map/ppermute | solution.py:37
  228.5 40.1 %collective-permute-start.10 = (bf16[32,128,128]{2,1,0:T(8,128)(2,1)}, bf16[32,128,128]{2,1,0:T(8,128)(2,1)}, u32[]{:S(2)}, u32[]{:S(2)}) collective-permute-start(bf16[32,128,128]{2,1,0:T(8,128)(2,1)} %get-tuple-element.34.refs_2_), channel_id=1, source_target_pairs={{0,12},{1,13},{2,14},{3,15},{4,0},{5,1},{6,2},{7,3},{8,4},{9,5},{1... | collective-permute-start | bytes 3145736 | tf_op jit(solution)/shard_map/ppermute | solution.py:33
  229.0 39.6 %collective-permute-start.11 = (bf16[32,128,128]{2,1,0:T(8,128)(2,1)}, bf16[32,128,128]{2,1,0:T(8,128)(2,1)}, u32[]{:S(2)}, u32[]{:S(2)}) collective-permute-start(bf16[32,128,128]{2,1,0:T(8,128)(2,1)} %get-tuple-element.36.refs_5_), channel_id=1, source_target_pairs={{0,4},{1,5},{2,6},{3,7},{4,8},{5,9},{6,10},{7,11},{8,12},{9,13},{1... | collective-permute-start | bytes 3145736 | tf_op jit(solution)/shard_map/ppermute | solution.py:33
  249.9 24.2 %collective-permute-start.15 = (bf16[32,128,128]{2,1,0:T(8,128)(2,1)}, bf16[32,128,128]{2,1,0:T(8,128)(2,1)}, u32[]{:S(2)}, u32[]{:S(2)}) collective-permute-start(bf16[32,128,128]{2,1,0:T(8,128)(2,1)} %get-tuple-element.42.refs_9_), channel_id=1, source_target_pairs={{0,96},{16,112},{32,0},{48,16},{64,32},{80,48},{96,64},{112,80},{1... | collective-permute-start | bytes 3145736 | tf_op jit(solution)/shard_map/ppermute | solution.py:37
  251.6 23.4 %collective-permute-start.16 = (bf16[32,128,128]{2,1,0:T(8,128)(2,1)}, bf16[32,128,128]{2,1,0:T(8,128)(2,1)}, u32[]{:S(2)}, u32[]{:S(2)}) collective-permute-start(bf16[32,128,128]{2,1,0:T(8,128)(2,1)} %get-tuple-element.42.refs_9_), channel_id=1, source_target_pairs={{0,32},{16,48},{32,64},{48,80},{64,96},{80,112},{96,0},{112,16},{1... | collective-permute-start | bytes 3145736 | tf_op jit(solution)/shard_map/ppermute | solution.py:37
  252.0 23.4 %collective-permute-start.17 = (bf16[32,128,128]{2,1,0:T(8,128)(2,1)}, bf16[32,128,128]{2,1,0:T(8,128)(2,1)}, u32[]{:S(2)}, u32[]{:S(2)}) collective-permute-start(bf16[32,128,128]{2,1,0:T(8,128)(2,1)} %get-tuple-element.43.refs_11_), channel_id=1, source_target_pairs={{0,16},{16,0},{32,48},{48,32},{64,80},{80,64},{96,112},{112,96},{1... | collective-permute-start | bytes 3145736 | tf_op jit(solution)/shard_map/ppermute | solution.py:37
  275.9 26.9 %collective-permute-start.20 = (bf16[32,128,128]{2,1,0:T(8,128)(2,1)}, bf16[32,128,128]{2,1,0:T(8,128)(2,1)}, u32[]{:S(2)}, u32[]{:S(2)}) collective-permute-start(bf16[32,128,128]{2,1,0:T(8,128)(2,1)} %get-tuple-element.46.refs_13_), channel_id=1, source_target_pairs={{0,96},{16,112},{32,0},{48,16},{64,32},{80,48},{96,64},{112,80},{1... | collective-permute-start | bytes 3145736 | tf_op jit(solution)/shard_map/ppermute | solution.py:37
  278.8 26.3 %collective-permute-start.21 = (bf16[32,128,128]{2,1,0:T(8,128)(2,1)}, bf16[32,128,128]{2,1,0:T(8,128)(2,1)}, u32[]{:S(2)}, u32[]{:S(2)}) collective-permute-start(bf16[32,128,128]{2,1,0:T(8,128)(2,1)} %get-tuple-element.46.refs_13_), channel_id=1, source_target_pairs={{0,32},{16,48},{32,64},{48,80},{64,96},{80,112},{96,0},{112,16},{1... | collective-permute-start | bytes 3145736 | tf_op jit(solution)/shard_map/ppermute | solution.py:37
  278.8 26.6 %collective-permute-start.22 = (bf16[32,128,128]{2,1,0:T(8,128)(2,1)}, bf16[32,128,128]{2,1,0:T(8,128)(2,1)}, u32[]{:S(2)}, u32[]{:S(2)}) collective-permute-start(bf16[32,128,128]{2,1,0:T(8,128)(2,1)} %get-tuple-element.47.refs_12_), channel_id=1, source_target_pairs={{0,16},{16,0},{32,48},{48,32},{64,80},{80,64},{96,112},{112,96},{1... | collective-permute-start | bytes 3145736 | tf_op jit(solution)/shard_map/ppermute | solution.py:37
  (5 other events, 156.3 us)
Sparse Core Ops, SparseCore 0:
  173.7 35.9 all-gather.1
